TPU v7x, 256 devices: a whole 4x4x8 slice. The times are simulated.
256 devices in a mesh: island: 16 (over x_hi, z), fsdp: 16 (over y, x_lo, core).
Axes of the slice: x: 4 (x_hi: 2, x_lo: 2; x = x_hi * 2 + x_lo), y: 4, z: 8, core: 2. Of those that a mesh axis runs over, the one named last changes fastest.
Arguments:
- pseudo_grad: bfloat16 [16, 3840, 5120], P('island', 'fsdp'), may hold values from -6 to 6
- error_buffer: bfloat16 [16, 3840, 5120], P('island', 'fsdp'), may hold values from -4 to 4
- basis_prev: bfloat16 [3840, 128], P('fsdp'), may hold values from -0.09375 to 0.09375
- master_weights: float32 [3840, 5120], P('fsdp', 'island'), may hold values from -1.2 to 1.2
- outer_momentum: float32 [3840, 5120], P('fsdp', 'island'), may hold values from -6 to 6
Outputs:
- error_next: bfloat16 [16, 3840, 5120], P('island', 'fsdp')
- weights_next: bfloat16 [3840, 5120], P('fsdp')
- master_next: float32 [3840, 5120], P('fsdp', 'island')
- momentum_next: float32 [3840, 5120], P('fsdp', 'island')
All inputs are finite; a program needn't handle non-finite values.
Results may differ from a plain program's by a relative error of at most 0.009.
Values may be sent and summed in bfloat16 or wider, within the bound.
No kernel may reach another device: no remote copies, remote signals or barrier semaphores. Data moves between devices by JAX's collectives and lax.ppermute only.
A program may use at most 64 MiB of HBM per device.

v0:
```python
import jax
import jax.numpy as jnp
from jax import lax
from jax.sharding import PartitionSpec as P

momentum_coef = 0.9
outer_rate = 0.7


def contract_rows(left_mat, right_mat):
    return lax.dot_general(
        left_mat, right_mat, (((0,), (0,)), ((), ())), preferred_element_type=jnp.float32
    )


def orthonormal(left_rows, gram_mat):
    factor_low = jnp.linalg.cholesky(gram_mat)
    return lax.linalg.triangular_solve(
        factor_low, left_rows, left_side=False, lower=True, transpose_a=True
    ).astype(jnp.bfloat16)


def local(pseudo_grad, error_buffer, basis_prev, master_weights, outer_momentum):
    merged = (pseudo_grad[0].astype(jnp.float32) + error_buffer[0].astype(jnp.float32)).astype(
        jnp.bfloat16
    )
    partial_left = contract_rows(merged, basis_prev)
    summed = lax.psum(partial_left, ("island", "fsdp"))
    gram_mat = lax.dot_general(
        summed,
        summed,
        (((0,), (0,)), ((), ())),
        precision=lax.Precision.HIGHEST,
        preferred_element_type=jnp.float32,
    )
    basis_bf = orthonormal(summed, gram_mat)
    right_local = jnp.dot(merged, basis_bf, preferred_element_type=jnp.float32)
    right_sum = lax.psum(right_local, "island")
    q_avg = (right_sum / lax.axis_size("island")).astype(jnp.bfloat16)
    approx = lax.dot_general(
        q_avg, basis_bf, (((1,), (1,)), ((), ())), preferred_element_type=jnp.float32
    )
    error_next = (merged.astype(jnp.float32) - approx).astype(jnp.bfloat16)[None]
    col_count = master_weights.shape[1]
    col_start = lax.axis_index("island") * col_count
    update = lax.dynamic_slice_in_dim(approx, col_start, col_count, 1)
    momentum_next = momentum_coef * outer_momentum + update
    master_next = master_weights - outer_rate * (update + momentum_coef * momentum_next)
    weights_next = lax.all_gather(master_next.astype(jnp.bfloat16), "island", axis=1, tiled=True)
    return (error_next, weights_next, master_next, momentum_next)


def solution(mesh):
    in_specs = (
        P("island", "fsdp", None),
        P("island", "fsdp", None),
        P("fsdp", None),
        P("fsdp", "island"),
        P("fsdp", "island"),
    )
    out_specs = (
        P("island", "fsdp", None),
        P("fsdp", None),
        P("fsdp", "island"),
        P("fsdp", "island"),
    )
    return jax.shard_map(local, mesh=mesh, in_specs=in_specs, out_specs=out_specs, check_vma=False)
```

profile of v0, /device:TPU:8, one launch (start us, length us, event | category | flops | bytes accessed | tf_op | source)
XLA Modules:
  0.0 571.7 jit_solution(6963494927450647758)
XLA Ops:
  7.2 0.0 copy-start
  7.2 0.0 all-reduce.3.cloned.1.call-start
  7.2 0.8 copy-done
  8.0 4.9 fusion.10
  12.9 0.0 all-reduce.3.cloned.1.call-update
  12.9 0.0 all-reduce.5.cloned.1.call-start
  12.9 266.2 %all-reduce.3.cloned.1.call-done = f32[5120,128]{1,0:T(8,128)} async-done(((f32[5120,128]{1,0:T(8,128)}), f32[5120,128]{1,0:T(8,128)}) %all-reduce.3.cloned.1.call-update) | async-done | bytes 2621456 | tf_op jit(solution)/shard_map/psum | solution.py:28
  279.2 6.9 %fusion.13 = f32[128,128]{1,0:T(8,128)S(1)} fusion(f32[5120,128]{1,0:T(8,128)} %all-reduce.3.cloned.1.call-done), kind=kOutput, calls=%fused_computation.23 | convolution fusion | flops 1006632960 | bytes 2686976 | tf_op jit(solution)/shard_map/dot_general | solution.py:29
  286.1 0.1 copy.14
  286.2 11.7 %cholesky.16 = f32[128,128]{1,0:T(8,128)S(1)} custom-call(f32[128,128]{1,0:T(8,128)S(1)} %fusion.4), custom_call_target="Cholesky" | custom-call | tf_op jit(solution)/shard_map/jit(cholesky)/cholesky | solution.py:17
  298.0 0.6 compare_reduce_fusion
  298.6 0.7 fusion.2
  299.3 9.8 %custom-call.6 = f32[1,128,128]{1,2,0:T(8,128)S(1)} custom-call(f32[1,128,128]{2,1,0:T(8,128)S(1)} %fusion.2), custom_call_target="InvertDiagBlocksLowerTriangular" | custom-call | tf_op jit(solution)/shard_map/triangular_solve | solution.py:18
  309.1 2.4 convolution_convert_fusion
  311.5 0.0 copy-start.5
  311.5 1.0 copy-done.5
  312.6 3.3 fusion.8
  315.9 0.0 all-reduce.5.cloned.1.call-update
  315.9 0.0 all-gather.2.cloned.1.call-start
  316.0 0.2 copy.16
  316.1 0.9 copy.15
  317.0 152.1 %all-reduce.5.cloned.1.call-done = f32[240,128]{1,0:T(8,128)} async-done(((f32[240,128]{1,0:T(8,128)}), f32[240,128]{1,0:T(8,128)}) %all-reduce.5.cloned.1.call-update) | async-done | bytes 122896 | tf_op jit(solution)/shard_map/psum | solution.py:38
  469.2 2.2 fusion.5
  471.4 2.2 copy-done.4
  473.6 0.9 fusion.12
  474.5 0.8 copy.17
  475.3 0.0 all-gather.2.cloned.1.call-update
  475.3 1.9 copy.19
  477.2 0.9 copy.20
  478.0 5.7 fusion.1
  483.7 77.1 %all-gather.2.cloned.1.call-done = bf16[240,5120]{0,1:T(8,128)(2,1)} async-done(((bf16[240,320]{0,1:T(8,128)(2,1)}), bf16[240,5120]{0,1:T(8,128)(2,1)}) %all-gather.2.cloned.1.call-update) | async-done | bytes 2457616 | tf_op jit(solution)/shard_map/all_gather | solution.py:49
  560.8 4.3 copy.18
  (15 shorter events, 0.1 us)
Async XLA Ops:
  7.2 0.8 copy-start
  7.2 272.0 %all-reduce.3.cloned.1.call-start = ((), (), s32[]{:S(2)}) async-start(), calls=%async_computation | async-start | bytes 5242880 | tf_op jit(solution)/shard_map/psum | solution.py:28
  12.9 456.3 %all-reduce.5.cloned.1.call-start = ((), (), s32[]{:S(2)}) async-start(), calls=%async_computation.1 | async-start | bytes 245760 | tf_op jit(solution)/shard_map/psum | solution.py:38
  279.1 29.9 %copy-start.1 = (f32[5120,128]{1,0:T(8,128)S(1)}, f32[5120,128]{1,0:T(8,128)}, u32[]{:S(2)}) copy-start(f32[5120,128]{1,0:T(8,128)} %all-reduce.3.cloned.1.call-done) | copy-start | bytes 7864324
  309.1 3.5 copy-start.2
  311.5 1.1 copy-start.5
  312.6 3.4 copy-start.7
  312.6 3.6 copy-start.8
  315.9 244.9 %all-gather.2.cloned.1.call-start = ((), (), s32[]{:S(2)}) async-start(), calls=%async_computation.2 | async-start | bytes 2785280 | tf_op jit(solution)/shard_map/all_gather | solution.py:49
  469.2 4.4 copy-start.6
  471.4 2.2 copy-start.4
  473.6 4.5 copy-start.3
Sparse Core Ops, SparseCore 0:
  13.5 265.6 all-reduce.2
  316.0 153.0 all-reduce.4
  475.4 85.3 all-gather.1
where the time goes:
time: 572 us
  waiting for transfers between devices  495 us (87%)
  other arithmetic  29.5 us (5%)
  matrix products  19.7 us (3%)
  between operations  13.9 us (2%)
  local copies, waits for them, and re-layouts  13 us (2%)
    psum x1, waiting for transfers between devices, local(): summed = lax.psum(partial_left, ('island', 'fsdp'))  266 us
    psum x1, waiting for transfers between devices, local(): right_sum = lax.psum(right_local, 'island')  152 us
    all_gather x1, waiting for transfers between devices, local(): lax.all_gather(master_next.astype(jnp.bfloat16), 'island', axis=1, tiled=...  77.1 us
    another operation x3, other arithmetic, orthonormal(): factor_low = jnp.linalg.cholesky(gram_mat)  12.4 us
    unnamed x23, local copies, waits for them, and re-layouts  12.2 us
  transfers between devices with their start and end apart: 3, of which 3 were waited for; matrix products, arithmetic and copies ran while one was open for 2% of the time, Pallas kernels for 0%

commit v1 on v0

v1 whole, which is shorter than its diff:
```python
import jax
import jax.numpy as jnp
from jax import lax
from jax.sharding import Mesh, PartitionSpec as P

momentum_coef = 0.9
outer_rate = 0.7
momentum_part = outer_rate * momentum_coef * momentum_coef
approx_part = outer_rate * (1.0 + momentum_coef)

island = ("xh", "z")
fsdp = ("y", "xl", "core")
plane = ("xh", "y", "xl")


def to_bf(values):
    return values.astype(jnp.bfloat16)


def to_f32(values):
    return values.astype(jnp.float32)


def swap(values, axis, size, bit):
    return lax.ppermute(values, axis, [(place, place ^ bit) for place in range(size)])


def contract_rows(left_mat, right_mat):
    return lax.dot_general(
        left_mat, right_mat, (((0,), (0,)), ((), ())), preferred_element_type=jnp.float32
    )


def contract_columns(left_mat, right_mat, precision=None):
    return lax.dot_general(
        left_mat,
        right_mat,
        (((1,), (1,)), ((), ())),
        precision=precision,
        preferred_element_type=jnp.float32,
    )


def sum_left(partial):
    half = partial.shape[0] // 2
    rank = partial.shape[1]
    core = lax.axis_index("core")
    kept = lax.dynamic_slice_in_dim(partial, core * half, half, 0)
    given = to_bf(lax.dynamic_slice_in_dim(partial, (1 - core) * half, half, 0))
    mine = to_bf(kept + to_f32(swap(given, "core", 2, 1)))
    chunks = lax.all_to_all(mine, plane, 0, 0, tiled=True)
    block = jnp.sum(to_f32(chunks.reshape(16, half // 16, rank)), axis=0)
    for bit in (1, 2, 4):
        block = block + swap(block, "z", 8, bit)
    copies = jnp.broadcast_to(to_bf(block)[None], (16,) + block.shape).reshape(half, rank)
    mine = lax.all_to_all(copies, plane, 0, 0, tiled=True)
    other = swap(mine, "core", 2, 1)
    return jnp.concatenate([jnp.where(core == 0, mine, other), jnp.where(core == 0, other, mine)])


def local(pseudo_grad, error_buffer, basis_prev, master_weights, outer_momentum):
    carried = to_bf(master_weights - momentum_part * outer_momentum)
    carried = lax.all_gather(carried.T, island, axis=0, tiled=True)

    merged = to_bf(to_f32(pseudo_grad[0]) + to_f32(error_buffer[0]))
    left = sum_left(contract_rows(merged, basis_prev))

    product = jnp.dot(merged, left, preferred_element_type=jnp.float32)
    for axis, size, bit in (("xh", 2, 1), ("z", 8, 1), ("z", 8, 2), ("z", 8, 4)):
        product = product + swap(product, axis, size, bit)

    gram_mat = contract_rows(left, left)
    factor_low = jnp.linalg.cholesky(gram_mat)
    inverse_low = lax.linalg.triangular_solve(
        factor_low, jnp.eye(gram_mat.shape[0], dtype=jnp.float32), left_side=True, lower=True
    )
    high = to_bf(inverse_low)
    low = to_bf(inverse_low - to_f32(high))
    basis_bf = to_bf(contract_columns(left, high) + contract_columns(left, low))

    q_avg = to_bf(contract_columns(product, inverse_low, lax.Precision.HIGHEST) / 16)
    approx = contract_columns(q_avg, basis_bf)
    error_next = to_bf(to_f32(merged) - approx)[None]
    weights_next = to_bf(to_f32(carried.T) - approx_part * approx)

    col_count = master_weights.shape[1]
    col_start = lax.axis_index(island) * col_count
    basis_block = lax.dynamic_slice_in_dim(basis_bf, col_start, col_count, 0)
    update = contract_columns(q_avg, basis_block)
    momentum_next = momentum_coef * outer_momentum + update
    master_next = master_weights - outer_rate * (update + momentum_coef * momentum_next)
    return (error_next, weights_next, master_next, momentum_next)


def solution(mesh):
    fine = Mesh(mesh.devices.reshape(2, 8, 4, 2, 2), island + fsdp)
    in_specs = (
        P(island, fsdp, None),
        P(island, fsdp, None),
        P(fsdp, None),
        P(fsdp, island),
        P(fsdp, island),
    )
    out_specs = (
        P(island, fsdp, None),
        P(fsdp, None),
        P(fsdp, island),
        P(fsdp, island),
    )
    return jax.shard_map(local, mesh=fine, in_specs=in_specs, out_specs=out_specs, check_vma=False)
```

time: 572 us -> 230 us (0.40)
  waiting for transfers between devices: 495 us -> 113 us
  blocking collectives: 0 us -> 33.5 us
  starting transfers between devices: 0.12 us -> 21 us
  local copies, waits for them, and re-layouts: 13 us -> 6.5 us
    psum x2 -> x0, waiting for transfers between devices: 418 us -> none  [the longest x1 266 us: local(): summed = lax.psum(partial_left, ('island', 'fsdp'))]
    all_to_all x0 -> x2, blocking collectives: none -> 33.5 us  [the longest x1 18.8 us: sum_left(): chunks = lax.all_to_all(mine, plane, 0, 0, tiled=True)]
    ppermute x0 -> x9, waiting for transfers between devices: none -> 26.7 us  [swap(): lax.ppermute(values, axis, [(place, place ^ bit) for place in range(size)])]
    ppermute x0 -> x9, starting transfers between devices: none -> 21 us  [swap(): lax.ppermute(values, axis, [(place, place ^ bit) for place in range(size)])]
    unnamed x23 -> x18, local copies, waits for them, and re-layouts: 12.2 us -> 1.92 us
    all_gather x1, waiting for transfers between devices: 77.1 us -> 86.7 us  [local(): carried = lax.all_gather(carried.T, island, axis=0, tiled=True)]
    dot_general x3 -> x6, matrix products: 12.5 us -> 11.2 us  [the longest x5 10.3 us: contract_columns(): lax.dot_general(left_mat, right_mat, (((1,), (1,)), ((), ())), precision=...]
  transfers between devices with their start and end apart: 3 -> 10, of which waited for: 3 -> 9; matrix products, arithmetic and copies ran while one was open for 2% -> 6% of each run, Pallas kernels for 0% -> 0%
where the time goes in v1:
time: 230 us
  waiting for transfers between devices  113 us (49%)
  blocking collectives  33.5 us (15%)
  other arithmetic  25.8 us (11%)
  starting transfers between devices  21 us (9%)
  matrix products  15.3 us (7%)
  between operations  14.3 us (6%)
  local copies, waits for them, and re-layouts  6.5 us (3%)
    all_gather x1, waiting for transfers between devices, local(): carried = lax.all_gather(carried.T, island, axis=0, tiled=True)  86.7 us
    ppermute x9, waiting for transfers between devices, swap(): lax.ppermute(values, axis, [(place, place ^ bit) for place in range(size)])  26.7 us
    ppermute x9, starting transfers between devices, swap(): lax.ppermute(values, axis, [(place, place ^ bit) for place in range(size)])  21 us
    all_to_all x1, blocking collectives, sum_left(): chunks = lax.all_to_all(mine, plane, 0, 0, tiled=True)  18.8 us
    all_to_all x1, blocking collectives, sum_left(): mine = lax.all_to_all(copies, plane, 0, 0, tiled=True)  14.8 us
    another operation x3, other arithmetic, local(): factor_low = jnp.linalg.cholesky(gram_mat)  12.4 us
    another operation x2, other arithmetic, local(): lax.linalg.triangular_solve(factor_low, jnp.eye(gram_mat.shape[0], dtype=...  10.5 us
    dot_general x5, matrix products, contract_columns(): lax.dot_general(left_mat, right_mat, (((1,), (1,)), ((), ())), precision=...  10.3 us
  transfers between devices with their start and end apart: 10, of which 9 were waited for; matrix products, arithmetic and copies ran while one was open for 6% of the time, Pallas kernels for 0%

profile of v1, /device:TPU:8, one launch (start us, length us, event | category | flops | bytes accessed | tf_op | source)
XLA Modules:
  0.0 229.8 jit_solution(1340983690982634183)
XLA Ops:
  7.2 0.8 copy-done
  8.0 3.3 %fusion.20 = f32[5120,128]{1,0:T(8,128)S(1)} fusion(bf16[240,128]{1,0:T(8,128)(2,1)S(1)} %copy-done, bf16[1,240,5120]{2,1,0:T(8,128)(2,1)} %param.6, bf16[1,240,5120]{2,1,0:T(8,128)(2,1)} %param.5), kind=kOutput, calls=%fused_computation.41 | convolution fusion | flops 319488000 | bytes 7598080 | tf_op jit(solution)/shard_map/dot_general | solution.py:29
  11.5 2.2 collective-permute-done
  13.8 1.3 add_convert_fusion.1
  15.0 18.8 %all_to_all.18 = bf16[16,160,128]{2,1,0:T(8,128)(2,1)S(1)} all-to-all(bf16[16,160,128]{2,1,0:T(8,128)(2,1)S(1)} %bitcast.33), channel_id=1, replica_groups=mesh['xh'=2,'z'=8,'y'=4,'xl'=2,'core'=2] {'xh','y','xl'}, dimensions={0} | all-to-all | bytes 1310720 | tf_op jit(solution)/shard_map/all_to_all | solution.py:51
  33.9 2.0 collective-permute-start.1
  35.9 2.5 %collective-permute-done.1 = f32[160,128]{1,0:T(8,128)S(1)} collective-permute-done((f32[160,128]{1,0:T(8,128)S(1)}, f32[160,128]{1,0:T(8,128)S(1)}, u32[]{:S(2)}, u32[]{:S(2)}) %collective-permute-start.1) | collective-permute-done | bytes 81952 | tf_op jit(solution)/shard_map/ppermute | solution.py:25
  38.4 3.4 %collective-permute-start.2 = (f32[160,128]{1,0:T(8,128)S(1)}, f32[160,128]{1,0:T(8,128)S(1)}, u32[]{:S(2)}, u32[]{:S(2)}) collective-permute-start(f32[160,128]{1,0:T(8,128)S(1)} %add.64), channel_id=1, source_target_pairs={{0,32},{16,48},{32,0},{48,16},{64,96},{80,112},{96,64},{112,80},{1... | collective-permute-start | bytes 245768 | tf_op jit(solution)/shard_map/ppermute | solution.py:25
  41.8 2.4 %collective-permute-done.2 = f32[160,128]{1,0:T(8,128)S(1)} collective-permute-done((f32[160,128]{1,0:T(8,128)S(1)}, f32[160,128]{1,0:T(8,128)S(1)}, u32[]{:S(2)}, u32[]{:S(2)}) %collective-permute-start.2) | collective-permute-done | bytes 81952 | tf_op jit(solution)/shard_map/ppermute | solution.py:25
  44.2 7.8 %collective-permute-start.3 = (f32[160,128]{1,0:T(8,128)S(1)}, f32[160,128]{1,0:T(8,128)S(1)}, u32[]{:S(2)}, u32[]{:S(2)}) collective-permute-start(f32[160,128]{1,0:T(8,128)S(1)} %add.65), channel_id=1, source_target_pairs={{0,64},{16,80},{32,96},{48,112},{64,0},{80,16},{96,32},{112,48},{1... | collective-permute-start | bytes 245768 | tf_op jit(solution)/shard_map/ppermute | solution.py:25
  52.0 2.4 %collective-permute-done.3 = f32[160,128]{1,0:T(8,128)S(1)} collective-permute-done((f32[160,128]{1,0:T(8,128)S(1)}, f32[160,128]{1,0:T(8,128)S(1)}, u32[]{:S(2)}, u32[]{:S(2)}) %collective-permute-start.3) | collective-permute-done | bytes 81952 | tf_op jit(solution)/shard_map/ppermute | solution.py:25
  54.6 14.8 %all_to_all.19 = bf16[16,160,128]{2,1,0:T(8,128)(2,1)S(1)} all-to-all(bf16[16,160,128]{2,1,0:T(8,128)(2,1)S(1)} %broadcast_in_dim.6), channel_id=1, replica_groups=mesh['xh'=2,'z'=8,'y'=4,'xl'=2,'core'=2] {'xh','y','xl'}, dimensions={0} | all-to-all | bytes 1310720 | tf_op jit(solution)/shard_map/all_to_all | solution.py:56
  69.3 0.8 copy-done.6
  70.2 1.4 collective-permute-done.4
  71.6 1.5 broadcast_select_fusion.1
  73.0 0.5 fusion.17
  73.9 0.9 fusion.18
  74.9 11.7 %cholesky.17 = f32[128,128]{1,0:T(8,128)S(1)} custom-call(f32[128,128]{1,0:T(8,128)S(1)} %fusion.12), custom_call_target="Cholesky" | custom-call | tf_op jit(solution)/shard_map/jit(cholesky)/cholesky | solution.py:73
  86.6 0.6 compare_reduce_fusion
  87.3 1.5 collective-permute-start.5
  88.8 0.7 fusion.9
  89.4 9.8 %custom-call.6 = f32[1,128,128]{1,2,0:T(8,128)S(1)} custom-call(f32[1,128,128]{2,1,0:T(8,128)S(1)} %fusion.9), custom_call_target="InvertDiagBlocksLowerTriangular" | custom-call | tf_op jit(solution)/shard_map/triangular_solve | solution.py:74
  99.7 4.7 %collective-permute-done.6 = f32[240,128]{1,0:T(8,128)S(1)} collective-permute-done((f32[240,128]{1,0:T(8,128)S(1)}, f32[240,128]{1,0:T(8,128)S(1)}, u32[]{:S(2)}, u32[]{:S(2)}) %collective-permute-start.6) | collective-permute-done | bytes 122912 | tf_op jit(solution)/shard_map/ppermute | solution.py:25
  104.4 0.9 collective-permute-start.7
  105.4 1.6 fusion.13
  107.0 5.2 %collective-permute-done.7 = f32[240,128]{1,0:T(8,128)S(1)} collective-permute-done((f32[240,128]{1,0:T(8,128)S(1)}, f32[240,128]{1,0:T(8,128)S(1)}, u32[]{:S(2)}, u32[]{:S(2)}) %collective-permute-start.7) | collective-permute-done | bytes 122912 | tf_op jit(solution)/shard_map/ppermute | solution.py:25
  112.2 5.2 %collective-permute-start.8 = (f32[240,128]{1,0:T(8,128)S(1)}, f32[240,128]{1,0:T(8,128)S(1)}, u32[]{:S(2)}, u32[]{:S(2)}) collective-permute-start(f32[240,128]{1,0:T(8,128)S(1)} %add.69), channel_id=1, source_target_pairs={{0,64},{16,80},{32,96},{48,112},{64,0},{80,16},{96,32},{112,48},{1... | collective-permute-start | bytes 368648 | tf_op jit(solution)/shard_map/ppermute | solution.py:25
  117.9 5.8 %collective-permute-done.8 = f32[240,128]{1,0:T(8,128)S(1)} collective-permute-done((f32[240,128]{1,0:T(8,128)S(1)}, f32[240,128]{1,0:T(8,128)S(1)}, u32[]{:S(2)}, u32[]{:S(2)}) %collective-permute-start.8) | collective-permute-done | bytes 122912 | tf_op jit(solution)/shard_map/ppermute | solution.py:25
  124.0 1.1 multiply_subtract_fusion
  125.2 86.7 %all-gather.2.cloned.1.call-done = bf16[5120,240]{1,0:T(8,128)(2,1)} async-done(((bf16[320,240]{1,0:T(8,128)(2,1)}), bf16[5120,240]{1,0:T(8,128)(2,1)}) %all-gather.2.cloned.1.call-update) | async-done | bytes 2457616 | tf_op jit(solution)/shard_map/all_gather | solution.py:63
  211.9 4.3 %copy.13 = bf16[5120,240]{0,1:T(8,128)(2,1)} copy(bf16[5120,240]{1,0:T(8,128)(2,1)} %all-gather.2.cloned.1.call-done) | data formatting | bytes 4915200 | tf_op jit(solution)/shard_map/all_gather | solution.py:63
  216.2 6.7 %fusion.1 = (bf16[240,5120]{1,0:T(8,128)(2,1)}, bf16[1,240,5120]{2,1,0:T(8,128)(2,1)}) fusion(bf16[5120,240]{0,1:T(8,128)(2,1)} %copy.13, bf16[1,240,5120]{2,1,0:T(8,128)(2,1)S(1)} %copy-done.1, bf16[1,240,5120]{2,1,0:T(8,128)(2,1)} %param.5, bf16[240,128]{1,0:T(8,128)(2,1)S(1)} %fusion.4, bf16[5120,128]{1,0:T(8,128)(2,1)} %copy-done.5), kind=kOutput, calls=%fused_computation.3 | convolution fusion | flops 328089600 | bytes 13660160 | tf_op jit(solution)/shard_map/dot_general | solution.py:35
  (37 shorter events, 2.1 us)
Async XLA Ops:
  7.2 0.8 copy-start
  7.2 204.7 %all-gather.2.cloned.1.call-start = ((), (), s32[]{:S(2)}) async-start(), calls=%async_computation.2 | async-start | bytes 2785280 | tf_op jit(solution)/shard_map/all_gather | solution.py:63
  11.4 2.3 %collective-permute-start = (bf16[2560,128]{1,0:T(8,128)(2,1)S(1)}, bf16[2560,128]{1,0:T(8,128)(2,1)}, u32[]{:S(2)}, u32[]{:S(2)}) collective-permute-start(bf16[2560,128]{1,0:T(8,128)(2,1)S(1)} %dynamic-slice_convert_fusion), channel_id=1, source_target_pairs={{0,1},{1,0},{2,3},{3,2},{4,5},{5,4},{6,7},{7,6},{8,9},{9,8},{10,11... | collective-permute-start | bytes 1966088 | tf_op jit(solution)/shard_map/ppermute | solution.py:25
  33.9 4.5 %collective-permute-start.1 = (f32[160,128]{1,0:T(8,128)S(1)}, f32[160,128]{1,0:T(8,128)S(1)}, u32[]{:S(2)}, u32[]{:S(2)}) collective-permute-start(f32[160,128]{1,0:T(8,128)S(1)} %convert_reduce_fusion), channel_id=1, source_target_pairs={{0,16},{16,0},{32,48},{48,32},{64,80},{80,64},{96,112},{112,96},{1... | collective-permute-start | bytes 245768 | tf_op jit(solution)/shard_map/ppermute | solution.py:25
  38.4 5.8 %collective-permute-start.2 = (f32[160,128]{1,0:T(8,128)S(1)}, f32[160,128]{1,0:T(8,128)S(1)}, u32[]{:S(2)}, u32[]{:S(2)}) collective-permute-start(f32[160,128]{1,0:T(8,128)S(1)} %add.64), channel_id=1, source_target_pairs={{0,32},{16,48},{32,0},{48,16},{64,96},{80,112},{96,64},{112,80},{1... | collective-permute-start | bytes 245768 | tf_op jit(solution)/shard_map/ppermute | solution.py:25
  44.2 10.2 %collective-permute-start.3 = (f32[160,128]{1,0:T(8,128)S(1)}, f32[160,128]{1,0:T(8,128)S(1)}, u32[]{:S(2)}, u32[]{:S(2)}) collective-permute-start(f32[160,128]{1,0:T(8,128)S(1)} %add.65), channel_id=1, source_target_pairs={{0,64},{16,80},{32,96},{48,112},{64,0},{80,16},{96,32},{112,48},{1... | collective-permute-start | bytes 245768 | tf_op jit(solution)/shard_map/ppermute | solution.py:25
  69.3 0.8 copy-start.6
  69.3 2.2 collective-permute-start.4
  70.2 3.7 %copy-start.1 = (bf16[1,240,5120]{2,1,0:T(8,128)(2,1)S(1)}, bf16[1,240,5120]{2,1,0:T(8,128)(2,1)}, u32[]{:S(2)}) copy-start(bf16[1,240,5120]{2,1,0:T(8,128)(2,1)} %param.6) | copy-start | bytes 7372804
  70.2 3.7 %copy-start.2 = (bf16[1,240,5120]{2,1,0:T(8,128)(2,1)S(1)}, bf16[1,240,5120]{2,1,0:T(8,128)(2,1)}, u32[]{:S(2)}) copy-start(bf16[1,240,5120]{2,1,0:T(8,128)(2,1)} %param.5) | copy-start | bytes 7372804
  73.0 0.8 copy-start.3
  87.3 12.0 %collective-permute-start.5 = (f32[240,128]{1,0:T(8,128)S(1)}, f32[240,128]{1,0:T(8,128)S(1)}, u32[]{:S(2)}, u32[]{:S(2)}) collective-permute-start(f32[240,128]{1,0:T(8,128)S(1)} %fusion.18), channel_id=1, source_target_pairs={{0,128},{128,0},{1,129},{129,1},{2,130},{130,2},{3,131},{131,3},{4... | collective-permute-start | bytes 368648 | tf_op jit(solution)/shard_map/ppermute | solution.py:25
  99.3 18.1 %copy-start.4 = (bf16[2560,128]{1,0:T(8,128)(2,1)S(1)}, bf16[2560,128]{1,0:T(8,128)(2,1)}, u32[]{:S(2)}) copy-start(bf16[2560,128]{1,0:T(8,128)(2,1)} %copy-done.3) | copy-start | bytes 1966084
  99.3 5.1 %collective-permute-start.6 = (f32[240,128]{1,0:T(8,128)S(1)}, f32[240,128]{1,0:T(8,128)S(1)}, u32[]{:S(2)}, u32[]{:S(2)}) collective-permute-start(f32[240,128]{1,0:T(8,128)S(1)} %add.67), channel_id=1, source_target_pairs={{0,16},{16,0},{32,48},{48,32},{64,80},{80,64},{96,112},{112,96},{1... | collective-permute-start | bytes 368648 | tf_op jit(solution)/shard_map/ppermute | solution.py:25
  104.4 7.7 %collective-permute-start.7 = (f32[240,128]{1,0:T(8,128)S(1)}, f32[240,128]{1,0:T(8,128)S(1)}, u32[]{:S(2)}, u32[]{:S(2)}) collective-permute-start(f32[240,128]{1,0:T(8,128)S(1)} %add.68), channel_id=1, source_target_pairs={{0,32},{16,48},{32,0},{48,16},{64,96},{80,112},{96,64},{112,80},{1... | collective-permute-start | bytes 368648 | tf_op jit(solution)/shard_map/ppermute | solution.py:25
  112.2 11.8 %copy-start.7 = (f32[240,320]{0,1:T(8,128)S(1)}, f32[240,320]{0,1:T(8,128)}, u32[]{:S(2)}) copy-start(f32[240,320]{0,1:T(8,128)} %param.8) | copy-start | bytes 921604
  112.2 11.8 %copy-start.8 = (f32[240,320]{0,1:T(8,128)S(1)}, f32[240,320]{0,1:T(8,128)}, u32[]{:S(2)}) copy-start(f32[240,320]{0,1:T(8,128)} %param.9) | copy-start | bytes 921604
  112.2 11.5 %collective-permute-start.8 = (f32[240,128]{1,0:T(8,128)S(1)}, f32[240,128]{1,0:T(8,128)S(1)}, u32[]{:S(2)}, u32[]{:S(2)}) collective-permute-start(f32[240,128]{1,0:T(8,128)S(1)} %add.69), channel_id=1, source_target_pairs={{0,64},{16,80},{32,96},{48,112},{64,0},{80,16},{96,32},{112,48},{1... | collective-permute-start | bytes 368648 | tf_op jit(solution)/shard_map/ppermute | solution.py:25
  117.9 6.1 %copy-start.5 = (bf16[5120,128]{1,0:T(8,128)(2,1)}, bf16[5120,128]{1,0:T(8,128)(2,1)S(1)}, u32[]{:S(2)}) copy-start(bf16[5120,128]{1,0:T(8,128)(2,1)S(1)} %fusion) | copy-start | bytes 3932164
Sparse Core Ops, SparseCore 0:
  125.3 86.4 all-gather.1

commit v2 on v1

v2 whole, which is shorter than its diff:
```python
import functools

import jax
import jax.numpy as jnp
from jax import lax
from jax.experimental import pallas as pl
from jax.experimental.pallas import tpu as pltpu
from jax.sharding import Mesh, PartitionSpec as P

momentum_coef = 0.9
outer_rate = 0.7
momentum_part = outer_rate * momentum_coef * momentum_coef
approx_part = outer_rate * (1.0 + momentum_coef)

island = ("xh", "z")
fsdp = ("y", "xl", "core")
plane = ("xh", "y", "xl")
panel = 32
whole = pl.BlockSpec(memory_space=pltpu.VMEM)
anywhere = pl.BlockSpec(memory_space=pl.ANY)
scalars = pl.BlockSpec(memory_space=pltpu.SMEM)


def to_bf(values):
    return values.astype(jnp.bfloat16)


def to_f32(values):
    return values.astype(jnp.float32)


def times(left_mat, right_mat, left_dim=1, right_dim=0, precision=None):
    return lax.dot_general(
        left_mat,
        right_mat,
        (((left_dim,), (right_dim,)), ((), ())),
        precision=precision,
        preferred_element_type=jnp.float32,
    )


def shaped(shape, dtype):
    return jax.ShapeDtypeStruct(shape, dtype)


def near(shape, dtype):
    return pltpu.VMEM(shape, dtype)


def to_near(values):
    return pltpu.with_memory_space_constraint(values, pltpu.VMEM)


def to_far(values):
    return pltpu.with_memory_space_constraint(values, pltpu.HBM)


def params(size=16):
    return pltpu.CompilerParams(vmem_limit_bytes=size * 2**20)


def cost(flops, size):
    return pl.CostEstimate(flops=flops, bytes_accessed=size, transcendentals=0)


def fetch(source, target, sem):
    copy = pltpu.make_async_copy(source, target, sem)
    copy.start()
    return copy


def project_kernel(pieces, which, grad, error, basis, *rest):
    first = len(rest) > 6
    if first:
        master, momentum, left_out, merged_out, own_out, grads, errors, bases, sems, masters, momenta = rest
    else:
        left_out, merged_out, grads, errors, bases, sems = rest
    half = left_out.shape[1]
    width = half // pieces
    start = which[0] * half
    waits = [fetch(basis, bases, sems.at[0])]
    for piece in range(pieces):
        there = pl.ds(pl.multiple_of(start + piece * width, width), width)
        here = pl.ds(piece * width, width)
        waits.append(fetch(grad.at[:, there], grads.at[:, here], sems.at[1 + 2 * piece]))
        waits.append(fetch(error.at[:, there], errors.at[:, here], sems.at[2 + 2 * piece]))
    if first:
        waits.append(fetch(master, masters, sems.at[1 + 2 * pieces]))
        waits.append(fetch(momentum, momenta, sems.at[2 + 2 * pieces]))
    waits[0].wait()
    turned = to_bf(to_f32(bases[...]).T)
    for piece in range(pieces):
        here = slice(piece * width, (piece + 1) * width)
        waits[1 + 2 * piece].wait()
        waits[2 + 2 * piece].wait()
        merged = to_bf(to_f32(grads[:, here]) + to_f32(errors[:, here]))
        merged_out[:, here] = merged
        left_out[:, here] = times(turned, merged).astype(left_out.dtype)
    if first:
        waits[-2].wait()
        waits[-1].wait()
        own_out[...] = to_bf(masters[...] - momentum_part * momenta[...])


def project(which, grad, error, basis, dtype, master=None, momentum=None):
    rows, cols = grad.shape
    rank = basis.shape[1]
    half = cols // 2
    pieces = 5
    out_shape = [near((rank, half), dtype), near((rows, half), jnp.bfloat16)]
    operands = [which, to_far(grad), to_far(error), to_far(basis)]
    scratch = [
        pltpu.VMEM((rows, half), jnp.bfloat16),
        pltpu.VMEM((rows, half), jnp.bfloat16),
        pltpu.VMEM((rows, rank), jnp.bfloat16),
        pltpu.SemaphoreType.DMA((3 + 2 * pieces,)),
    ]
    if master is not None:
        operands += [to_far(master), to_far(momentum)]
        out_shape.append(near(master.shape, jnp.bfloat16))
        scratch += [pltpu.VMEM(master.shape, jnp.float32)] * 2
    return pl.pallas_call(
        functools.partial(project_kernel, pieces),
        in_specs=[scalars] + [anywhere] * (len(operands) - 1),
        out_specs=[whole] * len(out_shape),
        out_shape=out_shape,
        scratch_shapes=scratch,
        compiler_params=params(24),
        cost_estimate=cost(rows * cols * rank, 2 * rows * cols),
    )(*operands)


def combine_kernel(kept, received, own, across, mine_out, bundle_out):
    mine_out[...] = to_bf(kept[...] + to_f32(received[...]))
    bundle_out[0] = own[...]
    bundle_out[1] = across[...]


def combine(kept, received, own, across):
    return pl.pallas_call(
        combine_kernel,
        in_specs=[whole] * 4,
        out_specs=[whole] * 2,
        out_shape=[near(kept.shape, jnp.bfloat16), near((2,) + own.shape, own.dtype)],
        compiler_params=params(),
        cost_estimate=cost(kept.size, 8 * kept.size),
    )(to_near(kept), received, to_near(own), across)


def sum_kernel(chunks, *rest):
    out = rest[-1]
    total = to_f32(chunks[0])
    for place in range(1, chunks.shape[0]):
        total = total + to_f32(chunks[place])
    out[...] = total


def sum_chunks(chunks, after):
    return pl.pallas_call(
        sum_kernel,
        in_specs=[whole] + [anywhere] * len(after),
        out_specs=whole,
        out_shape=near(chunks.shape[1:], jnp.float32),
        compiler_params=params(),
        cost_estimate=cost(chunks.size, 2 * chunks.size),
    )(chunks, *[to_far(array) for array in after])


def spread_kernel(count, block, arrived, *rest):
    out = rest[-1]
    total = to_bf(block[...] + arrived[...])
    for place in range(count):
        out[place] = total


def spread(block, arrived, count, held):
    outs = pl.pallas_call(
        functools.partial(spread_kernel, count),
        in_specs=[whole, whole] + [anywhere] * len(held),
        out_specs=[anywhere] * len(held) + [whole],
        out_shape=[shaped(array.shape, array.dtype) for array in held]
        + [near((count,) + block.shape, jnp.bfloat16)],
        input_output_aliases={2 + place: place for place in range(len(held))},
        compiler_params=params(),
        cost_estimate=cost(block.size, 2 * count * block.size),
    )(to_near(block), arrived, *[to_far(array) for array in held])
    return outs[-1], outs[:-1]


def product_kernel(first, merged, left, *rest):
    values = left[...]
    product = times(merged[...], values, 1, 1)
    gram_mat = times(values, values, 1, 1)
    if first:
        product_out, gram_out = rest
    else:
        product_out, gram_out = rest[-2:]
        product = rest[0][...] + product
        gram_mat = rest[1][...] + gram_mat
    product_out[...] = product
    gram_out[...] = gram_mat


def product_of(merged, left, before=(), held=()):
    rows = merged.shape[0]
    rank = left.shape[0]
    outs = pl.pallas_call(
        functools.partial(product_kernel, not before),
        in_specs=[whole] * (2 + len(before)) + [anywhere] * len(held),
        out_specs=[anywhere] * len(held) + [whole] * 2,
        out_shape=[shaped(array.shape, array.dtype) for array in held]
        + [near((rows, rank), jnp.float32), near((rank, rank), jnp.float32)],
        input_output_aliases={2 + len(before) + place: place for place in range(len(held))},
        compiler_params=params(),
        cost_estimate=cost(2 * rows * left.size, 4 * left.size),
    )(to_near(merged), left, *[to_near(array) for array in before], *[to_far(array) for array in held])
    return outs[-2:], outs[:-2]


def factor_kernel(start, state, *refs):
    rank = state.shape[0]
    stop = start + panel
    exact = lax.Precision.HIGHEST
    state_out, inverse_out = refs[-2:]
    if start == 0:
        full_row = lax.broadcasted_iota(jnp.int32, (rank, rank), 0)
        full_col = lax.broadcasted_iota(jnp.int32, (rank, rank), 1)
        inverse = jnp.where(full_row == full_col, 1.0, 0.0)
    else:
        inverse = refs[0]
    rows = state[start:stop, :]
    below = inverse[start:stop, :]
    small = rows[:, start:stop]
    row_of = lax.broadcasted_iota(jnp.int32, (panel, panel), 0)
    col_of = lax.broadcasted_iota(jnp.int32, (panel, panel), 1)
    turned = jnp.where(row_of == col_of, 1.0, 0.0)
    for k in range(panel):
        column = small[:, k : k + 1]
        pivot = small[k : k + 1, k : k + 1]
        factor = jnp.where(row_of[:, :1] > k, column / pivot, 0.0)
        small = small - factor * small[k : k + 1, :]
        turned = turned - factor * turned[k : k + 1, :]
    diagonal = jnp.sum(jnp.where(row_of == col_of, small, 0.0), axis=1, keepdims=True)
    turned = turned * lax.rsqrt(diagonal)
    rows = times(turned, rows, precision=exact)
    below = times(turned, below, precision=exact)
    if start > 0:
        inverse_out[0:start, :] = inverse[0:start, :]
    inverse_out[start:stop, :] = below
    if stop < rank:
        later = rows.T[stop:, :]
        state_out[0:stop, :] = state[0:stop, :]
        state_out[stop:, :] = state[stop:, :] - times(later, rows, precision=exact)
        inverse_out[stop:, :] = inverse[stop:, :] - times(later, below, precision=exact)
    else:
        state_out[...] = state[...]


def factor_step(start, state, *inverse):
    rank = state.shape[0]
    return pl.pallas_call(
        functools.partial(factor_kernel, start),
        in_specs=[whole] * (1 + len(inverse)),
        out_specs=[whole, whole],
        out_shape=[near((rank, rank), jnp.float32)] * 2,
        compiler_params=params(),
        cost_estimate=cost(10**9, 4 * rank * rank * 4),
    )(*[to_near(array) for array in (state, *inverse)])


def basis_kernel(which, inverse, mine, other, out):
    half = mine.shape[1]
    value = inverse[...]
    high = to_bf(value)
    low = to_bf(value - to_f32(high))

    def put(left, start):
        left = left[...]
        basis = times(high, left) + times(low, left)
        out[:, pl.ds(pl.multiple_of(start, half), half)] = to_bf(basis)

    put(mine, which[0] * half)
    put(other, (1 - which[0]) * half)


def basis_of(which, inverse, mine, other):
    rank, half = mine.shape
    return pl.pallas_call(
        basis_kernel,
        in_specs=[pl.BlockSpec(memory_space=pltpu.SMEM), whole, whole, whole],
        out_specs=whole,
        out_shape=near((rank, 2 * half), jnp.bfloat16),
        compiler_params=params(),
        cost_estimate=cost(8 * rank * rank * half, 8 * rank * half),
    )(which, to_near(inverse), mine, other)


def final_kernel(
    islands, pieces, which, inverse, product, arrived, basis, merged_mine, merged_other, carried, block, master,
    momentum, error_out, weights_out, master_out, momentum_out, errors, weights, masters, momenta, sems,
):
    total = product[...] + arrived[...]
    q_avg = to_bf(times(total, inverse[...], 1, 1, lax.Precision.HIGHEST) / islands)
    half = merged_mine.shape[1]
    width = half // pieces
    waits = []
    for number, merged in enumerate((merged_mine, merged_other)):
        start = lax.rem(which[0] + number, 2) * half
        for piece in range(pieces):
            lanes = pl.ds(pl.multiple_of(start + piece * width, width), width)
            approx = times(q_avg, basis[:, lanes])
            errors[:, lanes] = to_bf(to_f32(merged[:, piece * width : (piece + 1) * width]) - approx)
            waits.append(fetch(errors.at[:, lanes], error_out.at[:, lanes], sems.at[len(waits)]))
            weights[:, lanes] = to_bf(to_f32(carried[:, lanes]) - approx_part * approx)
            waits.append(fetch(weights.at[:, lanes], weights_out.at[:, lanes], sems.at[len(waits)]))
    update = times(block[...], q_avg, 1, 1)
    momentum_next = momentum_coef * momentum[...] + update
    momenta[...] = momentum_next
    waits.append(fetch(momenta, momentum_out, sems.at[len(waits)]))
    masters[...] = master[...] - outer_rate * (update + momentum_coef * momentum_next)
    waits.append(fetch(masters, master_out, sems.at[len(waits)]))
    for copy in waits:
        copy.wait()


def final(islands, which, inverse, product, arrived, basis, mine, other, carried, block, master, momentum):
    rows, half = mine.shape
    rank = basis.shape[0]
    cols = 2 * half
    own = master.shape
    pieces = 5
    return pl.pallas_call(
        functools.partial(final_kernel, islands, pieces),
        in_specs=[scalars] + [whole] * 10,
        out_specs=[anywhere] * 4,
        out_shape=[
            shaped((rows, cols), jnp.bfloat16),
            shaped((rows, cols), jnp.bfloat16),
            shaped(own, jnp.float32),
            shaped(own, jnp.float32),
        ],
        scratch_shapes=[pltpu.VMEM((rows, cols), jnp.bfloat16)] * 2
        + [pltpu.VMEM(own, jnp.float32)] * 2
        + [pltpu.SemaphoreType.DMA((4 * pieces + 2,))],
        compiler_params=params(24),
        cost_estimate=cost(2 * rows * cols * rank, 8 * rows * cols),
    )(
        which, to_near(inverse), to_near(product), arrived, to_near(basis), to_near(mine), to_near(other),
        to_near(carried), block, master, momentum,
    )


def gather_kernel(shifts, place, _, *refs):
    pieces, out, held, sems = refs[:-3], refs[-3], refs[-2], refs[-1]
    size = pieces[0].shape[1]
    count = len(shifts)
    waits = []
    for number in range(count):
        z_of = lax.rem(place[1] + (shifts[number] + count), count)
        rows = pl.ds(pl.multiple_of(z_of * size, size), size)
        for side in range(2):
            waits.append(fetch(pieces[number].at[side], held.at[side, rows], sems.at[len(waits)]))
    for copy in waits:
        copy.wait()
    span = count * size
    for side in range(2):
        start = lax.rem(place[0] + side, 2) * span
        for first in range(0, span, 2 * size):
            lanes = pl.ds(pl.multiple_of(start + first, 128), 2 * size)
            out[:, lanes] = to_bf(to_f32(held[side, first : first + 2 * size, :]).T)


def gather_pieces(place, pieces, shifts, after):
    rows, cols = pieces[0].shape[1:]
    count = 2 * len(pieces)
    return pl.pallas_call(
        functools.partial(gather_kernel, shifts),
        in_specs=[scalars] + [anywhere] * (1 + len(pieces)),
        out_specs=whole,
        out_shape=near((cols, count * rows), jnp.bfloat16),
        scratch_shapes=[
            pltpu.VMEM((2, len(pieces) * rows, cols), jnp.bfloat16),
            pltpu.SemaphoreType.DMA((count,)),
        ],
        compiler_params=params(),
        cost_estimate=cost(10**9, 4 * count * rows * cols),
    )(place, after, *pieces)


def add_kernel(first, second, *rest):
    rest[-1][...] = first[...] + second[...]


def add_after(first, second, after, held=()):
    outs = pl.pallas_call(
        add_kernel,
        in_specs=[whole, whole, anywhere] + [anywhere] * len(held),
        out_specs=[anywhere] * len(held) + [whole],
        out_shape=[shaped(array.shape, array.dtype) for array in held] + [near(first.shape, first.dtype)],
        input_output_aliases={3 + place: place for place in range(len(held))},
        compiler_params=params(),
        cost_estimate=cost(first.size, 12 * first.size),
    )(to_near(first), second, after, *[to_far(array) for array in held])
    return outs[-1], outs[:-1]


def shift(values, by):
    return lax.ppermute(values, "z", [(place, (place + by) % 8) for place in range(8)])


def swap(values, axis, size, bit):
    return lax.ppermute(values, axis, [(place, place ^ bit) for place in range(size)])


def shift(values, by):
    return lax.ppermute(values, "z", [(place, (place + by) % 8) for place in range(8)])


def local(pseudo_grad, error_buffer, basis_prev, master_weights, outer_momentum):
    core = lax.axis_index("core").astype(jnp.int32)
    rank = basis_prev.shape[1]
    grad, error = pseudo_grad[0], error_buffer[0]
    half = grad.shape[1] // 2
    which_mine, which_other = core.reshape(1), (1 - core).reshape(1)
    place = jnp.stack([lax.axis_index("xh"), lax.axis_index("z")]).astype(jnp.int32)
    master, momentum = master_weights.T, outer_momentum.T

    given, merged_other, own = project(which_other, grad, error, basis_prev, jnp.bfloat16, master, momentum)
    received = swap(given, "core", 2, 1)
    across = swap(own, "xh", 2, 1)
    kept, merged_mine = project(which_mine, grad, error, basis_prev, jnp.float32)
    mine, bundle = combine(kept, received, own, across)
    up, down = shift(bundle, 1), shift(bundle, -1)
    chunks = lax.all_to_all(mine.reshape(16, rank // 16, half), plane, 0, 0, tiled=True)
    block = sum_chunks(chunks, (up, down))
    for bit in (1, 2):
        block = block + swap(block, "z", 8, bit)
    copies, (up, down) = spread(block, swap(block, "z", 8, 4), 16, (up, down))
    pieces = [bundle, up, down]
    up, down = shift(up, 1), shift(down, -1)
    mine = lax.all_to_all(copies, plane, 0, 0, tiled=True).reshape(rank, half)
    other = swap(mine, "core", 2, 1)

    before, _ = product_of(merged_mine, mine)
    (product, gram_mat), (up, down) = product_of(merged_other, other, before, (up, down))
    pieces += [up, down]
    up, down = shift(up, 1), shift(down, -1)

    state, inverse = factor_step(0, gram_mat)
    state, inverse = factor_step(panel, state, inverse)
    product, _ = add_after(product, swap(product, "xh", 2, 1), state)
    state, inverse = factor_step(2 * panel, state, inverse)
    product, (up,) = add_after(product, swap(product, "z", 8, 1), state, (up,))
    pieces += [up, down]
    up = shift(up, 1)
    _, inverse = factor_step(3 * panel, state, inverse)
    basis_bf = basis_of(which_mine, inverse, mine, other)
    product, _ = add_after(product, swap(product, "z", 8, 2), basis_bf)
    pieces.append(up)
    arrived = swap(product, "z", 8, 4)
    carried = gather_pieces(place, pieces, (0, -1, 1, -2, 2, -3, 3, -4), product)

    col_count = master.shape[0]
    col_start = lax.axis_index(island) * col_count
    basis_block = lax.dynamic_slice_in_dim(basis_bf, col_start, col_count, 1).T
    error_next, weights_next, master_next, momentum_next = final(
        16, which_mine, inverse, product, arrived, basis_bf, merged_mine, merged_other, carried, basis_block,
        master, momentum,
    )
    return (error_next[None], weights_next, master_next.T, momentum_next.T)


def solution(mesh):
    fine = Mesh(mesh.devices.reshape(2, 8, 4, 2, 2), island + fsdp)
    in_specs = (
        P(island, fsdp, None),
        P(island, fsdp, None),
        P(fsdp, None),
        P(fsdp, island),
        P(fsdp, island),
    )
    out_specs = (
        P(island, fsdp, None),
        P(fsdp, None),
        P(fsdp, island),
        P(fsdp, island),
    )
    return jax.shard_map(local, mesh=fine, in_specs=in_specs, out_specs=out_specs, check_vma=False)
```

time: 230 us -> 131 us (0.57)
  the two profiles are of different devices: /device:TPU:8 before, /device:TPU:96 now
where the time goes in v2:
time: 131 us
  waiting for transfers between devices  42.4 us (32%)
  starting transfers between devices  35.8 us (27%)
  Pallas kernels  29.7 us (23%)
  blocking collectives  15.8 us (12%)
  local copies, waits for them, and re-layouts  5.84 us (4%)
    ppermute x10, waiting for transfers between devices, swap(): lax.ppermute(values, axis, [(place, place ^ bit) for place in range(size)])  22.2 us
    ppermute x7, waiting for transfers between devices, shift(): lax.ppermute(values, 'z', [(place, (place + by) % 8) for place in range(8)])  18.1 us
    ppermute x10, starting transfers between devices, swap(): lax.ppermute(values, axis, [(place, place ^ bit) for place in range(size)])  16.4 us
    all_to_all x1, blocking collectives, local(): mine = lax.all_to_all(copies, plane, 0, 0, tiled=True).reshape(rank, half)  15.8 us
    pallas_call x4, Pallas kernels, factor_step(): pl.pallas_call(functools.partial(factor_kernel, start), in_specs=[whole]...  12.5 us
    ppermute x7, starting transfers between devices, shift(): lax.ppermute(values, 'z', [(place, (place + by) % 8) for place in range(8)])  12.3 us
    all_to_all x1, starting transfers between devices, local(): lax.all_to_all(mine.reshape(16, rank // 16, half), plane, 0, 0, tiled=True)  7.08 us
    unnamed x37, local copies, waits for them, and re-layouts  5.74 us
  transfers between devices with their start and end apart: 18, of which 9 were waited for; matrix products, arithmetic and copies ran while one was open for 0% of the time, Pallas kernels for 16%

profile of v2, /device:TPU:96, one launch (start us, length us, event | category | flops | bytes accessed | tf_op | source)
XLA Modules:
  0.0 130.6 jit_solution(3773362446342986305)
XLA Ops:
  0.6 2.4 %shard_map.84 = (bf16[128,2560]{1,0:T(8,128)(2,1)S(1)}, bf16[240,2560]{1,0:T(8,128)(2,1)S(1)}, bf16[320,240]{1,0:T(8,128)(2,1)S(1)}) custom-call(s32[1]{0:T(128)} %bitcast.1.which, bf16[240,5120]{1,0:T(8,128)(2,1)} %bitcast.22, bf16[240,5120]{1,0:T(8,128)(2,1)} %bitcast.24, bf16[240,128]{1,0:T(8,128)(2,1)} %basis.3, f32[320,240]{1,0:T(8,128)} %bitcast.17, ...), custom_call_target="tpu_custom_call" | custom-call | flops 157286400 | bytes 2457600 | tf_op jit(solution)/shard_map/pallas_call | solution.py:122
  3.1 3.1 %collective-permute-start.1 = (bf16[320,240]{1,0:T(8,128)(2,1)S(1)}, bf16[320,240]{1,0:T(8,128)(2,1)S(1)}, u32[]{:S(2)}, u32[]{:S(2)}) collective-permute-start(bf16[320,240]{1,0:T(8,128)(2,1)S(1)} %get-tuple-element.36.own), channel_id=1, source_target_pairs={{0,128},{128,0},{1,129},{129,1},{2,130},{130,2},{3,131},{131,3},{4... | collective-permute-start | bytes 460808 | tf_op jit(solution)/shard_map/ppermute | solution.py:412
  6.3 2.3 %shard_map.85 = (f32[128,2560]{1,0:T(8,128)S(1)}, bf16[240,2560]{1,0:T(8,128)(2,1)S(1)}) custom-call(s32[1]{0:T(128)} %bitcast.which, bf16[240,5120]{1,0:T(8,128)(2,1)} %bitcast.23, bf16[240,5120]{1,0:T(8,128)(2,1)} %bitcast.25, bf16[240,128]{1,0:T(8,128)(2,1)} %basis.3), custom_call_target="tpu_custom_call" | custom-call | flops 157286400 | bytes 2457600 | tf_op jit(solution)/shard_map/pallas_call | solution.py:122
  8.6 2.7 %collective-permute-done.1.across = bf16[320,240]{1,0:T(8,128)(2,1)S(1)} collective-permute-done((bf16[320,240]{1,0:T(8,128)(2,1)S(1)}, bf16[320,240]{1,0:T(8,128)(2,1)S(1)}, u32[]{:S(2)}, u32[]{:S(2)}) %collective-permute-start.1) | collective-permute-done | bytes 153632 | tf_op jit(solution)/shard_map/ppermute | solution.py:412
  11.3 1.0 shard_map.86
  13.0 7.1 %all-to-all-start = ((bf16[16,8,2560]{2,1,0:T(8,128)(2,1)}), bf16[16,8,2560]{2,1,0:T(8,128)(2,1)}, u32[]{:S(2)}, u32[]{:S(2)}) async-start(bf16[16,8,2560]{2,1,0:T(8,128)(2,1)} %bitcast.6), calls=%async_computation | async-start | bytes 1310720 | tf_op jit(solution)/shard_map/all_to_all | solution.py:434
  20.3 3.1 %collective-permute-start.2 = (bf16[2,320,240]{2,1,0:T(8,128)(2,1)}, bf16[2,320,240]{2,1,0:T(8,128)(2,1)S(1)}, u32[]{:S(2)}, u32[]{:S(2)}) collective-permute-start(bf16[2,320,240]{2,1,0:T(8,128)(2,1)} %copy-done.14), channel_id=1, source_target_pairs={{0,16},{16,32},{32,48},{48,64},{64,80},{80,96},{96,112},{112,0},{1... | collective-permute-start | bytes 921608 | tf_op jit(solution)/shard_map/ppermute | solution.py:416
  23.4 7.3 %collective-permute-done.3.rest_1_ = bf16[2,320,240]{2,1,0:T(8,128)(2,1)S(1)} collective-permute-done((bf16[2,320,240]{2,1,0:T(8,128)(2,1)}, bf16[2,320,240]{2,1,0:T(8,128)(2,1)S(1)}, u32[]{:S(2)}, u32[]{:S(2)}) %collective-permute-start.3) | collective-permute-done | bytes 307232 | tf_op jit(solution)/shard_map/ppermute | solution.py:416
  30.8 2.1 %all-to-all-done.chunks = bf16[16,8,2560]{2,1,0:T(8,128)(2,1)} async-done(((bf16[16,8,2560]{2,1,0:T(8,128)(2,1)}), bf16[16,8,2560]{2,1,0:T(8,128)(2,1)}, u32[]{:S(2)}, u32[]{:S(2)}) %all-to-all-start) | async-done | bytes 655392 | tf_op jit(solution)/shard_map/all_to_all | solution.py:434
  32.9 1.2 shard_map.87
  34.3 4.3 %collective-permute-done.4 = f32[8,2560]{1,0:T(8,128)S(1)} collective-permute-done((f32[8,2560]{1,0:T(8,128)S(1)}, f32[8,2560]{1,0:T(8,128)S(1)}, u32[]{:S(2)}, u32[]{:S(2)}) %collective-permute-start.4) | collective-permute-done | bytes 81952 | tf_op jit(solution)/shard_map/ppermute | solution.py:412
  38.6 1.8 %collective-permute-start.5 = (f32[8,2560]{1,0:T(8,128)S(1)}, f32[8,2560]{1,0:T(8,128)S(1)}, u32[]{:S(2)}, u32[]{:S(2)}) collective-permute-start(f32[8,2560]{1,0:T(8,128)S(1)} %add.12), channel_id=1, source_target_pairs={{0,32},{16,48},{32,0},{48,16},{64,96},{80,112},{96,64},{112,80},{1... | collective-permute-start | bytes 245768 | tf_op jit(solution)/shard_map/ppermute | solution.py:412
  40.5 4.5 %collective-permute-done.5 = f32[8,2560]{1,0:T(8,128)S(1)} collective-permute-done((f32[8,2560]{1,0:T(8,128)S(1)}, f32[8,2560]{1,0:T(8,128)S(1)}, u32[]{:S(2)}, u32[]{:S(2)}) %collective-permute-start.5) | collective-permute-done | bytes 81952 | tf_op jit(solution)/shard_map/ppermute | solution.py:412
  44.9 4.6 %collective-permute-start.6 = (f32[8,2560]{1,0:T(8,128)S(1)}, f32[8,2560]{1,0:T(8,128)S(1)}, u32[]{:S(2)}, u32[]{:S(2)}) collective-permute-start(f32[8,2560]{1,0:T(8,128)S(1)} %add.13.block), channel_id=1, source_target_pairs={{0,64},{16,80},{32,96},{48,112},{64,0},{80,16},{96,32},{112,48},{1... | collective-permute-start | bytes 245768 | tf_op jit(solution)/shard_map/ppermute | solution.py:412
  49.5 3.9 %collective-permute-done.6.arrived = f32[8,2560]{1,0:T(8,128)S(1)} collective-permute-done((f32[8,2560]{1,0:T(8,128)S(1)}, f32[8,2560]{1,0:T(8,128)S(1)}, u32[]{:S(2)}, u32[]{:S(2)}) %collective-permute-start.6) | collective-permute-done | bytes 81952 | tf_op jit(solution)/shard_map/ppermute | solution.py:412
  53.4 15.8 %all_to_all.10 = bf16[16,8,2560]{2,1,0:T(8,128)(2,1)S(1)} all-to-all(bf16[16,8,2560]{2,1,0:T(8,128)(2,1)S(1)} %get-tuple-element.39), channel_id=1, replica_groups=mesh['xh'=2,'z'=8,'y'=4,'xl'=2,'core'=2] {'xh','y','xl'}, dimensions={0} | all-to-all | bytes 1310720 | tf_op jit(solution)/shard_map/all_to_all | solution.py:441
  69.2 4.8 %collective-permute-start.8 = (bf16[2,320,240]{2,1,0:T(8,128)(2,1)}, bf16[2,320,240]{2,1,0:T(8,128)(2,1)S(1)}, u32[]{:S(2)}, u32[]{:S(2)}) collective-permute-start(bf16[2,320,240]{2,1,0:T(8,128)(2,1)} %get-tuple-element.43.refs_1_), channel_id=1, source_target_pairs={{0,16},{16,32},{32,48},{48,64},{64,80},{80,96},{96,112},{112,0},{1... | collective-permute-start | bytes 921608 | tf_op jit(solution)/shard_map/ppermute | solution.py:416
  74.7 7.3 %collective-permute-done.8.rest_2_ = bf16[2,320,240]{2,1,0:T(8,128)(2,1)S(1)} collective-permute-done((bf16[2,320,240]{2,1,0:T(8,128)(2,1)}, bf16[2,320,240]{2,1,0:T(8,128)(2,1)S(1)}, u32[]{:S(2)}, u32[]{:S(2)}) %collective-permute-start.8) | collective-permute-done | bytes 307232 | tf_op jit(solution)/shard_map/ppermute | solution.py:416
  82.0 3.4 %collective-permute-done.9.rest_3_ = bf16[2,320,240]{2,1,0:T(8,128)(2,1)} collective-permute-done((bf16[2,320,240]{2,1,0:T(8,128)(2,1)}, bf16[2,320,240]{2,1,0:T(8,128)(2,1)}, u32[]{:S(2)}, u32[]{:S(2)}) %collective-permute-start.9) | collective-permute-done | bytes 307232 | tf_op jit(solution)/shard_map/ppermute | solution.py:416
  86.2 1.3 collective-permute-start.10
  88.3 3.0 %shard_map.91 = (f32[128,128]{1,0:T(8,128)S(1)}, f32[128,128]{1,0:T(8,128)S(1)}) custom-call(f32[128,128]{1,0:T(8,128)S(1)} %get-tuple-element.45.state), custom_call_target="tpu_custom_call" | custom-call | flops 1000000000 | bytes 262144 | tf_op jit(solution)/shard_map/pallas_call | solution.py:261
  91.4 3.1 %shard_map.92 = (f32[128,128]{1,0:T(8,128)S(1)}, f32[128,128]{1,0:T(8,128)S(1)}) custom-call(f32[128,128]{1,0:T(8,128)S(1)} %get-tuple-element.46.state, f32[128,128]{1,0:T(8,128)S(1)} %get-tuple-element.47.refs_0_), custom_call_target="tpu_custom_call" | custom-call | flops 1000000000 | bytes 262144 | tf_op jit(solution)/shard_map/pallas_call | solution.py:261
  94.5 1.3 collective-permute-start.11
  96.6 3.1 %shard_map.93 = (f32[128,128]{1,0:T(8,128)S(1)}, f32[128,128]{1,0:T(8,128)S(1)}) custom-call(f32[128,128]{1,0:T(8,128)S(1)} %get-tuple-element.48.state.rest_0_, f32[128,128]{1,0:T(8,128)S(1)} %get-tuple-element.49.refs_0_), custom_call_target="tpu_custom_call" | custom-call | flops 1000000000 | bytes 262144 | tf_op jit(solution)/shard_map/pallas_call | solution.py:261
  100.5 2.5 %collective-permute-start.16 = (bf16[2,320,240]{2,1,0:T(8,128)(2,1)}, bf16[2,320,240]{2,1,0:T(8,128)(2,1)}, u32[]{:S(2)}, u32[]{:S(2)}) collective-permute-start(bf16[2,320,240]{2,1,0:T(8,128)(2,1)} %get-tuple-element.57.refs_5_), channel_id=1, source_target_pairs={{0,16},{16,32},{32,48},{48,64},{64,80},{80,96},{96,112},{112,0},{1... | collective-permute-start | bytes 921608 | tf_op jit(solution)/shard_map/ppermute | solution.py:416
  103.1 1.4 %collective-permute-start.13 = (f32[240,128]{1,0:T(8,128)S(1)}, f32[240,128]{1,0:T(8,128)S(1)}, u32[]{:S(2)}, u32[]{:S(2)}) collective-permute-start(f32[240,128]{1,0:T(8,128)S(1)} %get-tuple-element.55.first), channel_id=1, source_target_pairs={{0,32},{16,48},{32,0},{48,16},{64,96},{80,112},{96,64},{112,80},{1... | collective-permute-start | bytes 368648 | tf_op jit(solution)/shard_map/ppermute | solution.py:412
  104.5 3.3 %shard_map.94 = (f32[128,128]{1,0:T(8,128)}, f32[128,128]{1,0:T(8,128)S(1)}) custom-call(f32[128,128]{1,0:T(8,128)S(1)} %get-tuple-element.50.state.rest_0_, f32[128,128]{1,0:T(8,128)S(1)} %get-tuple-element.51.refs_0_), custom_call_target="tpu_custom_call" | custom-call | flops 1000000000 | bytes 262144 | tf_op jit(solution)/shard_map/pallas_call | solution.py:261
  108.6 6.8 %collective-permute-done.13.second = f32[240,128]{1,0:T(8,128)S(1)} collective-permute-done((f32[240,128]{1,0:T(8,128)S(1)}, f32[240,128]{1,0:T(8,128)S(1)}, u32[]{:S(2)}, u32[]{:S(2)}) %collective-permute-start.13) | collective-permute-done | bytes 122912 | tf_op jit(solution)/shard_map/ppermute | solution.py:412
  115.5 2.6 %collective-permute-start.14 = (f32[240,128]{1,0:T(8,128)S(1)}, f32[240,128]{1,0:T(8,128)S(1)}, u32[]{:S(2)}, u32[]{:S(2)}) collective-permute-start(f32[240,128]{1,0:T(8,128)S(1)} %shard_map.98._.product), channel_id=1, source_target_pairs={{0,64},{16,80},{32,96},{48,112},{64,0},{80,16},{96,32},{112,48},{1... | collective-permute-start | bytes 368648 | tf_op jit(solution)/shard_map/ppermute | solution.py:412
  118.4 1.1 copy-done.5
  122.3 4.8 %shard_map.99.carried = bf16[240,5120]{1,0:T(8,128)(2,1)S(1)} custom-call(s32[2]{0:T(128)S(1)} %pad_add_fusion.place, f32[240,128]{1,0:T(8,128)S(1)} %shard_map.98._.product, bf16[2,320,240]{2,1,0:T(8,128)(2,1)S(1)} %copy-done.15, bf16[2,320,240]{2,1,0:T(8,128)(2,1)S(1)} %copy-done.5, bf16[2,320,240]{2,1,0:T(8,128)(2,1)S(1)} %copy-done.3, ...), custom_call_target="tpu_custom_call" | custom-call | flops 1000000000 | bytes 4915200 | tf_op jit(solution)/shard_map/pallas_call | solution.py:376
  127.2 3.3 %shard_map.100 = (bf16[240,5120]{1,0:T(8,128)(2,1)}, bf16[240,5120]{1,0:T(8,128)(2,1)}, f32[320,240]{1,0:T(8,128)}, f32[320,240]{1,0:T(8,128)}) custom-call(s32[1]{0:T(128)} %bitcast.which, f32[128,128]{1,0:T(8,128)S(1)} %copy-done.17, f32[240,128]{1,0:T(8,128)S(1)} %shard_map.98._.product, f32[240,128]{1,0:T(8,128)S(1)} %collective-permute-done.14.arrived, ...), custom_call_target="tpu_custom_call" | custom-call | flops 314572800 | bytes 9830400 | tf_op jit(solution)/shard_map/pallas_call | solution.py:332
  (63 shorter events, 9.3 us)
Async XLA Ops:
  3.0 82.4 %copy-start = (bf16[240,2560]{1,0:T(8,128)(2,1)}, bf16[240,2560]{1,0:T(8,128)(2,1)S(1)}, u32[]{:S(2)}) copy-start(bf16[240,2560]{1,0:T(8,128)(2,1)S(1)} %get-tuple-element.33.merged.merged_other) | copy-start | bytes 3686404
  3.0 8.2 %collective-permute-start = (bf16[128,2560]{1,0:T(8,128)(2,1)S(1)}, bf16[128,2560]{1,0:T(8,128)(2,1)S(1)}, u32[]{:S(2)}, u32[]{:S(2)}) collective-permute-start(bf16[128,2560]{1,0:T(8,128)(2,1)S(1)} %get-tuple-element.35), channel_id=1, source_target_pairs={{0,1},{1,0},{2,3},{3,2},{4,5},{5,4},{6,7},{7,6},{8,9},{9,8},{10,11... | collective-permute-start | bytes 1966088 | tf_op jit(solution)/shard_map/ppermute | solution.py:412
  3.1 8.1 %collective-permute-start.1 = (bf16[320,240]{1,0:T(8,128)(2,1)S(1)}, bf16[320,240]{1,0:T(8,128)(2,1)S(1)}, u32[]{:S(2)}, u32[]{:S(2)}) collective-permute-start(bf16[320,240]{1,0:T(8,128)(2,1)S(1)} %get-tuple-element.36.own), channel_id=1, source_target_pairs={{0,128},{128,0},{1,129},{129,1},{2,130},{130,2},{3,131},{131,3},{4... | collective-permute-start | bytes 460808 | tf_op jit(solution)/shard_map/ppermute | solution.py:412
  13.0 19.9 %all-to-all-start = ((bf16[16,8,2560]{2,1,0:T(8,128)(2,1)}), bf16[16,8,2560]{2,1,0:T(8,128)(2,1)}, u32[]{:S(2)}, u32[]{:S(2)}) async-start(bf16[16,8,2560]{2,1,0:T(8,128)(2,1)} %bitcast.6), calls=%async_computation | async-start | bytes 1310720 | tf_op jit(solution)/shard_map/all_to_all | solution.py:434
  20.1 10.7 %collective-permute-start.3 = (bf16[2,320,240]{2,1,0:T(8,128)(2,1)}, bf16[2,320,240]{2,1,0:T(8,128)(2,1)S(1)}, u32[]{:S(2)}, u32[]{:S(2)}) collective-permute-start(bf16[2,320,240]{2,1,0:T(8,128)(2,1)} %copy-done.14), channel_id=1, source_target_pairs={{0,112},{16,0},{32,16},{48,32},{64,48},{80,64},{96,80},{112,96},{1... | collective-permute-start | bytes 921608 | tf_op jit(solution)/shard_map/ppermute | solution.py:416
  20.3 10.5 %collective-permute-start.2 = (bf16[2,320,240]{2,1,0:T(8,128)(2,1)}, bf16[2,320,240]{2,1,0:T(8,128)(2,1)S(1)}, u32[]{:S(2)}, u32[]{:S(2)}) collective-permute-start(bf16[2,320,240]{2,1,0:T(8,128)(2,1)} %copy-done.14), channel_id=1, source_target_pairs={{0,16},{16,32},{32,48},{48,64},{64,80},{80,96},{96,112},{112,0},{1... | collective-permute-start | bytes 921608 | tf_op jit(solution)/shard_map/ppermute | solution.py:416
  30.7 2.2 %copy-start.2 = (bf16[2,320,240]{2,1,0:T(8,128)(2,1)}, bf16[2,320,240]{2,1,0:T(8,128)(2,1)S(1)}, u32[]{:S(2)}) copy-start(bf16[2,320,240]{2,1,0:T(8,128)(2,1)S(1)} %collective-permute-done.3.rest_1_) | copy-start | bytes 921604
  30.8 2.1 %copy-start.4 = (bf16[2,320,240]{2,1,0:T(8,128)(2,1)}, bf16[2,320,240]{2,1,0:T(8,128)(2,1)S(1)}, u32[]{:S(2)}) copy-start(bf16[2,320,240]{2,1,0:T(8,128)(2,1)S(1)} %collective-permute-done.2.rest_0_) | copy-start | bytes 921604
  34.1 4.5 %collective-permute-start.4 = (f32[8,2560]{1,0:T(8,128)S(1)}, f32[8,2560]{1,0:T(8,128)S(1)}, u32[]{:S(2)}, u32[]{:S(2)}) collective-permute-start(f32[8,2560]{1,0:T(8,128)S(1)} %shard_map.87), channel_id=1, source_target_pairs={{0,16},{16,0},{32,48},{48,32},{64,80},{80,64},{96,112},{112,96},{1... | collective-permute-start | bytes 245768 | tf_op jit(solution)/shard_map/ppermute | solution.py:412
  38.6 6.3 %collective-permute-start.5 = (f32[8,2560]{1,0:T(8,128)S(1)}, f32[8,2560]{1,0:T(8,128)S(1)}, u32[]{:S(2)}, u32[]{:S(2)}) collective-permute-start(f32[8,2560]{1,0:T(8,128)S(1)} %add.12), channel_id=1, source_target_pairs={{0,32},{16,48},{32,0},{48,16},{64,96},{80,112},{96,64},{112,80},{1... | collective-permute-start | bytes 245768 | tf_op jit(solution)/shard_map/ppermute | solution.py:412
  44.9 8.4 %collective-permute-start.6 = (f32[8,2560]{1,0:T(8,128)S(1)}, f32[8,2560]{1,0:T(8,128)S(1)}, u32[]{:S(2)}, u32[]{:S(2)}) collective-permute-start(f32[8,2560]{1,0:T(8,128)S(1)} %add.13.block), channel_id=1, source_target_pairs={{0,64},{16,80},{32,96},{48,112},{64,0},{80,16},{96,32},{112,48},{1... | collective-permute-start | bytes 245768 | tf_op jit(solution)/shard_map/ppermute | solution.py:412
  69.2 16.2 %collective-permute-start.7 = (bf16[128,2560]{1,0:T(8,128)(2,1)S(1)}, bf16[128,2560]{1,0:T(8,128)(2,1)S(1)}, u32[]{:S(2)}, u32[]{:S(2)}) collective-permute-start(bf16[128,2560]{1,0:T(8,128)(2,1)S(1)} %bitcast.14), channel_id=1, source_target_pairs={{0,1},{1,0},{2,3},{3,2},{4,5},{5,4},{6,7},{7,6},{8,9},{9,8},{10,11... | collective-permute-start | bytes 1966088 | tf_op jit(solution)/shard_map/ppermute | solution.py:412
  69.2 12.8 %collective-permute-start.8 = (bf16[2,320,240]{2,1,0:T(8,128)(2,1)}, bf16[2,320,240]{2,1,0:T(8,128)(2,1)S(1)}, u32[]{:S(2)}, u32[]{:S(2)}) collective-permute-start(bf16[2,320,240]{2,1,0:T(8,128)(2,1)} %get-tuple-element.43.refs_1_), channel_id=1, source_target_pairs={{0,16},{16,32},{32,48},{48,64},{64,80},{80,96},{96,112},{112,0},{1... | collective-permute-start | bytes 921608 | tf_op jit(solution)/shard_map/ppermute | solution.py:416
  74.0 11.4 %collective-permute-start.9 = (bf16[2,320,240]{2,1,0:T(8,128)(2,1)}, bf16[2,320,240]{2,1,0:T(8,128)(2,1)}, u32[]{:S(2)}, u32[]{:S(2)}) collective-permute-start(bf16[2,320,240]{2,1,0:T(8,128)(2,1)} %get-tuple-element.44.refs_2_), channel_id=1, source_target_pairs={{0,112},{16,0},{32,16},{48,32},{64,48},{80,64},{96,80},{112,96},{1... | collective-permute-start | bytes 921608 | tf_op jit(solution)/shard_map/ppermute | solution.py:416
  82.0 3.4 %copy-start.12 = (bf16[2,320,240]{2,1,0:T(8,128)(2,1)}, bf16[2,320,240]{2,1,0:T(8,128)(2,1)S(1)}, u32[]{:S(2)}) copy-start(bf16[2,320,240]{2,1,0:T(8,128)(2,1)S(1)} %collective-permute-done.8.rest_2_) | copy-start | bytes 921604
  86.2 8.3 %collective-permute-start.10 = (f32[240,128]{1,0:T(8,128)S(1)}, f32[240,128]{1,0:T(8,128)S(1)}, u32[]{:S(2)}, u32[]{:S(2)}) collective-permute-start(f32[240,128]{1,0:T(8,128)S(1)} %get-tuple-element.53.first), channel_id=1, source_target_pairs={{0,128},{128,0},{1,129},{129,1},{2,130},{130,2},{3,131},{131,3},{4... | collective-permute-start | bytes 368648 | tf_op jit(solution)/shard_map/ppermute | solution.py:412
  87.5 12.2 %collective-permute-start.12 = (bf16[2,320,240]{2,1,0:T(8,128)(2,1)}, bf16[2,320,240]{2,1,0:T(8,128)(2,1)S(1)}, u32[]{:S(2)}, u32[]{:S(2)}) collective-permute-start(bf16[2,320,240]{2,1,0:T(8,128)(2,1)} %get-tuple-element.54.refs_3_), channel_id=1, source_target_pairs={{0,16},{16,32},{32,48},{48,64},{64,80},{80,96},{96,112},{112,0},{1... | collective-permute-start | bytes 921608 | tf_op jit(solution)/shard_map/ppermute | solution.py:416
  94.5 5.2 %collective-permute-start.11 = (f32[240,128]{1,0:T(8,128)S(1)}, f32[240,128]{1,0:T(8,128)S(1)}, u32[]{:S(2)}, u32[]{:S(2)}) collective-permute-start(f32[240,128]{1,0:T(8,128)S(1)} %shard_map.95.first), channel_id=1, source_target_pairs={{0,16},{16,0},{32,48},{48,32},{64,80},{80,64},{96,112},{112,96},{1... | collective-permute-start | bytes 368648 | tf_op jit(solution)/shard_map/ppermute | solution.py:412
  95.8 22.5 %collective-permute-start.15 = (bf16[2,320,240]{2,1,0:T(8,128)(2,1)}, bf16[2,320,240]{2,1,0:T(8,128)(2,1)}, u32[]{:S(2)}, u32[]{:S(2)}) collective-permute-start(bf16[2,320,240]{2,1,0:T(8,128)(2,1)} %get-tuple-element.56.refs_4_), channel_id=1, source_target_pairs={{0,112},{16,0},{32,16},{48,32},{64,48},{80,64},{96,80},{112,96},{1... | collective-permute-start | bytes 921608 | tf_op jit(solution)/shard_map/ppermute | solution.py:416
  99.7 8.1 %copy-start.7 = (bf16[128,2560]{1,0:T(8,128)(2,1)S(1)}, bf16[128,2560]{1,0:T(8,128)(2,1)}, u32[]{:S(2)}) copy-start(bf16[128,2560]{1,0:T(8,128)(2,1)} %copy-done.6) | copy-start | bytes 1966084
  100.5 17.8 %collective-permute-start.16 = (bf16[2,320,240]{2,1,0:T(8,128)(2,1)}, bf16[2,320,240]{2,1,0:T(8,128)(2,1)}, u32[]{:S(2)}, u32[]{:S(2)}) collective-permute-start(bf16[2,320,240]{2,1,0:T(8,128)(2,1)} %get-tuple-element.57.refs_5_), channel_id=1, source_target_pairs={{0,16},{16,32},{32,48},{48,64},{64,80},{80,96},{96,112},{112,0},{1... | collective-permute-start | bytes 921608 | tf_op jit(solution)/shard_map/ppermute | solution.py:416
  103.1 12.4 %collective-permute-start.13 = (f32[240,128]{1,0:T(8,128)S(1)}, f32[240,128]{1,0:T(8,128)S(1)}, u32[]{:S(2)}, u32[]{:S(2)}) collective-permute-start(f32[240,128]{1,0:T(8,128)S(1)} %get-tuple-element.55.first), channel_id=1, source_target_pairs={{0,32},{16,48},{32,0},{48,16},{64,96},{80,112},{96,64},{112,80},{1... | collective-permute-start | bytes 368648 | tf_op jit(solution)/shard_map/ppermute | solution.py:412
  107.8 10.3 %copy-start.16 = (f32[128,128]{1,0:T(8,128)}, f32[128,128]{1,0:T(8,128)S(1)}, u32[]{:S(2)}) copy-start(f32[128,128]{1,0:T(8,128)S(1)} %get-tuple-element.52.inverse) | copy-start | bytes 196612
  107.8 10.6 %copy-start.3 = (bf16[2,320,240]{2,1,0:T(8,128)(2,1)S(1)}, bf16[2,320,240]{2,1,0:T(8,128)(2,1)}, u32[]{:S(2)}) copy-start(bf16[2,320,240]{2,1,0:T(8,128)(2,1)} %get-tuple-element.44.refs_2_) | copy-start | bytes 921604
  115.5 11.6 %collective-permute-start.14 = (f32[240,128]{1,0:T(8,128)S(1)}, f32[240,128]{1,0:T(8,128)S(1)}, u32[]{:S(2)}, u32[]{:S(2)}) collective-permute-start(f32[240,128]{1,0:T(8,128)S(1)} %shard_map.98._.product), channel_id=1, source_target_pairs={{0,64},{16,80},{32,96},{48,112},{64,0},{80,16},{96,32},{112,48},{1... | collective-permute-start | bytes 368648 | tf_op jit(solution)/shard_map/ppermute | solution.py:412
  118.2 9.0 %copy-start.17 = (f32[128,128]{1,0:T(8,128)S(1)}, f32[128,128]{1,0:T(8,128)}, u32[]{:S(2)}) copy-start(f32[128,128]{1,0:T(8,128)} %copy-done.16) | copy-start | bytes 196612
  118.3 8.8 %copy-start.1 = (bf16[240,2560]{1,0:T(8,128)(2,1)S(1)}, bf16[240,2560]{1,0:T(8,128)(2,1)}, u32[]{:S(2)}) copy-start(bf16[240,2560]{1,0:T(8,128)(2,1)} %copy-done) | copy-start | bytes 3686404
  118.4 1.1 copy-start.5
  119.4 1.0 copy-start.11
  120.4 1.0 copy-start.13
  122.3 4.8 %copy-start.8 = (f32[240,320]{0,1:T(8,128)S(1)}, f32[240,320]{0,1:T(8,128)}, u32[]{:S(2)}) copy-start(f32[240,320]{0,1:T(8,128)} %param.8) | copy-start | bytes 921604
  122.3 4.8 %copy-start.9 = (f32[240,320]{0,1:T(8,128)S(1)}, f32[240,320]{0,1:T(8,128)}, u32[]{:S(2)}) copy-start(f32[240,320]{0,1:T(8,128)} %param.9) | copy-start | bytes 921604
  (4 other events, 3.3 us)

commit v3 on v2

--- a/solution.py
+++ b/solution.py
@@ -16,6 +16,7 @@
 fsdp = ("y", "xl", "core")
 plane = ("xh", "y", "xl")
 panel = 32
+group = 8
 whole = pl.BlockSpec(memory_space=pltpu.VMEM)
 anywhere = pl.BlockSpec(memory_space=pl.ANY)
 scalars = pl.BlockSpec(memory_space=pltpu.SMEM)
@@ -41,6 +42,10 @@
 
 def shaped(shape, dtype):
     return jax.ShapeDtypeStruct(shape, dtype)
+
+
+def far(shape, dtype):
+    return pltpu.HBM(shape, dtype)
 
 
 def near(shape, dtype):
@@ -152,7 +157,7 @@
     total = to_f32(chunks[0])
     for place in range(1, chunks.shape[0]):
         total = total + to_f32(chunks[place])
-    out[...] = total
+    out[...] = to_bf(total)
 
 
 def sum_chunks(chunks, after):
@@ -160,7 +165,7 @@
         sum_kernel,
         in_specs=[whole] + [anywhere] * len(after),
         out_specs=whole,
-        out_shape=near(chunks.shape[1:], jnp.float32),
+        out_shape=near(chunks.shape[1:], jnp.bfloat16),
         compiler_params=params(),
         cost_estimate=cost(chunks.size, 2 * chunks.size),
     )(chunks, *[to_far(array) for array in after])
@@ -168,7 +173,7 @@
 
 def spread_kernel(count, block, arrived, *rest):
     out = rest[-1]
-    total = to_bf(block[...] + arrived[...])
+    total = to_bf(to_f32(block[...]) + to_f32(arrived[...]))
     for place in range(count):
         out[place] = total
 
@@ -178,8 +183,8 @@
         functools.partial(spread_kernel, count),
         in_specs=[whole, whole] + [anywhere] * len(held),
         out_specs=[anywhere] * len(held) + [whole],
-        out_shape=[shaped(array.shape, array.dtype) for array in held]
-        + [near((count,) + block.shape, jnp.bfloat16)],
+        out_shape=[far(array.shape, array.dtype) for array in held]
+        + [far((count,) + block.shape, jnp.bfloat16)],
         input_output_aliases={2 + place: place for place in range(len(held))},
         compiler_params=params(),
         cost_estimate=cost(block.size, 2 * count * block.size),
@@ -191,13 +196,11 @@
     values = left[...]
     product = times(merged[...], values, 1, 1)
     gram_mat = times(values, values, 1, 1)
-    if first:
-        product_out, gram_out = rest
-    else:
-        product_out, gram_out = rest[-2:]
+    product_out, gram_out = rest[-2:]
+    if not first:
         product = rest[0][...] + product
         gram_mat = rest[1][...] + gram_mat
-    product_out[...] = product
+    product_out[...] = product.astype(product_out.dtype)
     gram_out[...] = gram_mat
 
 
@@ -208,67 +211,62 @@
         functools.partial(product_kernel, not before),
         in_specs=[whole] * (2 + len(before)) + [anywhere] * len(held),
         out_specs=[anywhere] * len(held) + [whole] * 2,
-        out_shape=[shaped(array.shape, array.dtype) for array in held]
-        + [near((rows, rank), jnp.float32), near((rank, rank), jnp.float32)],
+        out_shape=[far(array.shape, array.dtype) for array in held]
+        + [near((rows, rank), jnp.bfloat16 if before else jnp.float32), near((rank, rank), jnp.float32)],
         input_output_aliases={2 + len(before) + place: place for place in range(len(held))},
         compiler_params=params(),
         cost_estimate=cost(2 * rows * left.size, 4 * left.size),
-    )(to_near(merged), left, *[to_near(array) for array in before], *[to_far(array) for array in held])
+    )(to_near(merged), to_near(left), *[to_near(array) for array in before], *[to_far(array) for array in held])
     return outs[-2:], outs[:-2]
 
 
-def factor_kernel(start, state, *refs):
-    rank = state.shape[0]
-    stop = start + panel
+def factor_kernel(gram_mat, inverse_out, state, below_all):
+    rank = gram_mat.shape[0]
     exact = lax.Precision.HIGHEST
-    state_out, inverse_out = refs[-2:]
-    if start == 0:
-        full_row = lax.broadcasted_iota(jnp.int32, (rank, rank), 0)
-        full_col = lax.broadcasted_iota(jnp.int32, (rank, rank), 1)
-        inverse = jnp.where(full_row == full_col, 1.0, 0.0)
-    else:
-        inverse = refs[0]
-    rows = state[start:stop, :]
-    below = inverse[start:stop, :]
-    small = rows[:, start:stop]
-    row_of = lax.broadcasted_iota(jnp.int32, (panel, panel), 0)
-    col_of = lax.broadcasted_iota(jnp.int32, (panel, panel), 1)
-    turned = jnp.where(row_of == col_of, 1.0, 0.0)
-    for k in range(panel):
-        column = small[:, k : k + 1]
-        pivot = small[k : k + 1, k : k + 1]
-        factor = jnp.where(row_of[:, :1] > k, column / pivot, 0.0)
-        small = small - factor * small[k : k + 1, :]
-        turned = turned - factor * turned[k : k + 1, :]
-    diagonal = jnp.sum(jnp.where(row_of == col_of, small, 0.0), axis=1, keepdims=True)
-    turned = turned * lax.rsqrt(diagonal)
-    rows = times(turned, rows, precision=exact)
-    below = times(turned, below, precision=exact)
-    if start > 0:
-        inverse_out[0:start, :] = inverse[0:start, :]
-    inverse_out[start:stop, :] = below
-    if stop < rank:
-        later = rows.T[stop:, :]
-        state_out[0:stop, :] = state[0:stop, :]
-        state_out[stop:, :] = state[stop:, :] - times(later, rows, precision=exact)
-        inverse_out[stop:, :] = inverse[stop:, :] - times(later, below, precision=exact)
-    else:
-        state_out[...] = state[...]
-
-
-def factor_step(start, state, *inverse):
-    rank = state.shape[0]
-    return pl.pallas_call(
-        functools.partial(factor_kernel, start),
-        in_specs=[whole] * (1 + len(inverse)),
-        out_specs=[whole, whole],
-        out_shape=[near((rank, rank), jnp.float32)] * 2,
+    row_of = lax.broadcasted_iota(jnp.int32, (rank, rank), 0)
+    col_of = lax.broadcasted_iota(jnp.int32, (rank, rank), 1)
+    state[...] = gram_mat[...]
+    below_all[...] = jnp.where(row_of == col_of, 1.0, 0.0)
+    row_of, col_of = row_of[:panel], col_of[:panel]
+    for start in range(0, rank, panel):
+        stop = start + panel
+        rows, below = state[start:stop, :], below_all[start:stop, :]
+        for first in range(0, panel, group):
+            columns = [
+                jnp.broadcast_to(rows[:, start + k : start + k + 1], (panel, rank))
+                for k in range(first, first + group)
+            ]
+            for place in range(group):
+                k = first + place
+                factor = jnp.where(row_of > k, columns[place], 0.0) * (1.0 / columns[place][k : k + 1, :])
+                for later in range(place + 1, group):
+                    columns[later] = columns[later] - factor * columns[later][k : k + 1, :]
+                rows = rows - factor * rows[k : k + 1, :]
+                below = below - factor * below[k : k + 1, :]
+        diagonal = jnp.sum(jnp.where(col_of == row_of + start, rows, 0.0), axis=1, keepdims=True)
+        scale = lax.rsqrt(diagonal)
+        rows, below = rows * scale, below * scale
+        inverse_out[start:stop, :] = below
+        if stop < rank:
+            later = rows.T[stop:, :]
+            state[stop:, :] -= times(later, rows, precision=exact)
+            below_all[stop:, :] -= times(later, below, precision=exact)
+
+
+def inverse_factor(gram_mat):
+    rank = gram_mat.shape[0]
+    return pl.pallas_call(
+        factor_kernel,
+        in_specs=[whole],
+        out_specs=whole,
+        out_shape=near((rank, rank), jnp.float32),
+        scratch_shapes=[pltpu.VMEM((rank, rank), jnp.float32)] * 2,
         compiler_params=params(),
         cost_estimate=cost(10**9, 4 * rank * rank * 4),
-    )(*[to_near(array) for array in (state, *inverse)])
-
-
-def basis_kernel(which, inverse, mine, other, out):
+    )(to_near(gram_mat))
+
+
+def basis_kernel(which, side, depth, inverse, mine, other, _, out, block_out, held):
     half = mine.shape[1]
     value = inverse[...]
     high = to_bf(value)
@@ -281,25 +279,30 @@
 
     put(mine, which[0] * half)
     put(other, (1 - which[0]) * half)
-
-
-def basis_of(which, inverse, mine, other):
+    size = block_out.shape[0]
+    pair = side[0] * half + (depth[0] // 2) * (2 * size)
+    held[...] = to_f32(out[:, pl.ds(pl.multiple_of(pair, 2 * size), 2 * size)]).T
+    block_out[...] = to_bf(held[pl.ds(pl.multiple_of(lax.rem(depth[0], 2) * size, size), size), :])
+
+
+def basis_of(which, side, depth, inverse, mine, other, size, after):
     rank, half = mine.shape
     return pl.pallas_call(
         basis_kernel,
-        in_specs=[pl.BlockSpec(memory_space=pltpu.SMEM), whole, whole, whole],
-        out_specs=whole,
-        out_shape=near((rank, 2 * half), jnp.bfloat16),
+        in_specs=[scalars] * 3 + [whole] * 3 + [anywhere],
+        out_specs=[whole] * 2,
+        out_shape=[near((rank, 2 * half), jnp.bfloat16), near((size, rank), jnp.bfloat16)],
+        scratch_shapes=[pltpu.VMEM((2 * size, rank), jnp.float32)],
         compiler_params=params(),
         cost_estimate=cost(8 * rank * rank * half, 8 * rank * half),
-    )(which, to_near(inverse), mine, other)
+    )(which, side, depth, to_near(inverse), to_near(mine), to_near(other), after)
 
 
 def final_kernel(
     islands, pieces, which, inverse, product, arrived, basis, merged_mine, merged_other, carried, block, master,
     momentum, error_out, weights_out, master_out, momentum_out, errors, weights, masters, momenta, sems,
 ):
-    total = product[...] + arrived[...]
+    total = to_f32(product[...]) + to_f32(arrived[...])
     q_avg = to_bf(times(total, inverse[...], 1, 1, lax.Precision.HIGHEST) / islands)
     half = merged_mine.shape[1]
     width = half // pieces
@@ -345,18 +348,18 @@
         compiler_params=params(24),
         cost_estimate=cost(2 * rows * cols * rank, 8 * rows * cols),
     )(
-        which, to_near(inverse), to_near(product), arrived, to_near(basis), to_near(mine), to_near(other),
-        to_near(carried), block, master, momentum,
+        which, to_near(inverse), to_near(product), to_near(arrived), to_near(basis), to_near(mine), to_near(other),
+        to_near(carried), to_near(block), master, momentum,
     )
 
 
-def gather_kernel(shifts, place, _, *refs):
+def gather_kernel(shifts, side_of, depth, _, *refs):
     pieces, out, held, sems = refs[:-3], refs[-3], refs[-2], refs[-1]
     size = pieces[0].shape[1]
     count = len(shifts)
     waits = []
     for number in range(count):
-        z_of = lax.rem(place[1] + (shifts[number] + count), count)
+        z_of = lax.rem(depth[0] + (shifts[number] + count), count)
         rows = pl.ds(pl.multiple_of(z_of * size, size), size)
         for side in range(2):
             waits.append(fetch(pieces[number].at[side], held.at[side, rows], sems.at[len(waits)]))
@@ -364,18 +367,18 @@
         copy.wait()
     span = count * size
     for side in range(2):
-        start = lax.rem(place[0] + side, 2) * span
+        start = lax.rem(side_of[0] + side, 2) * span
         for first in range(0, span, 2 * size):
             lanes = pl.ds(pl.multiple_of(start + first, 128), 2 * size)
             out[:, lanes] = to_bf(to_f32(held[side, first : first + 2 * size, :]).T)
 
 
-def gather_pieces(place, pieces, shifts, after):
+def gather_pieces(side, depth, pieces, shifts, after):
     rows, cols = pieces[0].shape[1:]
     count = 2 * len(pieces)
     return pl.pallas_call(
         functools.partial(gather_kernel, shifts),
-        in_specs=[scalars] + [anywhere] * (1 + len(pieces)),
+        in_specs=[scalars] * 2 + [anywhere] * (1 + len(pieces)),
         out_specs=whole,
         out_shape=near((cols, count * rows), jnp.bfloat16),
         scratch_shapes=[
@@ -384,23 +387,39 @@
         ],
         compiler_params=params(),
         cost_estimate=cost(10**9, 4 * count * rows * cols),
-    )(place, after, *pieces)
+    )(side, depth, after, *[to_far(piece) for piece in pieces])
+
+
+def pass_kernel(*refs):
+    pass
+
+
+def pass_after(values, after):
+    return pl.pallas_call(
+        pass_kernel,
+        in_specs=[anywhere] * (1 + len(after)),
+        out_specs=anywhere,
+        out_shape=shaped(values.shape, values.dtype),
+        input_output_aliases={0: 0},
+        compiler_params=params(),
+        cost_estimate=cost(1, 1),
+    )(values, *[to_far(array) for array in after])
 
 
 def add_kernel(first, second, *rest):
-    rest[-1][...] = first[...] + second[...]
+    rest[-1][...] = to_bf(to_f32(first[...]) + to_f32(second[...]))
 
 
 def add_after(first, second, after, held=()):
     outs = pl.pallas_call(
         add_kernel,
-        in_specs=[whole, whole, anywhere] + [anywhere] * len(held),
+        in_specs=[whole, whole] + [anywhere] * (len(after) + len(held)),
         out_specs=[anywhere] * len(held) + [whole],
-        out_shape=[shaped(array.shape, array.dtype) for array in held] + [near(first.shape, first.dtype)],
-        input_output_aliases={3 + place: place for place in range(len(held))},
+        out_shape=[far(array.shape, array.dtype) for array in held] + [near(first.shape, first.dtype)],
+        input_output_aliases={2 + len(after) + place: place for place in range(len(held))},
         compiler_params=params(),
         cost_estimate=cost(first.size, 12 * first.size),
-    )(to_near(first), second, after, *[to_far(array) for array in held])
+    )(to_near(first), second, *after, *[to_far(array) for array in held])
     return outs[-1], outs[:-1]
 
 
@@ -422,7 +441,8 @@
     grad, error = pseudo_grad[0], error_buffer[0]
     half = grad.shape[1] // 2
     which_mine, which_other = core.reshape(1), (1 - core).reshape(1)
-    place = jnp.stack([lax.axis_index("xh"), lax.axis_index("z")]).astype(jnp.int32)
+    side = lax.axis_index("xh").astype(jnp.int32).reshape(1)
+    depth = lax.axis_index("z").astype(jnp.int32).reshape(1)
     master, momentum = master_weights.T, outer_momentum.T
 
     given, merged_other, own = project(which_other, grad, error, basis_prev, jnp.bfloat16, master, momentum)
@@ -431,38 +451,32 @@
     kept, merged_mine = project(which_mine, grad, error, basis_prev, jnp.float32)
     mine, bundle = combine(kept, received, own, across)
     up, down = shift(bundle, 1), shift(bundle, -1)
+    up_two, down_two = shift(up, 1), shift(down, -1)
     chunks = lax.all_to_all(mine.reshape(16, rank // 16, half), plane, 0, 0, tiled=True)
     block = sum_chunks(chunks, (up, down))
-    for bit in (1, 2):
-        block = block + swap(block, "z", 8, bit)
-    copies, (up, down) = spread(block, swap(block, "z", 8, 4), 16, (up, down))
     pieces = [bundle, up, down]
-    up, down = shift(up, 1), shift(down, -1)
-    mine = lax.all_to_all(copies, plane, 0, 0, tiled=True).reshape(rank, half)
-    other = swap(mine, "core", 2, 1)
-
-    before, _ = product_of(merged_mine, mine)
-    (product, gram_mat), (up, down) = product_of(merged_other, other, before, (up, down))
+    block, _ = add_after(block, swap(block, "z", 8, 1), ())
+    block, _ = add_after(block, swap(block, "z", 8, 2), (up_two, down_two))
+    copies, (up, down) = spread(block, swap(block, "z", 8, 4), 16, (up_two, down_two))
     pieces += [up, down]
     up, down = shift(up, 1), shift(down, -1)
-
-    state, inverse = factor_step(0, gram_mat)
-    state, inverse = factor_step(panel, state, inverse)
-    product, _ = add_after(product, swap(product, "xh", 2, 1), state)
-    state, inverse = factor_step(2 * panel, state, inverse)
-    product, (up,) = add_after(product, swap(product, "z", 8, 1), state, (up,))
-    pieces += [up, down]
-    up = shift(up, 1)
-    _, inverse = factor_step(3 * panel, state, inverse)
-    basis_bf = basis_of(which_mine, inverse, mine, other)
-    product, _ = add_after(product, swap(product, "z", 8, 2), basis_bf)
-    pieces.append(up)
+    far_side = shift(up, 1)
+    pieces += [up, down, far_side]
+    mine = lax.all_to_all(copies, plane, 0, 0, tiled=True)
+    mine = pass_after(mine, (up, down)).reshape(rank, half)
+    other = swap(mine, "core", 2, 1)
+
+    before, _ = product_of(merged_mine, mine)
+    (product, gram_mat), _ = product_of(merged_other, other, before)
+
+    inverse = inverse_factor(gram_mat)
+    product, _ = add_after(product, swap(product, "xh", 2, 1), (inverse, far_side))
+    product, _ = add_after(product, swap(product, "z", 8, 1), ())
+    basis_bf, basis_block = basis_of(which_mine, side, depth, inverse, mine, other, master.shape[0], product)
+    product, _ = add_after(product, swap(product, "z", 8, 2), (basis_bf,))
+    carried = gather_pieces(side, depth, pieces, (0, -1, 1, -2, 2, -3, 3, -4), product)
     arrived = swap(product, "z", 8, 4)
-    carried = gather_pieces(place, pieces, (0, -1, 1, -2, 2, -3, 3, -4), product)
-
-    col_count = master.shape[0]
-    col_start = lax.axis_index(island) * col_count
-    basis_block = lax.dynamic_slice_in_dim(basis_bf, col_start, col_count, 1).T
+
     error_next, weights_next, master_next, momentum_next = final(
         16, which_mine, inverse, product, arrived, basis_bf, merged_mine, merged_other, carried, basis_block,
         master, momentum,

time: 131 us -> 109 us (0.83)
  the two profiles are of different devices: /device:TPU:96 before, /device:TPU:8 now
where the time goes in v3:
time: 109 us
  waiting for transfers between devices  45.4 us (42%)
  starting transfers between devices  39.6 us (36%)
  Pallas kernels  21.7 us (20%)
  local copies, waits for them, and re-layouts  1.13 us (1%)
    ppermute x10, waiting for transfers between devices, swap(): lax.ppermute(values, axis, [(place, place ^ bit) for place in range(size)])  29.2 us
    ppermute x7, waiting for transfers between devices, shift(): lax.ppermute(values, 'z', [(place, (place + by) % 8) for place in range(8)])  16.2 us
    ppermute x7, starting transfers between devices, shift(): lax.ppermute(values, 'z', [(place, (place + by) % 8) for place in range(8)])  14.3 us
    ppermute x10, starting transfers between devices, swap(): lax.ppermute(values, axis, [(place, place ^ bit) for place in range(size)])  10.7 us
    all_to_all x1, starting transfers between devices, local(): lax.all_to_all(mine.reshape(16, rank // 16, half), plane, 0, 0, tiled=True)  7.39 us
    all_to_all x1, starting transfers between devices, local(): mine = lax.all_to_all(copies, plane, 0, 0, tiled=True)  7.23 us
    pallas_call x2, Pallas kernels, project(): pl.pallas_call(functools.partial(project_kernel, pieces), in_specs=[scala...  4.73 us
    pallas_call x1, Pallas kernels, inverse_factor(): pl.pallas_call(factor_kernel, in_specs=[whole], out_specs=whole, out_shap...  4.15 us
  transfers between devices with their start and end apart: 19, of which 13 were waited for; matrix products, arithmetic and copies ran while one was open for 0% of the time, Pallas kernels for 12%

profile of v3, /device:TPU:8, one launch (start us, length us, event | category | flops | bytes accessed | tf_op | source)
XLA Modules:
  0.0 108.8 jit_solution(3247239326066925136)
XLA Ops:
  0.6 2.4 %shard_map.84 = (bf16[128,2560]{1,0:T(8,128)(2,1)S(1)}, bf16[240,2560]{1,0:T(8,128)(2,1)S(1)}, bf16[320,240]{1,0:T(8,128)(2,1)S(1)}) custom-call(s32[1]{0:T(128)} %bitcast.1.which, bf16[240,5120]{1,0:T(8,128)(2,1)} %bitcast.20, bf16[240,5120]{1,0:T(8,128)(2,1)} %bitcast.22, bf16[240,128]{1,0:T(8,128)(2,1)} %basis.3, f32[320,240]{1,0:T(8,128)} %bitcast.16, ...), custom_call_target="tpu_custom_call" | custom-call | flops 157286400 | bytes 2457600 | tf_op jit(solution)/shard_map/pallas_call | solution.py:127
  3.1 3.1 %collective-permute-start.1 = (bf16[320,240]{1,0:T(8,128)(2,1)S(1)}, bf16[320,240]{1,0:T(8,128)(2,1)S(1)}, u32[]{:S(2)}, u32[]{:S(2)}) collective-permute-start(bf16[320,240]{1,0:T(8,128)(2,1)S(1)} %get-tuple-element.27.own), channel_id=1, source_target_pairs={{0,128},{128,0},{1,129},{129,1},{2,130},{130,2},{3,131},{131,3},{4... | collective-permute-start | bytes 460808 | tf_op jit(solution)/shard_map/ppermute | solution.py:431
  6.2 2.3 %shard_map.85 = (f32[128,2560]{1,0:T(8,128)S(1)}, bf16[240,2560]{1,0:T(8,128)(2,1)S(1)}) custom-call(s32[1]{0:T(128)} %bitcast.which, bf16[240,5120]{1,0:T(8,128)(2,1)} %bitcast.21, bf16[240,5120]{1,0:T(8,128)(2,1)} %bitcast.23, bf16[240,128]{1,0:T(8,128)(2,1)} %basis.3), custom_call_target="tpu_custom_call" | custom-call | flops 157286400 | bytes 2457600 | tf_op jit(solution)/shard_map/pallas_call | solution.py:127
  8.6 2.7 %collective-permute-done.1.across = bf16[320,240]{1,0:T(8,128)(2,1)S(1)} collective-permute-done((bf16[320,240]{1,0:T(8,128)(2,1)S(1)}, bf16[320,240]{1,0:T(8,128)(2,1)S(1)}, u32[]{:S(2)}, u32[]{:S(2)}) %collective-permute-start.1) | collective-permute-done | bytes 153632 | tf_op jit(solution)/shard_map/ppermute | solution.py:431
  11.3 1.0 shard_map.86
  12.2 7.4 %all-to-all-start = ((bf16[16,8,2560]{2,1,0:T(8,128)(2,1)}), bf16[16,8,2560]{2,1,0:T(8,128)(2,1)}, u32[]{:S(2)}, u32[]{:S(2)}) async-start(bf16[16,8,2560]{2,1,0:T(8,128)(2,1)} %bitcast.6), calls=%async_computation | async-start | bytes 1310720 | tf_op jit(solution)/shard_map/all_to_all | solution.py:455
  19.6 5.9 %collective-permute-start.3 = (bf16[2,320,240]{2,1,0:T(8,128)(2,1)S(1)}, bf16[2,320,240]{2,1,0:T(8,128)(2,1)}, u32[]{:S(2)}, u32[]{:S(2)}) collective-permute-start(bf16[2,320,240]{2,1,0:T(8,128)(2,1)S(1)} %get-tuple-element.29.refs_0_), channel_id=1, source_target_pairs={{0,112},{16,0},{32,16},{48,32},{64,48},{80,64},{96,80},{112,96},{1... | collective-permute-start | bytes 921608 | tf_op jit(solution)/shard_map/ppermute | solution.py:435
  25.5 6.2 %collective-permute-done.3.rest_1_.refs_2_ = bf16[2,320,240]{2,1,0:T(8,128)(2,1)} collective-permute-done((bf16[2,320,240]{2,1,0:T(8,128)(2,1)S(1)}, bf16[2,320,240]{2,1,0:T(8,128)(2,1)}, u32[]{:S(2)}, u32[]{:S(2)}) %collective-permute-start.3) | collective-permute-done | bytes 307232 | tf_op jit(solution)/shard_map/ppermute | solution.py:435
  31.7 3.8 %collective-permute-start.7 = (bf16[2,320,240]{2,1,0:T(8,128)(2,1)}, bf16[2,320,240]{2,1,0:T(8,128)(2,1)S(1)}, u32[]{:S(2)}, u32[]{:S(2)}) collective-permute-start(bf16[2,320,240]{2,1,0:T(8,128)(2,1)} %collective-permute-done.3.rest_1_.refs_2_), channel_id=1, source_target_pairs={{0,112},{16,0},{32,16},{48,32},{64,48},{80,64},{96,80},{112,96},{1... | collective-permute-start | bytes 921608 | tf_op jit(solution)/shard_map/ppermute | solution.py:435
  35.5 1.2 %shard_map.87.first = bf16[8,2560]{1,0:T(8,128)(2,1)S(1)} custom-call(bf16[16,8,2560]{2,1,0:T(8,128)(2,1)} %all-to-all-done.chunks, bf16[2,320,240]{2,1,0:T(8,128)(2,1)} %collective-permute-done.2.rest_0_.refs_1_, bf16[2,320,240]{2,1,0:T(8,128)(2,1)} %collective-permute-done.3.rest_1_.refs_2_), custom_call_target="tpu_custom_call" | custom-call | flops 327680 | bytes 655360 | tf_op jit(solution)/shard_map/pallas_call | solution.py:164
  36.8 5.5 %collective-permute-done.4.second = bf16[8,2560]{1,0:T(8,128)(2,1)S(1)} collective-permute-done((bf16[8,2560]{1,0:T(8,128)(2,1)S(1)}, bf16[8,2560]{1,0:T(8,128)(2,1)S(1)}, u32[]{:S(2)}, u32[]{:S(2)}) %collective-permute-start.4) | collective-permute-done | bytes 40992 | tf_op jit(solution)/shard_map/ppermute | solution.py:431
  42.5 2.0 %collective-permute-done.6.rest_0_ = bf16[2,320,240]{2,1,0:T(8,128)(2,1)S(1)} collective-permute-done((bf16[2,320,240]{2,1,0:T(8,128)(2,1)}, bf16[2,320,240]{2,1,0:T(8,128)(2,1)S(1)}, u32[]{:S(2)}, u32[]{:S(2)}) %collective-permute-start.6) | collective-permute-done | bytes 307232 | tf_op jit(solution)/shard_map/ppermute | solution.py:435
  44.4 2.9 %collective-permute-done.5.second = bf16[8,2560]{1,0:T(8,128)(2,1)S(1)} collective-permute-done((bf16[8,2560]{1,0:T(8,128)(2,1)S(1)}, bf16[8,2560]{1,0:T(8,128)(2,1)S(1)}, u32[]{:S(2)}, u32[]{:S(2)}) %collective-permute-start.5) | collective-permute-done | bytes 40992 | tf_op jit(solution)/shard_map/ppermute | solution.py:431
  47.4 2.2 %collective-permute-start.8 = (bf16[8,2560]{1,0:T(8,128)(2,1)S(1)}, bf16[8,2560]{1,0:T(8,128)(2,1)S(1)}, u32[]{:S(2)}, u32[]{:S(2)}) collective-permute-start(bf16[8,2560]{1,0:T(8,128)(2,1)S(1)} %shard_map.89.block), channel_id=1, source_target_pairs={{0,64},{16,80},{32,96},{48,112},{64,0},{80,16},{96,32},{112,48},{1... | collective-permute-start | bytes 122888 | tf_op jit(solution)/shard_map/ppermute | solution.py:431
  49.6 5.8 %collective-permute-done.8.arrived = bf16[8,2560]{1,0:T(8,128)(2,1)S(1)} collective-permute-done((bf16[8,2560]{1,0:T(8,128)(2,1)S(1)}, bf16[8,2560]{1,0:T(8,128)(2,1)S(1)}, u32[]{:S(2)}, u32[]{:S(2)}) %collective-permute-start.8) | collective-permute-done | bytes 40992 | tf_op jit(solution)/shard_map/ppermute | solution.py:431
  55.4 0.9 shard_map.90
  56.2 7.2 %all-to-all-start.1 = ((bf16[16,8,2560]{2,1,0:T(8,128)(2,1)}), bf16[16,8,2560]{2,1,0:T(8,128)(2,1)S(1)}, u32[]{:S(2)}, u32[]{:S(2)}) async-start(bf16[16,8,2560]{2,1,0:T(8,128)(2,1)} %get-tuple-element.30), calls=%async_computation.1 | async-start | bytes 1310720 | tf_op jit(solution)/shard_map/all_to_all | solution.py:465
  63.5 2.5 %collective-permute-start.9 = (bf16[2,320,240]{2,1,0:T(8,128)(2,1)}, bf16[2,320,240]{2,1,0:T(8,128)(2,1)S(1)}, u32[]{:S(2)}, u32[]{:S(2)}) collective-permute-start(bf16[2,320,240]{2,1,0:T(8,128)(2,1)} %get-tuple-element.31.refs_3_), channel_id=1, source_target_pairs={{0,16},{16,32},{32,48},{48,64},{64,80},{80,96},{96,112},{112,0},{1... | collective-permute-start | bytes 921608 | tf_op jit(solution)/shard_map/ppermute | solution.py:435
  66.7 5.3 %collective-permute-done.9.refs_1_.refs_5_ = bf16[2,320,240]{2,1,0:T(8,128)(2,1)S(1)} collective-permute-done((bf16[2,320,240]{2,1,0:T(8,128)(2,1)}, bf16[2,320,240]{2,1,0:T(8,128)(2,1)S(1)}, u32[]{:S(2)}, u32[]{:S(2)}) %collective-permute-start.9) | collective-permute-done | bytes 307232 | tf_op jit(solution)/shard_map/ppermute | solution.py:435
  72.0 1.4 %collective-permute-done.10.refs_2_.refs_6_ = bf16[2,320,240]{2,1,0:T(8,128)(2,1)} collective-permute-done((bf16[2,320,240]{2,1,0:T(8,128)(2,1)}, bf16[2,320,240]{2,1,0:T(8,128)(2,1)}, u32[]{:S(2)}, u32[]{:S(2)}) %collective-permute-start.10) | collective-permute-done | bytes 307232 | tf_op jit(solution)/shard_map/ppermute | solution.py:435
  73.4 1.4 %collective-permute-start.13 = (bf16[2,320,240]{2,1,0:T(8,128)(2,1)}, bf16[2,320,240]{2,1,0:T(8,128)(2,1)S(1)}, u32[]{:S(2)}, u32[]{:S(2)}) collective-permute-start(bf16[2,320,240]{2,1,0:T(8,128)(2,1)} %copy-done.8), channel_id=1, source_target_pairs={{0,16},{16,32},{32,48},{48,64},{64,80},{80,96},{96,112},{112,0},{1... | collective-permute-start | bytes 921608 | tf_op jit(solution)/shard_map/ppermute | solution.py:435
  76.1 3.2 %collective-permute-start.12 = (bf16[240,128]{1,0:T(8,128)(2,1)S(1)}, bf16[240,128]{1,0:T(8,128)(2,1)S(1)}, u32[]{:S(2)}, u32[]{:S(2)}) collective-permute-start(bf16[240,128]{1,0:T(8,128)(2,1)S(1)} %get-tuple-element.37.first), channel_id=1, source_target_pairs={{0,128},{128,0},{1,129},{129,1},{2,130},{130,2},{3,131},{131,3},{4... | collective-permute-start | bytes 184328 | tf_op jit(solution)/shard_map/ppermute | solution.py:431
  79.4 4.2 %shard_map.94.rest_0_.inverse = f32[128,128]{1,0:T(8,128)S(1)} custom-call(f32[128,128]{1,0:T(8,128)S(1)} %get-tuple-element.36.gram_mat), custom_call_target="tpu_custom_call" | custom-call | flops 1000000000 | bytes 262144 | tf_op jit(solution)/shard_map/pallas_call | solution.py:258
  83.5 1.4 %collective-permute-done.13.rest_1_.refs_7_ = bf16[2,320,240]{2,1,0:T(8,128)(2,1)S(1)} collective-permute-done((bf16[2,320,240]{2,1,0:T(8,128)(2,1)}, bf16[2,320,240]{2,1,0:T(8,128)(2,1)S(1)}, u32[]{:S(2)}, u32[]{:S(2)}) %collective-permute-start.13) | collective-permute-done | bytes 307232 | tf_op jit(solution)/shard_map/ppermute | solution.py:435
  85.2 4.1 %collective-permute-done.14.second = bf16[240,128]{1,0:T(8,128)(2,1)S(1)} collective-permute-done((bf16[240,128]{1,0:T(8,128)(2,1)S(1)}, bf16[240,128]{1,0:T(8,128)(2,1)S(1)}, u32[]{:S(2)}, u32[]{:S(2)}) %collective-permute-start.14) | collective-permute-done | bytes 61472 | tf_op jit(solution)/shard_map/ppermute | solution.py:431
  89.9 1.1 copy-done.3
  91.0 1.0 shard_map.97
  92.0 3.6 %collective-permute-done.15.second = bf16[240,128]{1,0:T(8,128)(2,1)} collective-permute-done((bf16[240,128]{1,0:T(8,128)(2,1)}, bf16[240,128]{1,0:T(8,128)(2,1)}, u32[]{:S(2)}, u32[]{:S(2)}) %collective-permute-start.15) | collective-permute-done | bytes 61472 | tf_op jit(solution)/shard_map/ppermute | solution.py:431
  96.5 1.6 %collective-permute-start.16 = (bf16[240,128]{1,0:T(8,128)(2,1)S(1)}, bf16[240,128]{1,0:T(8,128)(2,1)S(1)}, u32[]{:S(2)}, u32[]{:S(2)}) collective-permute-start(bf16[240,128]{1,0:T(8,128)(2,1)S(1)} %shard_map.98._.product), channel_id=1, source_target_pairs={{0,64},{16,80},{32,96},{48,112},{64,0},{80,16},{96,32},{112,48},{1... | collective-permute-start | bytes 184328 | tf_op jit(solution)/shard_map/ppermute | solution.py:431
  98.1 2.7 %shard_map.99.carried = bf16[240,5120]{1,0:T(8,128)(2,1)S(1)} custom-call(s32[1]{0:T(128)} %bitcast.8.side.side_of, s32[1]{0:T(128)} %bitcast.9.depth, bf16[240,128]{1,0:T(8,128)(2,1)S(1)} %shard_map.98._.product, bf16[2,320,240]{2,1,0:T(8,128)(2,1)} %copy-done.7, bf16[2,320,240]{2,1,0:T(8,128)(2,1)} %collective-permute-done.2.rest_0_.refs_1_, ...), custom_call_target="tpu_custom_call" | custom-call | flops 1000000000 | bytes 4915200 | tf_op jit(solution)/shard_map/pallas_call | solution.py:379
  100.8 4.6 %collective-permute-done.16.arrived = bf16[240,128]{1,0:T(8,128)(2,1)S(1)} collective-permute-done((bf16[240,128]{1,0:T(8,128)(2,1)S(1)}, bf16[240,128]{1,0:T(8,128)(2,1)S(1)}, u32[]{:S(2)}, u32[]{:S(2)}) %collective-permute-start.16) | collective-permute-done | bytes 61472 | tf_op jit(solution)/shard_map/ppermute | solution.py:431
  105.3 3.3 %shard_map.100 = (bf16[240,5120]{1,0:T(8,128)(2,1)}, bf16[240,5120]{1,0:T(8,128)(2,1)}, f32[320,240]{1,0:T(8,128)}, f32[320,240]{1,0:T(8,128)}) custom-call(s32[1]{0:T(128)} %bitcast.which, f32[128,128]{1,0:T(8,128)S(1)} %shard_map.94.rest_0_.inverse, bf16[240,128]{1,0:T(8,128)(2,1)S(1)} %shard_map.98._.product, ...), custom_call_target="tpu_custom_call" | custom-call | flops 314572800 | bytes 9830400 | tf_op jit(solution)/shard_map/pallas_call | solution.py:335
  (41 shorter events, 4.3 us)
Async XLA Ops:
  3.0 8.2 %collective-permute-start = (bf16[128,2560]{1,0:T(8,128)(2,1)S(1)}, bf16[128,2560]{1,0:T(8,128)(2,1)S(1)}, u32[]{:S(2)}, u32[]{:S(2)}) collective-permute-start(bf16[128,2560]{1,0:T(8,128)(2,1)S(1)} %get-tuple-element.26), channel_id=1, source_target_pairs={{0,1},{1,0},{2,3},{3,2},{4,5},{5,4},{6,7},{7,6},{8,9},{9,8},{10,11... | collective-permute-start | bytes 1966088 | tf_op jit(solution)/shard_map/ppermute | solution.py:431
  3.1 8.1 %collective-permute-start.1 = (bf16[320,240]{1,0:T(8,128)(2,1)S(1)}, bf16[320,240]{1,0:T(8,128)(2,1)S(1)}, u32[]{:S(2)}, u32[]{:S(2)}) collective-permute-start(bf16[320,240]{1,0:T(8,128)(2,1)S(1)} %get-tuple-element.27.own), channel_id=1, source_target_pairs={{0,128},{128,0},{1,129},{129,1},{2,130},{130,2},{3,131},{131,3},{4... | collective-permute-start | bytes 460808 | tf_op jit(solution)/shard_map/ppermute | solution.py:431
  12.2 44.0 %copy-start.7 = (bf16[2,320,240]{2,1,0:T(8,128)(2,1)}, bf16[2,320,240]{2,1,0:T(8,128)(2,1)S(1)}, u32[]{:S(2)}) copy-start(bf16[2,320,240]{2,1,0:T(8,128)(2,1)S(1)} %get-tuple-element.29.refs_0_) | copy-start | bytes 921604
  12.2 23.3 %all-to-all-start = ((bf16[16,8,2560]{2,1,0:T(8,128)(2,1)}), bf16[16,8,2560]{2,1,0:T(8,128)(2,1)}, u32[]{:S(2)}, u32[]{:S(2)}) async-start(bf16[16,8,2560]{2,1,0:T(8,128)(2,1)} %bitcast.6), calls=%async_computation | async-start | bytes 1310720 | tf_op jit(solution)/shard_map/all_to_all | solution.py:455
  19.6 12.1 %collective-permute-start.3 = (bf16[2,320,240]{2,1,0:T(8,128)(2,1)S(1)}, bf16[2,320,240]{2,1,0:T(8,128)(2,1)}, u32[]{:S(2)}, u32[]{:S(2)}) collective-permute-start(bf16[2,320,240]{2,1,0:T(8,128)(2,1)S(1)} %get-tuple-element.29.refs_0_), channel_id=1, source_target_pairs={{0,112},{16,0},{32,16},{48,32},{64,48},{80,64},{96,80},{112,96},{1... | collective-permute-start | bytes 921608 | tf_op jit(solution)/shard_map/ppermute | solution.py:435
  25.5 10.0 %collective-permute-start.2 = (bf16[2,320,240]{2,1,0:T(8,128)(2,1)S(1)}, bf16[2,320,240]{2,1,0:T(8,128)(2,1)}, u32[]{:S(2)}, u32[]{:S(2)}) collective-permute-start(bf16[2,320,240]{2,1,0:T(8,128)(2,1)S(1)} %get-tuple-element.29.refs_0_), channel_id=1, source_target_pairs={{0,16},{16,32},{32,48},{48,64},{64,80},{80,96},{96,112},{112,0},{1... | collective-permute-start | bytes 921608 | tf_op jit(solution)/shard_map/ppermute | solution.py:435
  31.7 10.7 %collective-permute-start.7 = (bf16[2,320,240]{2,1,0:T(8,128)(2,1)}, bf16[2,320,240]{2,1,0:T(8,128)(2,1)S(1)}, u32[]{:S(2)}, u32[]{:S(2)}) collective-permute-start(bf16[2,320,240]{2,1,0:T(8,128)(2,1)} %collective-permute-done.3.rest_1_.refs_2_), channel_id=1, source_target_pairs={{0,112},{16,0},{32,16},{48,32},{64,48},{80,64},{96,80},{112,96},{1... | collective-permute-start | bytes 921608 | tf_op jit(solution)/shard_map/ppermute | solution.py:435
  35.5 8.9 %collective-permute-start.6 = (bf16[2,320,240]{2,1,0:T(8,128)(2,1)}, bf16[2,320,240]{2,1,0:T(8,128)(2,1)S(1)}, u32[]{:S(2)}, u32[]{:S(2)}) collective-permute-start(bf16[2,320,240]{2,1,0:T(8,128)(2,1)} %collective-permute-done.2.rest_0_.refs_1_), channel_id=1, source_target_pairs={{0,16},{16,32},{32,48},{48,64},{64,80},{80,96},{96,112},{112,0},{1... | collective-permute-start | bytes 921608 | tf_op jit(solution)/shard_map/ppermute | solution.py:435
  36.7 5.6 %collective-permute-start.4 = (bf16[8,2560]{1,0:T(8,128)(2,1)S(1)}, bf16[8,2560]{1,0:T(8,128)(2,1)S(1)}, u32[]{:S(2)}, u32[]{:S(2)}) collective-permute-start(bf16[8,2560]{1,0:T(8,128)(2,1)S(1)} %shard_map.87.first), channel_id=1, source_target_pairs={{0,16},{16,0},{32,48},{48,32},{64,80},{80,64},{96,112},{112,96},{1... | collective-permute-start | bytes 122888 | tf_op jit(solution)/shard_map/ppermute | solution.py:431
  42.3 5.0 %collective-permute-start.5 = (bf16[8,2560]{1,0:T(8,128)(2,1)S(1)}, bf16[8,2560]{1,0:T(8,128)(2,1)S(1)}, u32[]{:S(2)}, u32[]{:S(2)}) collective-permute-start(bf16[8,2560]{1,0:T(8,128)(2,1)S(1)} %shard_map.88.first), channel_id=1, source_target_pairs={{0,32},{16,48},{32,0},{48,16},{64,96},{80,112},{96,64},{112,80},{1... | collective-permute-start | bytes 122888 | tf_op jit(solution)/shard_map/ppermute | solution.py:431
  42.5 12.9 %copy-start = (bf16[2,320,240]{2,1,0:T(8,128)(2,1)}, bf16[2,320,240]{2,1,0:T(8,128)(2,1)S(1)}, u32[]{:S(2)}) copy-start(bf16[2,320,240]{2,1,0:T(8,128)(2,1)S(1)} %collective-permute-done.7.rest_1_) | copy-start | bytes 921604
  44.4 10.9 %copy-start.1 = (bf16[2,320,240]{2,1,0:T(8,128)(2,1)}, bf16[2,320,240]{2,1,0:T(8,128)(2,1)S(1)}, u32[]{:S(2)}) copy-start(bf16[2,320,240]{2,1,0:T(8,128)(2,1)S(1)} %collective-permute-done.6.rest_0_) | copy-start | bytes 921604
  47.4 8.0 %collective-permute-start.8 = (bf16[8,2560]{1,0:T(8,128)(2,1)S(1)}, bf16[8,2560]{1,0:T(8,128)(2,1)S(1)}, u32[]{:S(2)}, u32[]{:S(2)}) collective-permute-start(bf16[8,2560]{1,0:T(8,128)(2,1)S(1)} %shard_map.89.block), channel_id=1, source_target_pairs={{0,64},{16,80},{32,96},{48,112},{64,0},{80,16},{96,32},{112,48},{1... | collective-permute-start | bytes 122888 | tf_op jit(solution)/shard_map/ppermute | solution.py:431
  56.2 17.1 %all-to-all-start.1 = ((bf16[16,8,2560]{2,1,0:T(8,128)(2,1)}), bf16[16,8,2560]{2,1,0:T(8,128)(2,1)S(1)}, u32[]{:S(2)}, u32[]{:S(2)}) async-start(bf16[16,8,2560]{2,1,0:T(8,128)(2,1)} %get-tuple-element.30), calls=%async_computation.1 | async-start | bytes 1310720 | tf_op jit(solution)/shard_map/all_to_all | solution.py:465
  63.5 8.5 %collective-permute-start.9 = (bf16[2,320,240]{2,1,0:T(8,128)(2,1)}, bf16[2,320,240]{2,1,0:T(8,128)(2,1)S(1)}, u32[]{:S(2)}, u32[]{:S(2)}) collective-permute-start(bf16[2,320,240]{2,1,0:T(8,128)(2,1)} %get-tuple-element.31.refs_3_), channel_id=1, source_target_pairs={{0,16},{16,32},{32,48},{48,64},{64,80},{80,96},{96,112},{112,0},{1... | collective-permute-start | bytes 921608 | tf_op jit(solution)/shard_map/ppermute | solution.py:435
  66.0 7.4 %collective-permute-start.10 = (bf16[2,320,240]{2,1,0:T(8,128)(2,1)}, bf16[2,320,240]{2,1,0:T(8,128)(2,1)}, u32[]{:S(2)}, u32[]{:S(2)}) collective-permute-start(bf16[2,320,240]{2,1,0:T(8,128)(2,1)} %get-tuple-element.32.refs_4_), channel_id=1, source_target_pairs={{0,112},{16,0},{32,16},{48,32},{64,48},{80,64},{96,80},{112,96},{1... | collective-permute-start | bytes 921608 | tf_op jit(solution)/shard_map/ppermute | solution.py:435
  72.0 1.4 %copy-start.8 = (bf16[2,320,240]{2,1,0:T(8,128)(2,1)}, bf16[2,320,240]{2,1,0:T(8,128)(2,1)S(1)}, u32[]{:S(2)}) copy-start(bf16[2,320,240]{2,1,0:T(8,128)(2,1)S(1)} %collective-permute-done.9.refs_1_.refs_5_) | copy-start | bytes 921604
  73.3 2.1 %collective-permute-start.11 = (bf16[128,2560]{1,0:T(8,128)(2,1)S(1)}, bf16[128,2560]{1,0:T(8,128)(2,1)S(1)}, u32[]{:S(2)}, u32[]{:S(2)}) collective-permute-start(bf16[128,2560]{1,0:T(8,128)(2,1)S(1)} %bitcast.13), channel_id=1, source_target_pairs={{0,1},{1,0},{2,3},{3,2},{4,5},{5,4},{6,7},{7,6},{8,9},{9,8},{10,11... | collective-permute-start | bytes 1966088 | tf_op jit(solution)/shard_map/ppermute | solution.py:431
  73.4 11.6 %collective-permute-start.13 = (bf16[2,320,240]{2,1,0:T(8,128)(2,1)}, bf16[2,320,240]{2,1,0:T(8,128)(2,1)S(1)}, u32[]{:S(2)}, u32[]{:S(2)}) collective-permute-start(bf16[2,320,240]{2,1,0:T(8,128)(2,1)} %copy-done.8), channel_id=1, source_target_pairs={{0,16},{16,32},{32,48},{48,64},{64,80},{80,96},{96,112},{112,0},{1... | collective-permute-start | bytes 921608 | tf_op jit(solution)/shard_map/ppermute | solution.py:435
  75.4 8.1 %copy-start.2 = (bf16[128,2560]{1,0:T(8,128)(2,1)}, bf16[128,2560]{1,0:T(8,128)(2,1)S(1)}, u32[]{:S(2)}) copy-start(bf16[128,2560]{1,0:T(8,128)(2,1)S(1)} %collective-permute-done.11.left.other) | copy-start | bytes 1966084
  76.1 8.8 %collective-permute-start.12 = (bf16[240,128]{1,0:T(8,128)(2,1)S(1)}, bf16[240,128]{1,0:T(8,128)(2,1)S(1)}, u32[]{:S(2)}, u32[]{:S(2)}) collective-permute-start(bf16[240,128]{1,0:T(8,128)(2,1)S(1)} %get-tuple-element.37.first), channel_id=1, source_target_pairs={{0,128},{128,0},{1,129},{129,1},{2,130},{130,2},{3,131},{131,3},{4... | collective-permute-start | bytes 184328 | tf_op jit(solution)/shard_map/ppermute | solution.py:431
  84.9 13.2 %copy-start.6 = (bf16[2,320,240]{2,1,0:T(8,128)(2,1)}, bf16[2,320,240]{2,1,0:T(8,128)(2,1)S(1)}, u32[]{:S(2)}) copy-start(bf16[2,320,240]{2,1,0:T(8,128)(2,1)S(1)} %collective-permute-done.13.rest_1_.refs_7_) | copy-start | bytes 921604
  84.9 4.3 %collective-permute-start.14 = (bf16[240,128]{1,0:T(8,128)(2,1)S(1)}, bf16[240,128]{1,0:T(8,128)(2,1)S(1)}, u32[]{:S(2)}, u32[]{:S(2)}) collective-permute-start(bf16[240,128]{1,0:T(8,128)(2,1)S(1)} %shard_map.95.first), channel_id=1, source_target_pairs={{0,16},{16,0},{32,48},{48,32},{64,80},{80,64},{96,112},{112,96},{1... | collective-permute-start | bytes 184328 | tf_op jit(solution)/shard_map/ppermute | solution.py:431
  89.9 5.7 %collective-permute-start.15 = (bf16[240,128]{1,0:T(8,128)(2,1)}, bf16[240,128]{1,0:T(8,128)(2,1)}, u32[]{:S(2)}, u32[]{:S(2)}) collective-permute-start(bf16[240,128]{1,0:T(8,128)(2,1)} %shard_map.96._.first), channel_id=1, source_target_pairs={{0,32},{16,48},{32,0},{48,16},{64,96},{80,112},{96,64},{112,80},{1... | collective-permute-start | bytes 184328 | tf_op jit(solution)/shard_map/ppermute | solution.py:431
  89.9 1.1 copy-start.3
  96.5 8.9 %copy-start.4 = (f32[240,320]{0,1:T(8,128)S(1)}, f32[240,320]{0,1:T(8,128)}, u32[]{:S(2)}) copy-start(f32[240,320]{0,1:T(8,128)} %param.8) | copy-start | bytes 921604
  96.5 8.9 %copy-start.5 = (f32[240,320]{0,1:T(8,128)S(1)}, f32[240,320]{0,1:T(8,128)}, u32[]{:S(2)}) copy-start(f32[240,320]{0,1:T(8,128)} %param.9) | copy-start | bytes 921604
  96.5 8.8 %collective-permute-start.16 = (bf16[240,128]{1,0:T(8,128)(2,1)S(1)}, bf16[240,128]{1,0:T(8,128)(2,1)S(1)}, u32[]{:S(2)}, u32[]{:S(2)}) collective-permute-start(bf16[240,128]{1,0:T(8,128)(2,1)S(1)} %shard_map.98._.product), channel_id=1, source_target_pairs={{0,64},{16,80},{32,96},{48,112},{64,0},{80,16},{96,32},{112,48},{1... | collective-permute-start | bytes 184328 | tf_op jit(solution)/shard_map/ppermute | solution.py:431

commit v4 on v3

--- a/solution.py
+++ b/solution.py
@@ -135,21 +135,35 @@
     )(*operands)
 
 
-def combine_kernel(kept, received, own, across, mine_out, bundle_out):
+def combine_kernel(kept, received, mine_out):
     mine_out[...] = to_bf(kept[...] + to_f32(received[...]))
-    bundle_out[0] = own[...]
-    bundle_out[1] = across[...]
-
-
-def combine(kept, received, own, across):
+
+
+def combine(kept, received):
     return pl.pallas_call(
         combine_kernel,
-        in_specs=[whole] * 4,
-        out_specs=[whole] * 2,
-        out_shape=[near(kept.shape, jnp.bfloat16), near((2,) + own.shape, own.dtype)],
+        in_specs=[whole] * 2,
+        out_specs=whole,
+        out_shape=shaped(kept.shape, jnp.bfloat16),
         compiler_params=params(),
         cost_estimate=cost(kept.size, 8 * kept.size),
-    )(to_near(kept), received, to_near(own), across)
+    )(to_near(kept), to_near(received))
+
+
+def bundle_kernel(own, across, out):
+    out[0] = own[...]
+    out[1] = across[...]
+
+
+def bundle_of(own, across):
+    return pl.pallas_call(
+        bundle_kernel,
+        in_specs=[whole] * 2,
+        out_specs=whole,
+        out_shape=far((2,) + own.shape, own.dtype),
+        compiler_params=params(),
+        cost_estimate=cost(10**11, own.size),
+    )(to_near(own), to_near(across))
 
 
 def sum_kernel(chunks, *rest):
@@ -168,12 +182,16 @@
         out_shape=near(chunks.shape[1:], jnp.bfloat16),
         compiler_params=params(),
         cost_estimate=cost(chunks.size, 2 * chunks.size),
-    )(chunks, *[to_far(array) for array in after])
-
-
-def spread_kernel(count, block, arrived, *rest):
+    )(to_near(chunks), *[to_far(array) for array in after])
+
+
+def sum_pairs(own, opposite, before, after):
+    return (to_f32(own[...]) + to_f32(opposite[...])) + (to_f32(before[...]) + to_f32(after[...]))
+
+
+def spread_kernel(count, block, opposite, before, after, *rest):
     out = rest[-1]
-    total = to_bf(to_f32(block[...]) + to_f32(arrived[...]))
+    total = to_bf(sum_pairs(block, opposite, before, after))
     for place in range(count):
         out[place] = total
 
@@ -181,14 +199,14 @@
 def spread(block, arrived, count, held):
     outs = pl.pallas_call(
         functools.partial(spread_kernel, count),
-        in_specs=[whole, whole] + [anywhere] * len(held),
+        in_specs=[whole] * 4 + [anywhere] * len(held),
         out_specs=[anywhere] * len(held) + [whole],
         out_shape=[far(array.shape, array.dtype) for array in held]
         + [far((count,) + block.shape, jnp.bfloat16)],
-        input_output_aliases={2 + place: place for place in range(len(held))},
+        input_output_aliases={4 + place: place for place in range(len(held))},
         compiler_params=params(),
         cost_estimate=cost(block.size, 2 * count * block.size),
-    )(to_near(block), arrived, *[to_far(array) for array in held])
+    )(*[to_near(array) for array in (block, *arrived)], *[to_far(array) for array in held])
     return outs[-1], outs[:-1]
 
 
@@ -220,7 +238,8 @@
     return outs[-2:], outs[:-2]
 
 
-def factor_kernel(gram_mat, inverse_out, state, below_all):
+def factor_kernel(gram_mat, *refs):
+    inverse_out, state, below_all = refs[-3:]
     rank = gram_mat.shape[0]
     exact = lax.Precision.HIGHEST
     row_of = lax.broadcasted_iota(jnp.int32, (rank, rank), 0)
@@ -253,17 +272,17 @@
             below_all[stop:, :] -= times(later, below, precision=exact)
 
 
-def inverse_factor(gram_mat):
+def inverse_factor(gram_mat, kept):
     rank = gram_mat.shape[0]
     return pl.pallas_call(
         factor_kernel,
-        in_specs=[whole],
+        in_specs=[whole] + [anywhere] * len(kept),
         out_specs=whole,
         out_shape=near((rank, rank), jnp.float32),
         scratch_shapes=[pltpu.VMEM((rank, rank), jnp.float32)] * 2,
         compiler_params=params(),
         cost_estimate=cost(10**9, 4 * rank * rank * 4),
-    )(to_near(gram_mat))
+    )(to_near(gram_mat), *[to_near(array) for array in kept])
 
 
 def basis_kernel(which, side, depth, inverse, mine, other, _, out, block_out, held):
@@ -299,10 +318,10 @@
 
 
 def final_kernel(
-    islands, pieces, which, inverse, product, arrived, basis, merged_mine, merged_other, carried, block, master,
+    islands, pieces, which, inverse, product, opposite, before, after, basis, merged_mine, merged_other, carried, block, master,
     momentum, error_out, weights_out, master_out, momentum_out, errors, weights, masters, momenta, sems,
 ):
-    total = to_f32(product[...]) + to_f32(arrived[...])
+    total = sum_pairs(product, opposite, before, after)
     q_avg = to_bf(times(total, inverse[...], 1, 1, lax.Precision.HIGHEST) / islands)
     half = merged_mine.shape[1]
     width = half // pieces
@@ -334,7 +353,7 @@
     pieces = 5
     return pl.pallas_call(
         functools.partial(final_kernel, islands, pieces),
-        in_specs=[scalars] + [whole] * 10,
+        in_specs=[scalars] + [whole] * 12,
         out_specs=[anywhere] * 4,
         out_shape=[
             shaped((rows, cols), jnp.bfloat16),
@@ -348,7 +367,7 @@
         compiler_params=params(24),
         cost_estimate=cost(2 * rows * cols * rank, 8 * rows * cols),
     )(
-        which, to_near(inverse), to_near(product), to_near(arrived), to_near(basis), to_near(mine), to_near(other),
+        which, to_near(inverse), *[to_near(array) for array in (product, *arrived)], to_near(basis), to_near(mine), to_near(other),
         to_near(carried), to_near(block), master, momentum,
     )
 
@@ -419,8 +438,18 @@
         input_output_aliases={2 + len(after) + place: place for place in range(len(held))},
         compiler_params=params(),
         cost_estimate=cost(first.size, 12 * first.size),
-    )(to_near(first), second, *after, *[to_far(array) for array in held])
+    )(to_near(first), to_near(second), *after, *[to_far(array) for array in held])
     return outs[-1], outs[:-1]
+
+
+def from_pairs(values):
+    evens, odds = range(0, 8, 2), range(1, 8, 2)
+
+    def send(even_by, odd_by):
+        routes = [(place, (place + even_by) % 8) for place in evens]
+        return lax.ppermute(values, "z", routes + [(place, (place + odd_by) % 8) for place in odds])
+
+    return send(-3, 3), send(-1, 1), send(-2, 2)
 
 
 def shift(values, by):
@@ -449,33 +478,32 @@
     received = swap(given, "core", 2, 1)
     across = swap(own, "xh", 2, 1)
     kept, merged_mine = project(which_mine, grad, error, basis_prev, jnp.float32)
-    mine, bundle = combine(kept, received, own, across)
+    mine = combine(kept, received)
+    bundle = bundle_of(own, across)
     up, down = shift(bundle, 1), shift(bundle, -1)
     up_two, down_two = shift(up, 1), shift(down, -1)
     chunks = lax.all_to_all(mine.reshape(16, rank // 16, half), plane, 0, 0, tiled=True)
     block = sum_chunks(chunks, (up, down))
     pieces = [bundle, up, down]
     block, _ = add_after(block, swap(block, "z", 8, 1), ())
-    block, _ = add_after(block, swap(block, "z", 8, 2), (up_two, down_two))
-    copies, (up, down) = spread(block, swap(block, "z", 8, 4), 16, (up_two, down_two))
+    copies, (up, down) = spread(block, from_pairs(block), 16, (up_two, down_two))
     pieces += [up, down]
     up, down = shift(up, 1), shift(down, -1)
-    far_side = shift(up, 1)
-    pieces += [up, down, far_side]
     mine = lax.all_to_all(copies, plane, 0, 0, tiled=True)
     mine = pass_after(mine, (up, down)).reshape(rank, half)
     other = swap(mine, "core", 2, 1)
 
     before, _ = product_of(merged_mine, mine)
-    (product, gram_mat), _ = product_of(merged_other, other, before)
-
-    inverse = inverse_factor(gram_mat)
-    product, _ = add_after(product, swap(product, "xh", 2, 1), (inverse, far_side))
-    product, _ = add_after(product, swap(product, "z", 8, 1), ())
+    (product, gram_mat), (up,) = product_of(merged_other, other, before, (up,))
+    far_side = shift(up, 1)
+    pieces += [up, down, far_side]
+
+    inverse = inverse_factor(gram_mat, (mine, other))
+    product, _ = add_after(product, swap(product, "xh", 2, 1), (inverse,))
     basis_bf, basis_block = basis_of(which_mine, side, depth, inverse, mine, other, master.shape[0], product)
-    product, _ = add_after(product, swap(product, "z", 8, 2), (basis_bf,))
+    product, _ = add_after(product, swap(product, "z", 8, 1), (basis_bf, far_side))
     carried = gather_pieces(side, depth, pieces, (0, -1, 1, -2, 2, -3, 3, -4), product)
-    arrived = swap(product, "z", 8, 4)
+    arrived = from_pairs(product)
 
     error_next, weights_next, master_next, momentum_next = final(
         16, which_mine, inverse, product, arrived, basis_bf, merged_mine, merged_other, carried, basis_block,

time: 109 us -> 101 us (0.927)
  waiting for transfers between devices: 45.4 us -> 33.3 us
  starting transfers between devices: 39.6 us -> 43 us
    ppermute x10 -> x6, waiting for transfers between devices: 29.2 us -> 10.6 us  [swap(): lax.ppermute(values, axis, [(place, place ^ bit) for place in range(size)])]
    ppermute x0 -> x6, starting transfers between devices: none -> 10.9 us  [send(): lax.ppermute(values, 'z', routes + [(place, (place + odd_by) % 8) for pla...]
    ppermute x0 -> x6, waiting for transfers between devices: none -> 10.1 us  [send(): lax.ppermute(values, 'z', routes + [(place, (place + odd_by) % 8) for pla...]
    ppermute x10 -> x6, starting transfers between devices: 10.7 us -> 6.36 us  [swap(): lax.ppermute(values, axis, [(place, place ^ bit) for place in range(size)])]
    ppermute x7, waiting for transfers between devices: 16.2 us -> 12.3 us  [shift(): lax.ppermute(values, 'z', [(place, (place + by) % 8) for place in range(8)])]
    all_to_all x1, starting transfers between devices: 7.39 us -> 5.51 us  [local(): lax.all_to_all(mine.reshape(16, rank // 16, half), plane, 0, 0, tiled=True)]
    ppermute x7, starting transfers between devices: 14.3 us -> 13 us  [shift(): lax.ppermute(values, 'z', [(place, (place + by) % 8) for place in range(8)])]
    pallas_call x3 -> x4, Pallas kernels: 6.02 us -> 6.74 us  [the longest x1 4.15 us: inverse_factor(): pl.pallas_call(factor_kernel, in_specs=[whole] + [anywhere] * len(kept),...]
  transfers between devices with their start and end apart: 19 -> 21, of which waited for: 13 -> 10; matrix products, arithmetic and copies ran while one was open for 0% -> 0% of each run, Pallas kernels for 12% -> 13%
where the time goes in v4:
time: 101 us; the launch traced here: 100 us
  starting transfers between devices  43 us (43%)
  waiting for transfers between devices  33.3 us (33%)
  Pallas kernels  21.5 us (21%)
  local copies, waits for them, and re-layouts  1.55 us (2%)
    ppermute x7, starting transfers between devices, shift(): lax.ppermute(values, 'z', [(place, (place + by) % 8) for place in range(8)])  13 us
    ppermute x7, waiting for transfers between devices, shift(): lax.ppermute(values, 'z', [(place, (place + by) % 8) for place in range(8)])  12.3 us
    ppermute x6, starting transfers between devices, send(): lax.ppermute(values, 'z', routes + [(place, (place + odd_by) % 8) for pla...  10.9 us
    ppermute x6, waiting for transfers between devices, swap(): lax.ppermute(values, axis, [(place, place ^ bit) for place in range(size)])  10.6 us
    ppermute x6, waiting for transfers between devices, send(): lax.ppermute(values, 'z', routes + [(place, (place + odd_by) % 8) for pla...  10.1 us
    all_to_all x1, starting transfers between devices, local(): mine = lax.all_to_all(copies, plane, 0, 0, tiled=True)  7.23 us
    ppermute x6, starting transfers between devices, swap(): lax.ppermute(values, axis, [(place, place ^ bit) for place in range(size)])  6.36 us
    all_to_all x1, starting transfers between devices, local(): lax.all_to_all(mine.reshape(16, rank // 16, half), plane, 0, 0, tiled=True)  5.51 us
  transfers between devices with their start and end apart: 21, of which 10 were waited for; matrix products, arithmetic and copies ran while one was open for 0% of the time, Pallas kernels for 13%

profile of v4, /device:TPU:8, one launch (start us, length us, event | category | flops | bytes accessed | tf_op | source)
XLA Modules:
  0.0 100.3 jit_solution(11246800070575997111)
XLA Ops:
  0.6 2.4 %shard_map.84 = (bf16[128,2560]{1,0:T(8,128)(2,1)S(1)}, bf16[240,2560]{1,0:T(8,128)(2,1)S(1)}, bf16[320,240]{1,0:T(8,128)(2,1)S(1)}) custom-call(s32[1]{0:T(128)} %bitcast.1.which, bf16[240,5120]{1,0:T(8,128)(2,1)} %bitcast.21, bf16[240,5120]{1,0:T(8,128)(2,1)} %bitcast.23, bf16[240,128]{1,0:T(8,128)(2,1)} %basis.3, f32[320,240]{1,0:T(8,128)} %bitcast.17, ...), custom_call_target="tpu_custom_call" | custom-call | flops 157286400 | bytes 2457600 | tf_op jit(solution)/shard_map/pallas_call | solution.py:127
  3.1 3.1 %collective-permute-start.1 = (bf16[320,240]{1,0:T(8,128)(2,1)S(1)}, bf16[320,240]{1,0:T(8,128)(2,1)S(1)}, u32[]{:S(2)}, u32[]{:S(2)}) collective-permute-start(bf16[320,240]{1,0:T(8,128)(2,1)S(1)} %get-tuple-element.26.own), channel_id=1, source_target_pairs={{0,128},{128,0},{1,129},{129,1},{2,130},{130,2},{3,131},{131,3},{4... | collective-permute-start | bytes 460808 | tf_op jit(solution)/shard_map/ppermute | solution.py:460
  6.2 2.3 %shard_map.85 = (f32[128,2560]{1,0:T(8,128)S(1)}, bf16[240,2560]{1,0:T(8,128)(2,1)S(1)}) custom-call(s32[1]{0:T(128)} %bitcast.which, bf16[240,5120]{1,0:T(8,128)(2,1)} %bitcast.22, bf16[240,5120]{1,0:T(8,128)(2,1)} %bitcast.24, bf16[240,128]{1,0:T(8,128)(2,1)} %basis.3), custom_call_target="tpu_custom_call" | custom-call | flops 157286400 | bytes 2457600 | tf_op jit(solution)/shard_map/pallas_call | solution.py:127
  8.6 0.9 shard_map.86
  9.6 5.5 %all-to-all-start = ((bf16[16,8,2560]{2,1,0:T(8,128)(2,1)}), bf16[16,8,2560]{2,1,0:T(8,128)(2,1)S(1)}, u32[]{:S(2)}, u32[]{:S(2)}) async-start(bf16[16,8,2560]{2,1,0:T(8,128)(2,1)} %bitcast.6), calls=%async_computation | async-start | bytes 1310720 | tf_op jit(solution)/shard_map/all_to_all | solution.py:485
  15.1 0.7 shard_map.87.refs_0_
  15.8 5.9 %collective-permute-start.3 = (bf16[2,320,240]{2,1,0:T(8,128)(2,1)}, bf16[2,320,240]{2,1,0:T(8,128)(2,1)}, u32[]{:S(2)}, u32[]{:S(2)}) collective-permute-start(bf16[2,320,240]{2,1,0:T(8,128)(2,1)} %shard_map.87.refs_0_), channel_id=1, source_target_pairs={{0,112},{16,0},{32,16},{48,32},{64,48},{80,64},{96,80},{112,96},{1... | collective-permute-start | bytes 921608 | tf_op jit(solution)/shard_map/ppermute | solution.py:464
  21.7 7.0 %collective-permute-done.3.rest_1_.refs_2_ = bf16[2,320,240]{2,1,0:T(8,128)(2,1)} collective-permute-done((bf16[2,320,240]{2,1,0:T(8,128)(2,1)}, bf16[2,320,240]{2,1,0:T(8,128)(2,1)}, u32[]{:S(2)}, u32[]{:S(2)}) %collective-permute-start.3) | collective-permute-done | bytes 307232 | tf_op jit(solution)/shard_map/ppermute | solution.py:464
  28.7 3.7 %collective-permute-start.9 = (bf16[2,320,240]{2,1,0:T(8,128)(2,1)}, bf16[2,320,240]{2,1,0:T(8,128)(2,1)S(1)}, u32[]{:S(2)}, u32[]{:S(2)}) collective-permute-start(bf16[2,320,240]{2,1,0:T(8,128)(2,1)} %collective-permute-done.3.rest_1_.refs_2_), channel_id=1, source_target_pairs={{0,112},{16,0},{32,16},{48,32},{64,48},{80,64},{96,80},{112,96},{1... | collective-permute-start | bytes 921608 | tf_op jit(solution)/shard_map/ppermute | solution.py:464
  32.6 6.7 %collective-permute-done.4.second = bf16[8,2560]{1,0:T(8,128)(2,1)S(1)} collective-permute-done((bf16[8,2560]{1,0:T(8,128)(2,1)S(1)}, bf16[8,2560]{1,0:T(8,128)(2,1)S(1)}, u32[]{:S(2)}, u32[]{:S(2)}) %collective-permute-start.4) | collective-permute-done | bytes 40992 | tf_op jit(solution)/shard_map/ppermute | solution.py:460
  39.3 2.3 %collective-permute-start.7 = (bf16[8,2560]{1,0:T(8,128)(2,1)S(1)}, bf16[8,2560]{1,0:T(8,128)(2,1)S(1)}, u32[]{:S(2)}, u32[]{:S(2)}) collective-permute-start(bf16[8,2560]{1,0:T(8,128)(2,1)S(1)} %shard_map.89.block), channel_id=1, source_target_pairs={{0,96},{32,0},{64,32},{96,64},{16,48},{48,80},{80,112},{112,16},{1... | collective-permute-start | bytes 122888 | tf_op jit(solution)/shard_map/ppermute | solution.py:450
  41.6 3.0 %collective-permute-start.6 = (bf16[8,2560]{1,0:T(8,128)(2,1)S(1)}, bf16[8,2560]{1,0:T(8,128)(2,1)S(1)}, u32[]{:S(2)}, u32[]{:S(2)}) collective-permute-start(bf16[8,2560]{1,0:T(8,128)(2,1)S(1)} %shard_map.89.block), channel_id=1, source_target_pairs={{0,112},{32,16},{64,48},{96,80},{16,32},{48,64},{80,96},{112,0},{1... | collective-permute-start | bytes 122888 | tf_op jit(solution)/shard_map/ppermute | solution.py:450
  44.6 2.4 %collective-permute-done.6.before = bf16[8,2560]{1,0:T(8,128)(2,1)S(1)} collective-permute-done((bf16[8,2560]{1,0:T(8,128)(2,1)S(1)}, bf16[8,2560]{1,0:T(8,128)(2,1)S(1)}, u32[]{:S(2)}, u32[]{:S(2)}) %collective-permute-start.6) | collective-permute-done | bytes 40992 | tf_op jit(solution)/shard_map/ppermute | solution.py:450
  47.0 4.7 %collective-permute-done.5.opposite = bf16[8,2560]{1,0:T(8,128)(2,1)S(1)} collective-permute-done((bf16[8,2560]{1,0:T(8,128)(2,1)S(1)}, bf16[8,2560]{1,0:T(8,128)(2,1)S(1)}, u32[]{:S(2)}, u32[]{:S(2)}) %collective-permute-start.5) | collective-permute-done | bytes 40992 | tf_op jit(solution)/shard_map/ppermute | solution.py:450
  51.7 0.9 shard_map.90
  52.6 7.2 %all-to-all-start.1 = ((bf16[16,8,2560]{2,1,0:T(8,128)(2,1)}), bf16[16,8,2560]{2,1,0:T(8,128)(2,1)S(1)}, u32[]{:S(2)}, u32[]{:S(2)}) async-start(bf16[16,8,2560]{2,1,0:T(8,128)(2,1)} %get-tuple-element.27), calls=%async_computation.1 | async-start | bytes 1310720 | tf_op jit(solution)/shard_map/all_to_all | solution.py:492
  59.8 3.2 %collective-permute-start.11 = (bf16[2,320,240]{2,1,0:T(8,128)(2,1)}, bf16[2,320,240]{2,1,0:T(8,128)(2,1)}, u32[]{:S(2)}, u32[]{:S(2)}) collective-permute-start(bf16[2,320,240]{2,1,0:T(8,128)(2,1)} %get-tuple-element.29.refs_4_), channel_id=1, source_target_pairs={{0,112},{16,0},{32,16},{48,32},{64,48},{80,64},{96,80},{112,96},{1... | collective-permute-start | bytes 921608 | tf_op jit(solution)/shard_map/ppermute | solution.py:464
  63.1 5.3 %collective-permute-done.10.refs_1_.rest_2_ = bf16[2,320,240]{2,1,0:T(8,128)(2,1)S(1)} collective-permute-done((bf16[2,320,240]{2,1,0:T(8,128)(2,1)}, bf16[2,320,240]{2,1,0:T(8,128)(2,1)S(1)}, u32[]{:S(2)}, u32[]{:S(2)}) %collective-permute-start.10) | collective-permute-done | bytes 307232 | tf_op jit(solution)/shard_map/ppermute | solution.py:464
  69.7 1.4 %collective-permute-done.12.left.refs_1_.other = bf16[128,2560]{1,0:T(8,128)(2,1)S(1)} collective-permute-done((bf16[128,2560]{1,0:T(8,128)(2,1)S(1)}, bf16[128,2560]{1,0:T(8,128)(2,1)S(1)}, u32[]{:S(2)}, u32[]{:S(2)}) %collective-permute-start.12) | collective-permute-done | bytes 655392 | tf_op jit(solution)/shard_map/ppermute | solution.py:460
  71.1 0.7 shard_map.93
  72.1 3.1 %collective-permute-start.13 = (bf16[240,128]{1,0:T(8,128)(2,1)S(1)}, bf16[240,128]{1,0:T(8,128)(2,1)S(1)}, u32[]{:S(2)}, u32[]{:S(2)}) collective-permute-start(bf16[240,128]{1,0:T(8,128)(2,1)S(1)} %get-tuple-element.34.first), channel_id=1, source_target_pairs={{0,128},{128,0},{1,129},{129,1},{2,130},{130,2},{3,131},{131,3},{4... | collective-permute-start | bytes 184328 | tf_op jit(solution)/shard_map/ppermute | solution.py:460
  75.1 4.2 %shard_map.94.rest_0_.inverse = f32[128,128]{1,0:T(8,128)S(1)} custom-call(f32[128,128]{1,0:T(8,128)S(1)} %get-tuple-element.33.gram_mat, bf16[128,2560]{1,0:T(8,128)(2,1)S(1)} %bitcast.15, bf16[128,2560]{1,0:T(8,128)(2,1)S(1)} %collective-permute-done.12.left.refs_1_.other), custom_call_target="tpu_custom_call" | custom-call | flops 1000000000 | bytes 262144 | tf_op jit(solution)/shard_map/pallas_call | solution.py:277
  80.0 1.1 %copy-done.1 = bf16[128,2560]{1,0:T(8,128)(2,1)S(1)} copy-done((bf16[128,2560]{1,0:T(8,128)(2,1)S(1)}, bf16[128,2560]{1,0:T(8,128)(2,1)}, u32[]{:S(2)}) %copy-start.1) | copy-done | bytes 655384
  81.1 1.0 shard_map.96
  82.0 2.5 %collective-permute-done.14.second = bf16[240,128]{1,0:T(8,128)(2,1)} collective-permute-done((bf16[240,128]{1,0:T(8,128)(2,1)}, bf16[240,128]{1,0:T(8,128)(2,1)}, u32[]{:S(2)}, u32[]{:S(2)}) %collective-permute-start.14) | collective-permute-done | bytes 61472 | tf_op jit(solution)/shard_map/ppermute | solution.py:460
  84.5 1.0 shard_map.97._.product
  85.5 4.1 %collective-permute-start.18 = (bf16[240,128]{1,0:T(8,128)(2,1)S(1)}, bf16[240,128]{1,0:T(8,128)(2,1)S(1)}, u32[]{:S(2)}, u32[]{:S(2)}) collective-permute-start(bf16[240,128]{1,0:T(8,128)(2,1)S(1)} %shard_map.97._.product), channel_id=1, source_target_pairs={{0,96},{32,0},{64,32},{96,64},{16,48},{48,80},{80,112},{112,16},{1... | collective-permute-start | bytes 184328 | tf_op jit(solution)/shard_map/ppermute | solution.py:450
  89.6 1.6 %collective-permute-start.16 = (bf16[240,128]{1,0:T(8,128)(2,1)S(1)}, bf16[240,128]{1,0:T(8,128)(2,1)S(1)}, u32[]{:S(2)}, u32[]{:S(2)}) collective-permute-start(bf16[240,128]{1,0:T(8,128)(2,1)S(1)} %shard_map.97._.product), channel_id=1, source_target_pairs={{0,80},{32,112},{64,16},{96,48},{16,64},{48,96},{80,0},{112,32},{1... | collective-permute-start | bytes 184328 | tf_op jit(solution)/shard_map/ppermute | solution.py:450
  91.1 2.7 %shard_map.98.carried = bf16[240,5120]{1,0:T(8,128)(2,1)S(1)} custom-call(s32[1]{0:T(128)} %bitcast.8.side.side_of, s32[1]{0:T(128)} %bitcast.9.depth, bf16[240,128]{1,0:T(8,128)(2,1)S(1)} %shard_map.97._.product, bf16[2,320,240]{2,1,0:T(8,128)(2,1)} %shard_map.87.refs_0_, bf16[2,320,240]{2,1,0:T(8,128)(2,1)} %collective-permute-done.2.rest_0_.refs_1_, ...), custom_call_target="tpu_custom_call" | custom-call | flops 1000000000 | bytes 4915200 | tf_op jit(solution)/shard_map/pallas_call | solution.py:398
  93.8 1.3 %collective-permute-done.17.before = bf16[240,128]{1,0:T(8,128)(2,1)S(1)} collective-permute-done((bf16[240,128]{1,0:T(8,128)(2,1)S(1)}, bf16[240,128]{1,0:T(8,128)(2,1)S(1)}, u32[]{:S(2)}, u32[]{:S(2)}) %collective-permute-start.17) | collective-permute-done | bytes 61472 | tf_op jit(solution)/shard_map/ppermute | solution.py:450
  95.1 1.7 %collective-permute-done.16.opposite = bf16[240,128]{1,0:T(8,128)(2,1)S(1)} collective-permute-done((bf16[240,128]{1,0:T(8,128)(2,1)S(1)}, bf16[240,128]{1,0:T(8,128)(2,1)S(1)}, u32[]{:S(2)}, u32[]{:S(2)}) %collective-permute-start.16) | collective-permute-done | bytes 61472 | tf_op jit(solution)/shard_map/ppermute | solution.py:450
  96.8 3.3 %shard_map.99 = (bf16[240,5120]{1,0:T(8,128)(2,1)}, bf16[240,5120]{1,0:T(8,128)(2,1)}, f32[320,240]{1,0:T(8,128)}, f32[320,240]{1,0:T(8,128)}) custom-call(s32[1]{0:T(128)} %bitcast.which, f32[128,128]{1,0:T(8,128)S(1)} %shard_map.94.rest_0_.inverse, bf16[240,128]{1,0:T(8,128)(2,1)S(1)} %shard_map.97._.product, ...), custom_call_target="tpu_custom_call" | custom-call | flops 314572800 | bytes 9830400 | tf_op jit(solution)/shard_map/pallas_call | solution.py:354
  (40 shorter events, 2.6 us)
Async XLA Ops:
  3.0 5.6 %collective-permute-start = (bf16[128,2560]{1,0:T(8,128)(2,1)S(1)}, bf16[128,2560]{1,0:T(8,128)(2,1)S(1)}, u32[]{:S(2)}, u32[]{:S(2)}) collective-permute-start(bf16[128,2560]{1,0:T(8,128)(2,1)S(1)} %get-tuple-element.25), channel_id=1, source_target_pairs={{0,1},{1,0},{2,3},{3,2},{4,5},{5,4},{6,7},{7,6},{8,9},{9,8},{10,11... | collective-permute-start | bytes 1966088 | tf_op jit(solution)/shard_map/ppermute | solution.py:460
  3.1 11.9 %collective-permute-start.1 = (bf16[320,240]{1,0:T(8,128)(2,1)S(1)}, bf16[320,240]{1,0:T(8,128)(2,1)S(1)}, u32[]{:S(2)}, u32[]{:S(2)}) collective-permute-start(bf16[320,240]{1,0:T(8,128)(2,1)S(1)} %get-tuple-element.26.own), channel_id=1, source_target_pairs={{0,128},{128,0},{1,129},{129,1},{2,130},{130,2},{3,131},{131,3},{4... | collective-permute-start | bytes 460808 | tf_op jit(solution)/shard_map/ppermute | solution.py:460
  9.6 22.9 %all-to-all-start = ((bf16[16,8,2560]{2,1,0:T(8,128)(2,1)}), bf16[16,8,2560]{2,1,0:T(8,128)(2,1)S(1)}, u32[]{:S(2)}, u32[]{:S(2)}) async-start(bf16[16,8,2560]{2,1,0:T(8,128)(2,1)} %bitcast.6), calls=%async_computation | async-start | bytes 1310720 | tf_op jit(solution)/shard_map/all_to_all | solution.py:485
  15.8 12.9 %collective-permute-start.3 = (bf16[2,320,240]{2,1,0:T(8,128)(2,1)}, bf16[2,320,240]{2,1,0:T(8,128)(2,1)}, u32[]{:S(2)}, u32[]{:S(2)}) collective-permute-start(bf16[2,320,240]{2,1,0:T(8,128)(2,1)} %shard_map.87.refs_0_), channel_id=1, source_target_pairs={{0,112},{16,0},{32,16},{48,32},{64,48},{80,64},{96,80},{112,96},{1... | collective-permute-start | bytes 921608 | tf_op jit(solution)/shard_map/ppermute | solution.py:464
  21.7 10.7 %collective-permute-start.2 = (bf16[2,320,240]{2,1,0:T(8,128)(2,1)}, bf16[2,320,240]{2,1,0:T(8,128)(2,1)}, u32[]{:S(2)}, u32[]{:S(2)}) collective-permute-start(bf16[2,320,240]{2,1,0:T(8,128)(2,1)} %shard_map.87.refs_0_), channel_id=1, source_target_pairs={{0,16},{16,32},{32,48},{48,64},{64,80},{80,96},{96,112},{112,0},{1... | collective-permute-start | bytes 921608 | tf_op jit(solution)/shard_map/ppermute | solution.py:464
  28.7 15.9 %collective-permute-start.9 = (bf16[2,320,240]{2,1,0:T(8,128)(2,1)}, bf16[2,320,240]{2,1,0:T(8,128)(2,1)S(1)}, u32[]{:S(2)}, u32[]{:S(2)}) collective-permute-start(bf16[2,320,240]{2,1,0:T(8,128)(2,1)} %collective-permute-done.3.rest_1_.refs_2_), channel_id=1, source_target_pairs={{0,112},{16,0},{32,16},{48,32},{64,48},{80,64},{96,80},{112,96},{1... | collective-permute-start | bytes 921608 | tf_op jit(solution)/shard_map/ppermute | solution.py:464
  32.4 12.2 %collective-permute-start.8 = (bf16[2,320,240]{2,1,0:T(8,128)(2,1)}, bf16[2,320,240]{2,1,0:T(8,128)(2,1)}, u32[]{:S(2)}, u32[]{:S(2)}) collective-permute-start(bf16[2,320,240]{2,1,0:T(8,128)(2,1)} %collective-permute-done.2.rest_0_.refs_1_), channel_id=1, source_target_pairs={{0,16},{16,32},{32,48},{48,64},{64,80},{80,96},{96,112},{112,0},{1... | collective-permute-start | bytes 921608 | tf_op jit(solution)/shard_map/ppermute | solution.py:464
  32.5 6.8 %collective-permute-start.4 = (bf16[8,2560]{1,0:T(8,128)(2,1)S(1)}, bf16[8,2560]{1,0:T(8,128)(2,1)S(1)}, u32[]{:S(2)}, u32[]{:S(2)}) collective-permute-start(bf16[8,2560]{1,0:T(8,128)(2,1)S(1)} %shard_map.88.first), channel_id=1, source_target_pairs={{0,16},{16,0},{32,48},{48,32},{64,80},{80,64},{96,112},{112,96},{1... | collective-permute-start | bytes 122888 | tf_op jit(solution)/shard_map/ppermute | solution.py:460
  39.3 5.3 %collective-permute-start.7 = (bf16[8,2560]{1,0:T(8,128)(2,1)S(1)}, bf16[8,2560]{1,0:T(8,128)(2,1)S(1)}, u32[]{:S(2)}, u32[]{:S(2)}) collective-permute-start(bf16[8,2560]{1,0:T(8,128)(2,1)S(1)} %shard_map.89.block), channel_id=1, source_target_pairs={{0,96},{32,0},{64,32},{96,64},{16,48},{48,80},{80,112},{112,16},{1... | collective-permute-start | bytes 122888 | tf_op jit(solution)/shard_map/ppermute | solution.py:450
  41.6 5.4 %collective-permute-start.6 = (bf16[8,2560]{1,0:T(8,128)(2,1)S(1)}, bf16[8,2560]{1,0:T(8,128)(2,1)S(1)}, u32[]{:S(2)}, u32[]{:S(2)}) collective-permute-start(bf16[8,2560]{1,0:T(8,128)(2,1)S(1)} %shard_map.89.block), channel_id=1, source_target_pairs={{0,112},{32,16},{64,48},{96,80},{16,32},{48,64},{80,96},{112,0},{1... | collective-permute-start | bytes 122888 | tf_op jit(solution)/shard_map/ppermute | solution.py:450
  44.6 7.1 %collective-permute-start.5 = (bf16[8,2560]{1,0:T(8,128)(2,1)S(1)}, bf16[8,2560]{1,0:T(8,128)(2,1)S(1)}, u32[]{:S(2)}, u32[]{:S(2)}) collective-permute-start(bf16[8,2560]{1,0:T(8,128)(2,1)S(1)} %shard_map.89.block), channel_id=1, source_target_pairs={{0,80},{32,112},{64,16},{96,48},{16,64},{48,96},{80,0},{112,32},{1... | collective-permute-start | bytes 122888 | tf_op jit(solution)/shard_map/ppermute | solution.py:450
  44.6 7.1 %copy-start.6 = (bf16[2,320,240]{2,1,0:T(8,128)(2,1)}, bf16[2,320,240]{2,1,0:T(8,128)(2,1)S(1)}, u32[]{:S(2)}) copy-start(bf16[2,320,240]{2,1,0:T(8,128)(2,1)S(1)} %collective-permute-done.9.rest_1_) | copy-start | bytes 921604
  52.6 16.0 %all-to-all-start.1 = ((bf16[16,8,2560]{2,1,0:T(8,128)(2,1)}), bf16[16,8,2560]{2,1,0:T(8,128)(2,1)S(1)}, u32[]{:S(2)}, u32[]{:S(2)}) async-start(bf16[16,8,2560]{2,1,0:T(8,128)(2,1)} %get-tuple-element.27), calls=%async_computation.1 | async-start | bytes 1310720 | tf_op jit(solution)/shard_map/all_to_all | solution.py:492
  59.8 8.5 %collective-permute-start.10 = (bf16[2,320,240]{2,1,0:T(8,128)(2,1)}, bf16[2,320,240]{2,1,0:T(8,128)(2,1)S(1)}, u32[]{:S(2)}, u32[]{:S(2)}) collective-permute-start(bf16[2,320,240]{2,1,0:T(8,128)(2,1)} %get-tuple-element.28.refs_3_), channel_id=1, source_target_pairs={{0,16},{16,32},{32,48},{48,64},{64,80},{80,96},{96,112},{112,0},{1... | collective-permute-start | bytes 921608 | tf_op jit(solution)/shard_map/ppermute | solution.py:464
  59.8 8.5 %collective-permute-start.11 = (bf16[2,320,240]{2,1,0:T(8,128)(2,1)}, bf16[2,320,240]{2,1,0:T(8,128)(2,1)}, u32[]{:S(2)}, u32[]{:S(2)}) collective-permute-start(bf16[2,320,240]{2,1,0:T(8,128)(2,1)} %get-tuple-element.29.refs_4_), channel_id=1, source_target_pairs={{0,112},{16,0},{32,16},{48,32},{64,48},{80,64},{96,80},{112,96},{1... | collective-permute-start | bytes 921608 | tf_op jit(solution)/shard_map/ppermute | solution.py:464
  68.3 0.7 copy-start.5
  69.0 2.1 %collective-permute-start.12 = (bf16[128,2560]{1,0:T(8,128)(2,1)S(1)}, bf16[128,2560]{1,0:T(8,128)(2,1)S(1)}, u32[]{:S(2)}, u32[]{:S(2)}) collective-permute-start(bf16[128,2560]{1,0:T(8,128)(2,1)S(1)} %bitcast.13), channel_id=1, source_target_pairs={{0,1},{1,0},{2,3},{3,2},{4,5},{5,4},{6,7},{7,6},{8,9},{9,8},{10,11... | collective-permute-start | bytes 1966088 | tf_op jit(solution)/shard_map/ppermute | solution.py:460
  71.1 8.2 %copy-start = (bf16[128,2560]{1,0:T(8,128)(2,1)}, bf16[128,2560]{1,0:T(8,128)(2,1)S(1)}, u32[]{:S(2)}) copy-start(bf16[128,2560]{1,0:T(8,128)(2,1)S(1)} %collective-permute-done.12.left.refs_1_.other) | copy-start | bytes 1966084
  71.8 12.7 %collective-permute-start.15 = (bf16[2,320,240]{2,1,0:T(8,128)(2,1)}, bf16[2,320,240]{2,1,0:T(8,128)(2,1)S(1)}, u32[]{:S(2)}, u32[]{:S(2)}) collective-permute-start(bf16[2,320,240]{2,1,0:T(8,128)(2,1)} %get-tuple-element.36.refs_5_), channel_id=1, source_target_pairs={{0,16},{16,32},{32,48},{48,64},{64,80},{80,96},{96,112},{112,0},{1... | collective-permute-start | bytes 921608 | tf_op jit(solution)/shard_map/ppermute | solution.py:464
  72.1 7.2 %collective-permute-start.13 = (bf16[240,128]{1,0:T(8,128)(2,1)S(1)}, bf16[240,128]{1,0:T(8,128)(2,1)S(1)}, u32[]{:S(2)}, u32[]{:S(2)}) collective-permute-start(bf16[240,128]{1,0:T(8,128)(2,1)S(1)} %get-tuple-element.34.first), channel_id=1, source_target_pairs={{0,128},{128,0},{1,129},{129,1},{2,130},{130,2},{3,131},{131,3},{4... | collective-permute-start | bytes 184328 | tf_op jit(solution)/shard_map/ppermute | solution.py:460
  80.0 4.5 %collective-permute-start.14 = (bf16[240,128]{1,0:T(8,128)(2,1)}, bf16[240,128]{1,0:T(8,128)(2,1)}, u32[]{:S(2)}, u32[]{:S(2)}) collective-permute-start(bf16[240,128]{1,0:T(8,128)(2,1)} %shard_map.95._.first), channel_id=1, source_target_pairs={{0,16},{16,0},{32,48},{48,32},{64,80},{80,64},{96,112},{112,96},{1... | collective-permute-start | bytes 184328 | tf_op jit(solution)/shard_map/ppermute | solution.py:460
  80.0 1.1 %copy-start.1 = (bf16[128,2560]{1,0:T(8,128)(2,1)S(1)}, bf16[128,2560]{1,0:T(8,128)(2,1)}, u32[]{:S(2)}) copy-start(bf16[128,2560]{1,0:T(8,128)(2,1)} %copy-done) | copy-start | bytes 1966084
  84.5 6.6 %copy-start.4 = (bf16[2,320,240]{2,1,0:T(8,128)(2,1)}, bf16[2,320,240]{2,1,0:T(8,128)(2,1)S(1)}, u32[]{:S(2)}) copy-start(bf16[2,320,240]{2,1,0:T(8,128)(2,1)S(1)} %collective-permute-done.15.rest_1_.refs_7_) | copy-start | bytes 921604
  85.5 11.3 %copy-start.2 = (f32[240,320]{0,1:T(8,128)S(1)}, f32[240,320]{0,1:T(8,128)}, u32[]{:S(2)}) copy-start(f32[240,320]{0,1:T(8,128)} %param.8) | copy-start | bytes 921604
  85.5 11.3 %copy-start.3 = (f32[240,320]{0,1:T(8,128)S(1)}, f32[240,320]{0,1:T(8,128)}, u32[]{:S(2)}) copy-start(f32[240,320]{0,1:T(8,128)} %param.9) | copy-start | bytes 921604
  85.5 8.3 %collective-permute-start.18 = (bf16[240,128]{1,0:T(8,128)(2,1)S(1)}, bf16[240,128]{1,0:T(8,128)(2,1)S(1)}, u32[]{:S(2)}, u32[]{:S(2)}) collective-permute-start(bf16[240,128]{1,0:T(8,128)(2,1)S(1)} %shard_map.97._.product), channel_id=1, source_target_pairs={{0,96},{32,0},{64,32},{96,64},{16,48},{48,80},{80,112},{112,16},{1... | collective-permute-start | bytes 184328 | tf_op jit(solution)/shard_map/ppermute | solution.py:450
  89.6 5.6 %collective-permute-start.17 = (bf16[240,128]{1,0:T(8,128)(2,1)S(1)}, bf16[240,128]{1,0:T(8,128)(2,1)S(1)}, u32[]{:S(2)}, u32[]{:S(2)}) collective-permute-start(bf16[240,128]{1,0:T(8,128)(2,1)S(1)} %shard_map.97._.product), channel_id=1, source_target_pairs={{0,112},{32,16},{64,48},{96,80},{16,32},{48,64},{80,96},{112,0},{1... | collective-permute-start | bytes 184328 | tf_op jit(solution)/shard_map/ppermute | solution.py:450
  89.6 7.2 %collective-permute-start.16 = (bf16[240,128]{1,0:T(8,128)(2,1)S(1)}, bf16[240,128]{1,0:T(8,128)(2,1)S(1)}, u32[]{:S(2)}, u32[]{:S(2)}) collective-permute-start(bf16[240,128]{1,0:T(8,128)(2,1)S(1)} %shard_map.97._.product), channel_id=1, source_target_pairs={{0,80},{32,112},{64,16},{96,48},{16,64},{48,96},{80,0},{112,32},{1... | collective-permute-start | bytes 184328 | tf_op jit(solution)/shard_map/ppermute | solution.py:450

commit v5 on v4

--- a/solution.py
+++ b/solution.py
@@ -16,7 +16,7 @@
 fsdp = ("y", "xl", "core")
 plane = ("xh", "y", "xl")
 panel = 32
-group = 8
+group = 16
 whole = pl.BlockSpec(memory_space=pltpu.VMEM)
 anywhere = pl.BlockSpec(memory_space=pl.ANY)
 scalars = pl.BlockSpec(memory_space=pltpu.SMEM)
@@ -48,6 +48,10 @@
     return pltpu.HBM(shape, dtype)
 
 
+def all_near(arrays):
+    return [to_near(array) for array in arrays]
+
+
 def near(shape, dtype):
     return pltpu.VMEM(shape, dtype)
 
@@ -75,11 +79,11 @@
 
 
 def project_kernel(pieces, which, grad, error, basis, *rest):
-    first = len(rest) > 6
+    first = len(rest) > 7
     if first:
         master, momentum, left_out, merged_out, own_out, grads, errors, bases, sems, masters, momenta = rest
     else:
-        left_out, merged_out, grads, errors, bases, sems = rest
+        left_out, merged_out, grads, errors, bases, sems = rest[-6:]
     half = left_out.shape[1]
     width = half // pieces
     start = which[0] * half
@@ -107,7 +111,7 @@
         own_out[...] = to_bf(masters[...] - momentum_part * momenta[...])
 
 
-def project(which, grad, error, basis, dtype, master=None, momentum=None):
+def project(which, grad, error, basis, dtype, master=None, momentum=None, held=()):
     rows, cols = grad.shape
     rank = basis.shape[1]
     half = cols // 2
@@ -120,6 +124,7 @@
         pltpu.VMEM((rows, rank), jnp.bfloat16),
         pltpu.SemaphoreType.DMA((3 + 2 * pieces,)),
     ]
+    operands += all_near(held)
     if master is not None:
         operands += [to_far(master), to_far(momentum)]
         out_shape.append(near(master.shape, jnp.bfloat16))
@@ -135,19 +140,19 @@
     )(*operands)
 
 
-def combine_kernel(kept, received, mine_out):
-    mine_out[...] = to_bf(kept[...] + to_f32(received[...]))
-
-
-def combine(kept, received):
+def combine_kernel(kept, received, *rest):
+    rest[-1][...] = to_bf(kept[...] + to_f32(received[...]))
+
+
+def combine(kept, received, held):
     return pl.pallas_call(
         combine_kernel,
-        in_specs=[whole] * 2,
+        in_specs=[whole] * 2 + [anywhere] * len(held),
         out_specs=whole,
         out_shape=shaped(kept.shape, jnp.bfloat16),
         compiler_params=params(),
         cost_estimate=cost(kept.size, 8 * kept.size),
-    )(to_near(kept), to_near(received))
+    )(to_near(kept), to_near(received), *all_near(held))
 
 
 def bundle_kernel(own, across, out):
@@ -174,22 +179,22 @@
     out[...] = to_bf(total)
 
 
-def sum_chunks(chunks, after):
+def sum_chunks(chunks, after, held):
     return pl.pallas_call(
         sum_kernel,
-        in_specs=[whole] + [anywhere] * len(after),
+        in_specs=[whole] + [anywhere] * (len(after) + len(held)),
         out_specs=whole,
         out_shape=near(chunks.shape[1:], jnp.bfloat16),
         compiler_params=params(),
         cost_estimate=cost(chunks.size, 2 * chunks.size),
-    )(to_near(chunks), *[to_far(array) for array in after])
+    )(to_near(chunks), *[to_far(array) for array in after], *all_near(held))
 
 
 def sum_pairs(own, opposite, before, after):
     return (to_f32(own[...]) + to_f32(opposite[...])) + (to_f32(before[...]) + to_f32(after[...]))
 
 
-def spread_kernel(count, block, opposite, before, after, *rest):
+def spread_kernel(count, block, before, after, opposite, *rest):
     out = rest[-1]
     total = to_bf(sum_pairs(block, opposite, before, after))
     for place in range(count):
@@ -318,7 +323,7 @@
 
 
 def final_kernel(
-    islands, pieces, which, inverse, product, opposite, before, after, basis, merged_mine, merged_other, carried, block, master,
+    islands, pieces, which, inverse, product, before, after, opposite, basis, merged_mine, merged_other, carried, block, master,
     momentum, error_out, weights_out, master_out, momentum_out, errors, weights, masters, momenta, sems,
 ):
     total = sum_pairs(product, opposite, before, after)
@@ -372,57 +377,79 @@
     )
 
 
-def gather_kernel(shifts, side_of, depth, _, *refs):
-    pieces, out, held, sems = refs[:-3], refs[-3], refs[-2], refs[-1]
+def gather_kernel(shifts, side_of, depth, *refs):
+    count = len(shifts)
+    pieces, out, token, held, sems = refs[:count], *refs[-4:]
+    token[...] = jnp.zeros_like(token)
     size = pieces[0].shape[1]
-    count = len(shifts)
+    ring = held.shape[1] // size
     waits = []
     for number in range(count):
-        z_of = lax.rem(depth[0] + (shifts[number] + count), count)
+        z_of = lax.rem(depth[0] + (shifts[number] + ring), ring)
         rows = pl.ds(pl.multiple_of(z_of * size, size), size)
-        for side in range(2):
-            waits.append(fetch(pieces[number].at[side], held.at[side, rows], sems.at[len(waits)]))
+        for half in range(2):
+            waits.append(fetch(pieces[number].at[half], held.at[half, rows], sems.at[len(waits)]))
     for copy in waits:
         copy.wait()
-    span = count * size
-    for side in range(2):
-        start = lax.rem(side_of[0] + side, 2) * span
-        for first in range(0, span, 2 * size):
-            lanes = pl.ds(pl.multiple_of(start + first, 128), 2 * size)
-            out[:, lanes] = to_bf(to_f32(held[side, first : first + 2 * size, :]).T)
-
-
-def gather_pieces(side, depth, pieces, shifts, after):
+    pairs = ring // 2
+    own = depth[0] // 2
+    beyond = own + lax.rem(depth[0], 2) * 2 + (pairs - 1)
+    turn = 0 if len(refs) == count + 4 else 2
+    span = ring * size
+    for pair in (own, beyond):
+        first = lax.rem(pair + turn, pairs) * (2 * size)
+        for half in range(2):
+            start = lax.rem(side_of[0] + half, 2) * span
+            lanes = pl.ds(pl.multiple_of(start + first, 2 * size), 2 * size)
+            rows = pl.ds(pl.multiple_of(first, 2 * size), 2 * size)
+            out[:, lanes] = to_bf(to_f32(held[half, rows, :]).T)
+
+
+def gather_pieces(side, depth, pieces, shifts, before=()):
     rows, cols = pieces[0].shape[1:]
-    count = 2 * len(pieces)
+    count = len(pieces)
+    ring = 8
     return pl.pallas_call(
         functools.partial(gather_kernel, shifts),
-        in_specs=[scalars] * 2 + [anywhere] * (1 + len(pieces)),
-        out_specs=whole,
-        out_shape=near((cols, count * rows), jnp.bfloat16),
+        in_specs=[scalars] * 2 + [anywhere] * count + ([whole, anywhere] if before else []),
+        out_specs=[whole] * 2,
+        out_shape=[near((cols, 2 * ring * rows), jnp.bfloat16), near((8, 128), jnp.float32)],
         scratch_shapes=[
-            pltpu.VMEM((2, len(pieces) * rows, cols), jnp.bfloat16),
-            pltpu.SemaphoreType.DMA((count,)),
+            pltpu.VMEM((2, ring * rows, cols), jnp.bfloat16),
+            pltpu.SemaphoreType.DMA((2 * count,)),
         ],
+        input_output_aliases={2 + count: 0} if before else {},
         compiler_params=params(),
         cost_estimate=cost(10**9, 4 * count * rows * cols),
-    )(side, depth, after, *[to_far(piece) for piece in pieces])
+    )(side, depth, *pieces, *all_near(before))
 
 
 def pass_kernel(*refs):
     pass
 
 
+def pass_through(arrays):
+    return pl.pallas_call(
+        pass_kernel,
+        in_specs=[anywhere] * len(arrays),
+        out_specs=[anywhere] * len(arrays),
+        out_shape=[far(array.shape, array.dtype) for array in arrays],
+        input_output_aliases={place: place for place in range(len(arrays))},
+        compiler_params=params(),
+        cost_estimate=cost(10**11, 1),
+    )(*[to_far(array) for array in arrays])
+
+
 def pass_after(values, after):
     return pl.pallas_call(
         pass_kernel,
-        in_specs=[anywhere] * (1 + len(after)),
+        in_specs=[anywhere] * (len(after) + len(after[-1])),
         out_specs=anywhere,
         out_shape=shaped(values.shape, values.dtype),
         input_output_aliases={0: 0},
         compiler_params=params(),
         cost_estimate=cost(1, 1),
-    )(values, *[to_far(array) for array in after])
+    )(values, *after[:-1], *all_near(after[-1]))
 
 
 def add_kernel(first, second, *rest):
@@ -449,7 +476,33 @@
         routes = [(place, (place + even_by) % 8) for place in evens]
         return lax.ppermute(values, "z", routes + [(place, (place + odd_by) % 8) for place in odds])
 
-    return send(-3, 3), send(-1, 1), send(-2, 2)
+    before = send(-1, 1)
+    after = send(-2, 2)
+    return before, after, send(-3, 3)
+
+
+def from_quad(values):
+    def send(mask):
+        return lax.ppermute(values, island, [(place, place ^ mask) for place in range(16)])
+
+    beside = send(1)
+    across = send(8)
+    return beside, across, send(9)
+
+
+def add_quad_kernel(own, beside, across, corner, *rest):
+    rest[-1][...] = to_bf(sum_pairs(own, across, beside, corner))
+
+
+def add_quad(own, arrived, after):
+    return pl.pallas_call(
+        add_quad_kernel,
+        in_specs=[whole] * 4 + [anywhere] * len(after),
+        out_specs=whole,
+        out_shape=near(own.shape, own.dtype),
+        compiler_params=params(),
+        cost_estimate=cost(own.size, 12 * own.size),
+    )(*all_near((own, *arrived, *after)))
 
 
 def shift(values, by):
@@ -477,33 +530,35 @@
     given, merged_other, own = project(which_other, grad, error, basis_prev, jnp.bfloat16, master, momentum)
     received = swap(given, "core", 2, 1)
     across = swap(own, "xh", 2, 1)
-    kept, merged_mine = project(which_mine, grad, error, basis_prev, jnp.float32)
-    mine = combine(kept, received)
+    kept, merged_mine = project(which_mine, grad, error, basis_prev, jnp.float32, held=(merged_other,))
+    merged = (merged_mine, merged_other)
+    mine = combine(kept, received, merged)
     bundle = bundle_of(own, across)
     up, down = shift(bundle, 1), shift(bundle, -1)
-    up_two, down_two = shift(up, 1), shift(down, -1)
     chunks = lax.all_to_all(mine.reshape(16, rank // 16, half), plane, 0, 0, tiled=True)
-    block = sum_chunks(chunks, (up, down))
+    block = sum_chunks(chunks, (up, down), merged)
+    block, _ = add_after(block, swap(block, "z", 8, 1), [to_near(array) for array in merged])
+    copies, (up, down) = spread(block, from_pairs(block), 16, (up, down))
     pieces = [bundle, up, down]
-    block, _ = add_after(block, swap(block, "z", 8, 1), ())
-    copies, (up, down) = spread(block, from_pairs(block), 16, (up_two, down_two))
+    up, down = pass_through((shift(up, 1), shift(down, -1)))
     pieces += [up, down]
+    begun, token = gather_pieces(side, depth, [to_far(piece) for piece in pieces], (0, -1, 1, -2, 2))
     up, down = shift(up, 1), shift(down, -1)
+    far_side = shift(up, 1)
     mine = lax.all_to_all(copies, plane, 0, 0, tiled=True)
-    mine = pass_after(mine, (up, down)).reshape(rank, half)
+    mine = pass_after(mine, (up, down, token, merged)).reshape(rank, half)
     other = swap(mine, "core", 2, 1)
 
     before, _ = product_of(merged_mine, mine)
-    (product, gram_mat), (up,) = product_of(merged_other, other, before, (up,))
-    far_side = shift(up, 1)
-    pieces += [up, down, far_side]
-
-    inverse = inverse_factor(gram_mat, (mine, other))
-    product, _ = add_after(product, swap(product, "xh", 2, 1), (inverse,))
+    (product, gram_mat), _ = product_of(merged_other, other, before)
+
+    inverse = inverse_factor(gram_mat, (mine, other, *merged))
+    product = add_quad(product, from_quad(product), (inverse, mine, other, *merged))
+    arrived = from_pairs(product)
     basis_bf, basis_block = basis_of(which_mine, side, depth, inverse, mine, other, master.shape[0], product)
-    product, _ = add_after(product, swap(product, "z", 8, 1), (basis_bf, far_side))
-    carried = gather_pieces(side, depth, pieces, (0, -1, 1, -2, 2, -3, 3, -4), product)
-    arrived = from_pairs(product)
+    carried, _ = gather_pieces(
+        side, depth, [*map(to_far, (*pieces[3:], up, down)), to_near(far_side)], (-2, 2, -3, 3, -4), (begun, product)
+    )
 
     error_next, weights_next, master_next, momentum_next = final(
         16, which_mine, inverse, product, arrived, basis_bf, merged_mine, merged_other, carried, basis_block,

time: 101 us -> 96.3 us (0.953)
  waiting for transfers between devices: 33.3 us -> 23.2 us
  starting transfers between devices: 43 us -> 48.9 us
    ppermute x6 -> x4, waiting for transfers between devices: 10.6 us -> 4.55 us  [swap(): lax.ppermute(values, axis, [(place, place ^ bit) for place in range(size)])]
    ppermute x0 -> x3, starting transfers between devices: none -> 5.08 us  [send(): lax.ppermute(values, island, [(place, place ^ mask) for place in range(16)])]
    ppermute x6, waiting for transfers between devices: 10.1 us -> 5.17 us  [send(): lax.ppermute(values, 'z', routes + [(place, (place + odd_by) % 8) for pla...]
    ppermute x6, starting transfers between devices: 10.9 us -> 14.5 us  [send(): lax.ppermute(values, 'z', routes + [(place, (place + odd_by) % 8) for pla...]
    ppermute x6 -> x4, starting transfers between devices: 6.36 us -> 3.39 us  [swap(): lax.ppermute(values, axis, [(place, place ^ bit) for place in range(size)])]
    pallas_call x3 -> x1, Pallas kernels: 1.66 us -> 0.01 us  [add_after(): pl.pallas_call(add_kernel, in_specs=[whole, whole] + [anywhere] * (len(af...]
    pallas_call x1 -> x2, Pallas kernels: 2.68 us -> 4.12 us  [gather_pieces(): pl.pallas_call(functools.partial(gather_kernel, shifts), in_specs=[scalar...]
    ppermute x0 -> x3, waiting for transfers between devices: none -> 1.18 us  [send(): lax.ppermute(values, island, [(place, place ^ mask) for place in range(16)])]
  transfers between devices with their start and end apart: 21 -> 22, of which waited for: 10 -> 9; matrix products, arithmetic and copies ran while one was open for 0% -> 0% of each run, Pallas kernels for 13% -> 15%
where the time goes in v5:
time: 96.3 us; the launch traced here: 95.9 us
  starting transfers between devices  48.9 us (51%)
  waiting for transfers between devices  23.2 us (24%)
  Pallas kernels  20.7 us (21%)
  local copies, waits for them, and re-layouts  2.17 us (2%)
  between operations  1.02 us (1%)
    ppermute x6, starting transfers between devices, send(): lax.ppermute(values, 'z', routes + [(place, (place + odd_by) % 8) for pla...  14.5 us
    ppermute x7, starting transfers between devices, shift(): lax.ppermute(values, 'z', [(place, (place + by) % 8) for place in range(8)])  13.2 us
    ppermute x7, waiting for transfers between devices, shift(): lax.ppermute(values, 'z', [(place, (place + by) % 8) for place in range(8)])  12.3 us
    all_to_all x1, starting transfers between devices, local(): mine = lax.all_to_all(copies, plane, 0, 0, tiled=True)  7.23 us
    all_to_all x1, starting transfers between devices, local(): lax.all_to_all(mine.reshape(16, rank // 16, half), plane, 0, 0, tiled=True)  5.51 us
    ppermute x6, waiting for transfers between devices, send(): lax.ppermute(values, 'z', routes + [(place, (place + odd_by) % 8) for pla...  5.17 us
    ppermute x3, starting transfers between devices, send(): lax.ppermute(values, island, [(place, place ^ mask) for place in range(16)])  5.08 us
    pallas_call x2, Pallas kernels, project(): pl.pallas_call(functools.partial(project_kernel, pieces), in_specs=[scala...  4.73 us
  transfers between devices with their start and end apart: 22, of which 9 were waited for; matrix products, arithmetic and copies ran while one was open for 0% of the time, Pallas kernels for 15%

profile of v5, /device:TPU:8, one launch (start us, length us, event | category | flops | bytes accessed | tf_op | source)
XLA Modules:
  0.0 95.9 jit_solution(5025901977901167113)
XLA Ops:
  0.6 2.4 %shard_map.84 = (bf16[128,2560]{1,0:T(8,128)(2,1)S(1)}, bf16[240,2560]{1,0:T(8,128)(2,1)S(1)}, bf16[320,240]{1,0:T(8,128)(2,1)S(1)}) custom-call(s32[1]{0:T(128)} %bitcast.1.which, bf16[240,5120]{1,0:T(8,128)(2,1)} %bitcast.22, bf16[240,5120]{1,0:T(8,128)(2,1)} %bitcast.24, bf16[240,128]{1,0:T(8,128)(2,1)} %basis.3, f32[320,240]{1,0:T(8,128)} %bitcast.18, ...), custom_call_target="tpu_custom_call" | custom-call | flops 157286400 | bytes 2457600 | tf_op jit(solution)/shard_map/pallas_call | solution.py:132
  3.1 3.1 %collective-permute-start.1 = (bf16[320,240]{1,0:T(8,128)(2,1)S(1)}, bf16[320,240]{1,0:T(8,128)(2,1)S(1)}, u32[]{:S(2)}, u32[]{:S(2)}) collective-permute-start(bf16[320,240]{1,0:T(8,128)(2,1)S(1)} %get-tuple-element.31.own), channel_id=1, source_target_pairs={{0,128},{128,0},{1,129},{129,1},{2,130},{130,2},{3,131},{131,3},{4... | collective-permute-start | bytes 460808 | tf_op jit(solution)/shard_map/ppermute | solution.py:513
  6.2 2.3 %shard_map.85 = (f32[128,2560]{1,0:T(8,128)S(1)}, bf16[240,2560]{1,0:T(8,128)(2,1)S(1)}) custom-call(s32[1]{0:T(128)} %bitcast.which, bf16[240,5120]{1,0:T(8,128)(2,1)} %bitcast.23, bf16[240,5120]{1,0:T(8,128)(2,1)} %bitcast.25, bf16[240,128]{1,0:T(8,128)(2,1)} %basis.3, ...), custom_call_target="tpu_custom_call" | custom-call | flops 157286400 | bytes 2457600 | tf_op jit(solution)/shard_map/pallas_call | solution.py:132
  8.6 0.9 shard_map.86
  9.6 5.5 %all-to-all-start = ((bf16[16,8,2560]{2,1,0:T(8,128)(2,1)}), bf16[16,8,2560]{2,1,0:T(8,128)(2,1)S(1)}, u32[]{:S(2)}, u32[]{:S(2)}) async-start(bf16[16,8,2560]{2,1,0:T(8,128)(2,1)} %bitcast.6), calls=%async_computation | async-start | bytes 1310720 | tf_op jit(solution)/shard_map/all_to_all | solution.py:538
  15.1 0.7 shard_map.87.refs_0_
  15.8 5.9 %collective-permute-start.3 = (bf16[2,320,240]{2,1,0:T(8,128)(2,1)}, bf16[2,320,240]{2,1,0:T(8,128)(2,1)S(1)}, u32[]{:S(2)}, u32[]{:S(2)}) collective-permute-start(bf16[2,320,240]{2,1,0:T(8,128)(2,1)} %shard_map.87.refs_0_), channel_id=1, source_target_pairs={{0,112},{16,0},{32,16},{48,32},{64,48},{80,64},{96,80},{112,96},{1... | collective-permute-start | bytes 921608 | tf_op jit(solution)/shard_map/ppermute | solution.py:517
  21.7 7.0 %collective-permute-done.3.rest_1_ = bf16[2,320,240]{2,1,0:T(8,128)(2,1)S(1)} collective-permute-done((bf16[2,320,240]{2,1,0:T(8,128)(2,1)}, bf16[2,320,240]{2,1,0:T(8,128)(2,1)S(1)}, u32[]{:S(2)}, u32[]{:S(2)}) %collective-permute-start.3) | collective-permute-done | bytes 307232 | tf_op jit(solution)/shard_map/ppermute | solution.py:517
  28.7 3.4 %collective-permute-done.2.rest_0_ = bf16[2,320,240]{2,1,0:T(8,128)(2,1)} collective-permute-done((bf16[2,320,240]{2,1,0:T(8,128)(2,1)}, bf16[2,320,240]{2,1,0:T(8,128)(2,1)}, u32[]{:S(2)}, u32[]{:S(2)}) %collective-permute-start.2) | collective-permute-done | bytes 307232 | tf_op jit(solution)/shard_map/ppermute | solution.py:517
  32.3 4.0 %collective-permute-done.4.second = bf16[8,2560]{1,0:T(8,128)(2,1)S(1)} collective-permute-done((bf16[8,2560]{1,0:T(8,128)(2,1)S(1)}, bf16[8,2560]{1,0:T(8,128)(2,1)S(1)}, u32[]{:S(2)}, u32[]{:S(2)}) %collective-permute-start.4) | collective-permute-done | bytes 40992 | tf_op jit(solution)/shard_map/ppermute | solution.py:513
  36.3 0.8 collective-permute-start.7
  37.1 1.8 %collective-permute-start.6 = (bf16[8,2560]{1,0:T(8,128)(2,1)S(1)}, bf16[8,2560]{1,0:T(8,128)(2,1)S(1)}, u32[]{:S(2)}, u32[]{:S(2)}) collective-permute-start(bf16[8,2560]{1,0:T(8,128)(2,1)S(1)} %shard_map.89.block), channel_id=1, source_target_pairs={{0,96},{32,0},{64,32},{96,64},{16,48},{48,80},{80,112},{112,16},{1... | collective-permute-start | bytes 122888 | tf_op jit(solution)/shard_map/ppermute | solution.py:477
  38.9 2.3 %collective-permute-start.5 = (bf16[8,2560]{1,0:T(8,128)(2,1)S(1)}, bf16[8,2560]{1,0:T(8,128)(2,1)S(1)}, u32[]{:S(2)}, u32[]{:S(2)}) collective-permute-start(bf16[8,2560]{1,0:T(8,128)(2,1)S(1)} %shard_map.89.block), channel_id=1, source_target_pairs={{0,112},{32,16},{64,48},{96,80},{16,32},{48,64},{80,96},{112,0},{1... | collective-permute-start | bytes 122888 | tf_op jit(solution)/shard_map/ppermute | solution.py:477
  41.3 2.5 %collective-permute-done.7.opposite = bf16[8,2560]{1,0:T(8,128)(2,1)S(1)} collective-permute-done((bf16[8,2560]{1,0:T(8,128)(2,1)S(1)}, bf16[8,2560]{1,0:T(8,128)(2,1)S(1)}, u32[]{:S(2)}, u32[]{:S(2)}) %collective-permute-start.7) | collective-permute-done | bytes 40992 | tf_op jit(solution)/shard_map/ppermute | solution.py:477
  44.2 0.9 shard_map.90
  45.1 0.7 collective-permute-start.8
  45.8 2.5 %collective-permute-start.9 = (bf16[2,320,240]{2,1,0:T(8,128)(2,1)}, bf16[2,320,240]{2,1,0:T(8,128)(2,1)}, u32[]{:S(2)}, u32[]{:S(2)}) collective-permute-start(bf16[2,320,240]{2,1,0:T(8,128)(2,1)} %get-tuple-element.34.refs_2_), channel_id=1, source_target_pairs={{0,112},{16,0},{32,16},{48,32},{64,48},{80,64},{96,80},{112,96},{1... | collective-permute-start | bytes 921608 | tf_op jit(solution)/shard_map/ppermute | solution.py:517
  48.3 7.2 %all-to-all-start.1 = ((bf16[16,8,2560]{2,1,0:T(8,128)(2,1)}), bf16[16,8,2560]{2,1,0:T(8,128)(2,1)S(1)}, u32[]{:S(2)}, u32[]{:S(2)}) async-start(bf16[16,8,2560]{2,1,0:T(8,128)(2,1)} %get-tuple-element.32), calls=%async_computation.1 | async-start | bytes 1310720 | tf_op jit(solution)/shard_map/all_to_all | solution.py:548
  56.3 3.2 %collective-permute-start.11 = (bf16[2,320,240]{2,1,0:T(8,128)(2,1)}, bf16[2,320,240]{2,1,0:T(8,128)(2,1)}, u32[]{:S(2)}, u32[]{:S(2)}) collective-permute-start(bf16[2,320,240]{2,1,0:T(8,128)(2,1)} %get-tuple-element.36.refs_4_.refs_1_), channel_id=1, source_target_pairs={{0,112},{16,0},{32,16},{48,32},{64,48},{80,64},{96,80},{112,96},{1... | collective-permute-start | bytes 921608 | tf_op jit(solution)/shard_map/ppermute | solution.py:517
  59.5 2.0 %shard_map.92 = (bf16[240,5120]{1,0:T(8,128)(2,1)S(1)}, f32[8,128]{1,0:T(8,128)S(1)}) custom-call(s32[1]{0:T(128)} %bitcast.7.side_of.side, s32[1]{0:T(128)} %bitcast.8.depth, bf16[2,320,240]{2,1,0:T(8,128)(2,1)} %shard_map.87.refs_0_, bf16[2,320,240]{2,1,0:T(8,128)(2,1)} %get-tuple-element.33.refs_1_, bf16[2,320,240]{2,1,0:T(8,128)(2,1)} %get-tuple-element.34.refs_2_, ...), custom_call_target="tpu_custom_call" | custom-call | flops 1000000000 | bytes 1536000 | tf_op jit(solution)/shard_map/pallas_call | solution.py:412
  61.5 1.4 %copy-done = bf16[240,5120]{1,0:T(8,128)(2,1)} copy-done((bf16[240,5120]{1,0:T(8,128)(2,1)}, bf16[240,5120]{1,0:T(8,128)(2,1)S(1)}, u32[]{:S(2)}) %copy-start) | copy-done | bytes 2457624
  62.9 1.8 %collective-permute-done.10.refs_1_.refs_2_ = bf16[2,320,240]{2,1,0:T(8,128)(2,1)S(1)} collective-permute-done((bf16[2,320,240]{2,1,0:T(8,128)(2,1)}, bf16[2,320,240]{2,1,0:T(8,128)(2,1)S(1)}, u32[]{:S(2)}, u32[]{:S(2)}) %collective-permute-start.10) | collective-permute-done | bytes 307232 | tf_op jit(solution)/shard_map/ppermute | solution.py:517
  64.9 0.9 collective-permute-start.19
  67.6 4.0 %collective-permute-start.15 = (bf16[240,128]{1,0:T(8,128)(2,1)S(1)}, bf16[240,128]{1,0:T(8,128)(2,1)S(1)}, u32[]{:S(2)}, u32[]{:S(2)}) collective-permute-start(bf16[240,128]{1,0:T(8,128)(2,1)S(1)} %get-tuple-element.41.own), channel_id=1, source_target_pairs={{0,144},{16,128},{32,176},{48,160},{64,208},{80,192},{96,240},{112... | collective-permute-start | bytes 184328 | tf_op jit(solution)/shard_map/ppermute | solution.py:486
  72.7 3.5 %shard_map.96.rest_0_.inverse = f32[128,128]{1,0:T(8,128)S(1)} custom-call(f32[128,128]{1,0:T(8,128)S(1)} %get-tuple-element.40.gram_mat, bf16[128,2560]{1,0:T(8,128)(2,1)S(1)} %bitcast.15, bf16[128,2560]{1,0:T(8,128)(2,1)S(1)} %collective-permute-done.12.left.refs_1_.rest_2_.other, ...), custom_call_target="tpu_custom_call" | custom-call | flops 1000000000 | bytes 262144 | tf_op jit(solution)/shard_map/pallas_call | solution.py:282
  76.2 1.2 %collective-permute-done.14.across = bf16[240,128]{1,0:T(8,128)(2,1)S(1)} collective-permute-done((bf16[240,128]{1,0:T(8,128)(2,1)S(1)}, bf16[240,128]{1,0:T(8,128)(2,1)S(1)}, u32[]{:S(2)}, u32[]{:S(2)}) %collective-permute-start.14) | collective-permute-done | bytes 61472 | tf_op jit(solution)/shard_map/ppermute | solution.py:486
  77.5 4.9 %collective-permute-start.18 = (bf16[240,128]{1,0:T(8,128)(2,1)S(1)}, bf16[240,128]{1,0:T(8,128)(2,1)S(1)}, u32[]{:S(2)}, u32[]{:S(2)}) collective-permute-start(bf16[240,128]{1,0:T(8,128)(2,1)S(1)} %shard_map.97._.refs_6_.product), channel_id=1, source_target_pairs={{0,80},{32,112},{64,16},{96,48},{16,64},{48,96},{80,0},{112,32},{1... | collective-permute-start | bytes 184328 | tf_op jit(solution)/shard_map/ppermute | solution.py:477
  82.3 4.7 %collective-permute-start.17 = (bf16[240,128]{1,0:T(8,128)(2,1)S(1)}, bf16[240,128]{1,0:T(8,128)(2,1)S(1)}, u32[]{:S(2)}, u32[]{:S(2)}) collective-permute-start(bf16[240,128]{1,0:T(8,128)(2,1)S(1)} %shard_map.97._.refs_6_.product), channel_id=1, source_target_pairs={{0,96},{32,0},{64,32},{96,64},{16,48},{48,80},{80,112},{112,16},{1... | collective-permute-start | bytes 184328 | tf_op jit(solution)/shard_map/ppermute | solution.py:477
  87.1 2.1 %shard_map.99 = (bf16[240,5120]{1,0:T(8,128)(2,1)S(1)}, f32[8,128]{1,0:T(8,128)}) custom-call(s32[1]{0:T(128)} %bitcast.7.side_of.side, s32[1]{0:T(128)} %bitcast.8.depth, bf16[2,320,240]{2,1,0:T(8,128)(2,1)} %get-tuple-element.35.refs_3_.refs_0_, bf16[2,320,240]{2,1,0:T(8,128)(2,1)} %get-tuple-element.36.refs_4_.refs_1_, ...), custom_call_target="tpu_custom_call", output_to_operand_aliasing={{0}: (7, {})} | custom-call | flops 1000000000 | bytes 1536000 | tf_op jit(solution)/shard_map/pallas_call | solution.py:412
  89.2 1.0 %shard_map.98 = (bf16[128,5120]{1,0:T(8,128)(2,1)S(1)}, bf16[320,128]{1,0:T(8,128)(2,1)S(1)}) custom-call(s32[1]{0:T(128)} %bitcast.which, s32[1]{0:T(128)} %bitcast.7.side_of.side, s32[1]{0:T(128)} %bitcast.8.depth, f32[128,128]{1,0:T(8,128)S(1)} %shard_map.96.rest_0_.inverse, bf16[128,2560]{1,0:T(8,128)(2,1)S(1)} %bitcast.17, ...), custom_call_target="tpu_custom_call" | custom-call | flops 335544320 | bytes 2621440 | tf_op jit(solution)/shard_map/pallas_call | solution.py:314
  90.2 2.2 %collective-permute-done.16.before = bf16[240,128]{1,0:T(8,128)(2,1)S(1)} collective-permute-done((bf16[240,128]{1,0:T(8,128)(2,1)S(1)}, bf16[240,128]{1,0:T(8,128)(2,1)S(1)}, u32[]{:S(2)}, u32[]{:S(2)}) %collective-permute-start.16) | collective-permute-done | bytes 61472 | tf_op jit(solution)/shard_map/ppermute | solution.py:477
  92.5 3.3 %shard_map.100 = (bf16[240,5120]{1,0:T(8,128)(2,1)}, bf16[240,5120]{1,0:T(8,128)(2,1)}, f32[320,240]{1,0:T(8,128)}, f32[320,240]{1,0:T(8,128)}) custom-call(s32[1]{0:T(128)} %bitcast.which, f32[128,128]{1,0:T(8,128)S(1)} %shard_map.96.rest_0_.inverse, bf16[240,128]{1,0:T(8,128)(2,1)S(1)} %shard_map.97._.refs_6_.product, ...), custom_call_target="tpu_custom_call" | custom-call | flops 314572800 | bytes 9830400 | tf_op jit(solution)/shard_map/pallas_call | solution.py:359
  (43 shorter events, 4.5 us)
Async XLA Ops:
  3.0 5.6 %collective-permute-start = (bf16[128,2560]{1,0:T(8,128)(2,1)S(1)}, bf16[128,2560]{1,0:T(8,128)(2,1)S(1)}, u32[]{:S(2)}, u32[]{:S(2)}) collective-permute-start(bf16[128,2560]{1,0:T(8,128)(2,1)S(1)} %get-tuple-element.29), channel_id=1, source_target_pairs={{0,1},{1,0},{2,3},{3,2},{4,5},{5,4},{6,7},{7,6},{8,9},{9,8},{10,11... | collective-permute-start | bytes 1966088 | tf_op jit(solution)/shard_map/ppermute | solution.py:513
  3.1 11.9 %collective-permute-start.1 = (bf16[320,240]{1,0:T(8,128)(2,1)S(1)}, bf16[320,240]{1,0:T(8,128)(2,1)S(1)}, u32[]{:S(2)}, u32[]{:S(2)}) collective-permute-start(bf16[320,240]{1,0:T(8,128)(2,1)S(1)} %get-tuple-element.31.own), channel_id=1, source_target_pairs={{0,128},{128,0},{1,129},{129,1},{2,130},{130,2},{3,131},{131,3},{4... | collective-permute-start | bytes 460808 | tf_op jit(solution)/shard_map/ppermute | solution.py:513
  9.6 22.6 %all-to-all-start = ((bf16[16,8,2560]{2,1,0:T(8,128)(2,1)}), bf16[16,8,2560]{2,1,0:T(8,128)(2,1)S(1)}, u32[]{:S(2)}, u32[]{:S(2)}) async-start(bf16[16,8,2560]{2,1,0:T(8,128)(2,1)} %bitcast.6), calls=%async_computation | async-start | bytes 1310720 | tf_op jit(solution)/shard_map/all_to_all | solution.py:538
  15.8 12.9 %collective-permute-start.3 = (bf16[2,320,240]{2,1,0:T(8,128)(2,1)}, bf16[2,320,240]{2,1,0:T(8,128)(2,1)S(1)}, u32[]{:S(2)}, u32[]{:S(2)}) collective-permute-start(bf16[2,320,240]{2,1,0:T(8,128)(2,1)} %shard_map.87.refs_0_), channel_id=1, source_target_pairs={{0,112},{16,0},{32,16},{48,32},{64,48},{80,64},{96,80},{112,96},{1... | collective-permute-start | bytes 921608 | tf_op jit(solution)/shard_map/ppermute | solution.py:517
  21.7 10.5 %collective-permute-start.2 = (bf16[2,320,240]{2,1,0:T(8,128)(2,1)}, bf16[2,320,240]{2,1,0:T(8,128)(2,1)}, u32[]{:S(2)}, u32[]{:S(2)}) collective-permute-start(bf16[2,320,240]{2,1,0:T(8,128)(2,1)} %shard_map.87.refs_0_), channel_id=1, source_target_pairs={{0,16},{16,32},{32,48},{48,64},{64,80},{80,96},{96,112},{112,0},{1... | collective-permute-start | bytes 921608 | tf_op jit(solution)/shard_map/ppermute | solution.py:517
  28.7 3.4 %copy-start.5 = (bf16[2,320,240]{2,1,0:T(8,128)(2,1)}, bf16[2,320,240]{2,1,0:T(8,128)(2,1)S(1)}, u32[]{:S(2)}) copy-start(bf16[2,320,240]{2,1,0:T(8,128)(2,1)S(1)} %collective-permute-done.3.rest_1_) | copy-start | bytes 921604
  32.2 4.1 %collective-permute-start.4 = (bf16[8,2560]{1,0:T(8,128)(2,1)S(1)}, bf16[8,2560]{1,0:T(8,128)(2,1)S(1)}, u32[]{:S(2)}, u32[]{:S(2)}) collective-permute-start(bf16[8,2560]{1,0:T(8,128)(2,1)S(1)} %shard_map.88.first), channel_id=1, source_target_pairs={{0,16},{16,0},{32,48},{48,32},{64,80},{80,64},{96,112},{112,96},{1... | collective-permute-start | bytes 122888 | tf_op jit(solution)/shard_map/ppermute | solution.py:513
  36.3 7.4 %collective-permute-start.7 = (bf16[8,2560]{1,0:T(8,128)(2,1)S(1)}, bf16[8,2560]{1,0:T(8,128)(2,1)S(1)}, u32[]{:S(2)}, u32[]{:S(2)}) collective-permute-start(bf16[8,2560]{1,0:T(8,128)(2,1)S(1)} %shard_map.89.block), channel_id=1, source_target_pairs={{0,80},{32,112},{64,16},{96,48},{16,64},{48,96},{80,0},{112,32},{1... | collective-permute-start | bytes 122888 | tf_op jit(solution)/shard_map/ppermute | solution.py:477
  37.1 6.7 %collective-permute-start.6 = (bf16[8,2560]{1,0:T(8,128)(2,1)S(1)}, bf16[8,2560]{1,0:T(8,128)(2,1)S(1)}, u32[]{:S(2)}, u32[]{:S(2)}) collective-permute-start(bf16[8,2560]{1,0:T(8,128)(2,1)S(1)} %shard_map.89.block), channel_id=1, source_target_pairs={{0,96},{32,0},{64,32},{96,64},{16,48},{48,80},{80,112},{112,16},{1... | collective-permute-start | bytes 122888 | tf_op jit(solution)/shard_map/ppermute | solution.py:477
  38.9 5.3 %collective-permute-start.5 = (bf16[8,2560]{1,0:T(8,128)(2,1)S(1)}, bf16[8,2560]{1,0:T(8,128)(2,1)S(1)}, u32[]{:S(2)}, u32[]{:S(2)}) collective-permute-start(bf16[8,2560]{1,0:T(8,128)(2,1)S(1)} %shard_map.89.block), channel_id=1, source_target_pairs={{0,112},{32,16},{64,48},{96,80},{16,32},{48,64},{80,96},{112,0},{1... | collective-permute-start | bytes 122888 | tf_op jit(solution)/shard_map/ppermute | solution.py:477
  45.1 10.5 %collective-permute-start.8 = (bf16[2,320,240]{2,1,0:T(8,128)(2,1)}, bf16[2,320,240]{2,1,0:T(8,128)(2,1)S(1)}, u32[]{:S(2)}, u32[]{:S(2)}) collective-permute-start(bf16[2,320,240]{2,1,0:T(8,128)(2,1)} %get-tuple-element.33.refs_1_), channel_id=1, source_target_pairs={{0,16},{16,32},{32,48},{48,64},{64,80},{80,96},{96,112},{112,0},{1... | collective-permute-start | bytes 921608 | tf_op jit(solution)/shard_map/ppermute | solution.py:517
  45.8 9.7 %collective-permute-start.9 = (bf16[2,320,240]{2,1,0:T(8,128)(2,1)}, bf16[2,320,240]{2,1,0:T(8,128)(2,1)}, u32[]{:S(2)}, u32[]{:S(2)}) collective-permute-start(bf16[2,320,240]{2,1,0:T(8,128)(2,1)} %get-tuple-element.34.refs_2_), channel_id=1, source_target_pairs={{0,112},{16,0},{32,16},{48,32},{64,48},{80,64},{96,80},{112,96},{1... | collective-permute-start | bytes 921608 | tf_op jit(solution)/shard_map/ppermute | solution.py:517
  48.3 16.5 %all-to-all-start.1 = ((bf16[16,8,2560]{2,1,0:T(8,128)(2,1)}), bf16[16,8,2560]{2,1,0:T(8,128)(2,1)S(1)}, u32[]{:S(2)}, u32[]{:S(2)}) async-start(bf16[16,8,2560]{2,1,0:T(8,128)(2,1)} %get-tuple-element.32), calls=%async_computation.1 | async-start | bytes 1310720 | tf_op jit(solution)/shard_map/all_to_all | solution.py:548
  55.5 0.7 copy-start.6
  56.3 8.5 %collective-permute-start.10 = (bf16[2,320,240]{2,1,0:T(8,128)(2,1)}, bf16[2,320,240]{2,1,0:T(8,128)(2,1)S(1)}, u32[]{:S(2)}, u32[]{:S(2)}) collective-permute-start(bf16[2,320,240]{2,1,0:T(8,128)(2,1)} %get-tuple-element.35.refs_3_.refs_0_), channel_id=1, source_target_pairs={{0,16},{16,32},{32,48},{48,64},{64,80},{80,96},{96,112},{112,0},{1... | collective-permute-start | bytes 921608 | tf_op jit(solution)/shard_map/ppermute | solution.py:517
  56.3 8.5 %collective-permute-start.11 = (bf16[2,320,240]{2,1,0:T(8,128)(2,1)}, bf16[2,320,240]{2,1,0:T(8,128)(2,1)}, u32[]{:S(2)}, u32[]{:S(2)}) collective-permute-start(bf16[2,320,240]{2,1,0:T(8,128)(2,1)} %get-tuple-element.36.refs_4_.refs_1_), channel_id=1, source_target_pairs={{0,112},{16,0},{32,16},{48,32},{64,48},{80,64},{96,80},{112,96},{1... | collective-permute-start | bytes 921608 | tf_op jit(solution)/shard_map/ppermute | solution.py:517
  61.5 1.4 %copy-start = (bf16[240,5120]{1,0:T(8,128)(2,1)}, bf16[240,5120]{1,0:T(8,128)(2,1)S(1)}, u32[]{:S(2)}) copy-start(bf16[240,5120]{1,0:T(8,128)(2,1)S(1)} %get-tuple-element.43.refs_5_) | copy-start | bytes 7372804
  64.8 1.6 %copy-start.4 = (bf16[2,320,240]{2,1,0:T(8,128)(2,1)}, bf16[2,320,240]{2,1,0:T(8,128)(2,1)S(1)}, u32[]{:S(2)}) copy-start(bf16[2,320,240]{2,1,0:T(8,128)(2,1)S(1)} %collective-permute-done.10.refs_1_.refs_2_) | copy-start | bytes 921604
  64.8 2.2 %collective-permute-start.12 = (bf16[128,2560]{1,0:T(8,128)(2,1)S(1)}, bf16[128,2560]{1,0:T(8,128)(2,1)S(1)}, u32[]{:S(2)}, u32[]{:S(2)}) collective-permute-start(bf16[128,2560]{1,0:T(8,128)(2,1)S(1)} %bitcast.13), channel_id=1, source_target_pairs={{0,1},{1,0},{2,3},{3,2},{4,5},{5,4},{6,7},{7,6},{8,9},{9,8},{10,11... | collective-permute-start | bytes 1966088 | tf_op jit(solution)/shard_map/ppermute | solution.py:513
  64.9 22.1 %collective-permute-start.19 = (bf16[2,320,240]{2,1,0:T(8,128)(2,1)S(1)}, bf16[2,320,240]{2,1,0:T(8,128)(2,1)S(1)}, u32[]{:S(2)}, u32[]{:S(2)}) collective-permute-start(bf16[2,320,240]{2,1,0:T(8,128)(2,1)S(1)} %collective-permute-done.10.refs_1_.refs_2_), channel_id=1, source_target_pairs={{0,16},{16,32},{32,48},{48,64},{64,80},{80,96},{96,112},{112,0},{1... | collective-permute-start | bytes 921608 | tf_op jit(solution)/shard_map/ppermute | solution.py:517
  67.6 8.6 %collective-permute-start.15 = (bf16[240,128]{1,0:T(8,128)(2,1)S(1)}, bf16[240,128]{1,0:T(8,128)(2,1)S(1)}, u32[]{:S(2)}, u32[]{:S(2)}) collective-permute-start(bf16[240,128]{1,0:T(8,128)(2,1)S(1)} %get-tuple-element.41.own), channel_id=1, source_target_pairs={{0,144},{16,128},{32,176},{48,160},{64,208},{80,192},{96,240},{112... | collective-permute-start | bytes 184328 | tf_op jit(solution)/shard_map/ppermute | solution.py:486
  71.7 5.7 %collective-permute-start.14 = (bf16[240,128]{1,0:T(8,128)(2,1)S(1)}, bf16[240,128]{1,0:T(8,128)(2,1)S(1)}, u32[]{:S(2)}, u32[]{:S(2)}) collective-permute-start(bf16[240,128]{1,0:T(8,128)(2,1)S(1)} %get-tuple-element.41.own), channel_id=1, source_target_pairs={{0,128},{16,144},{32,160},{48,176},{64,192},{80,208},{96,224},{112... | collective-permute-start | bytes 184328 | tf_op jit(solution)/shard_map/ppermute | solution.py:486
  72.2 5.2 %collective-permute-start.13 = (bf16[240,128]{1,0:T(8,128)(2,1)S(1)}, bf16[240,128]{1,0:T(8,128)(2,1)S(1)}, u32[]{:S(2)}, u32[]{:S(2)}) collective-permute-start(bf16[240,128]{1,0:T(8,128)(2,1)S(1)} %get-tuple-element.41.own), channel_id=1, source_target_pairs={{0,16},{16,0},{32,48},{48,32},{64,80},{80,64},{96,112},{112,96},{1... | collective-permute-start | bytes 184328 | tf_op jit(solution)/shard_map/ppermute | solution.py:486
  76.2 10.8 %copy-start.1 = (bf16[240,5120]{1,0:T(8,128)(2,1)S(1)}, bf16[240,5120]{1,0:T(8,128)(2,1)}, u32[]{:S(2)}) copy-start(bf16[240,5120]{1,0:T(8,128)(2,1)} %copy-done) | copy-start | bytes 7372804
  77.5 12.7 %collective-permute-start.18 = (bf16[240,128]{1,0:T(8,128)(2,1)S(1)}, bf16[240,128]{1,0:T(8,128)(2,1)S(1)}, u32[]{:S(2)}, u32[]{:S(2)}) collective-permute-start(bf16[240,128]{1,0:T(8,128)(2,1)S(1)} %shard_map.97._.refs_6_.product), channel_id=1, source_target_pairs={{0,80},{32,112},{64,16},{96,48},{16,64},{48,96},{80,0},{112,32},{1... | collective-permute-start | bytes 184328 | tf_op jit(solution)/shard_map/ppermute | solution.py:477
  82.3 7.9 %collective-permute-start.17 = (bf16[240,128]{1,0:T(8,128)(2,1)S(1)}, bf16[240,128]{1,0:T(8,128)(2,1)S(1)}, u32[]{:S(2)}, u32[]{:S(2)}) collective-permute-start(bf16[240,128]{1,0:T(8,128)(2,1)S(1)} %shard_map.97._.refs_6_.product), channel_id=1, source_target_pairs={{0,96},{32,0},{64,32},{96,64},{16,48},{48,80},{80,112},{112,16},{1... | collective-permute-start | bytes 184328 | tf_op jit(solution)/shard_map/ppermute | solution.py:477
  87.0 5.4 %collective-permute-start.16 = (bf16[240,128]{1,0:T(8,128)(2,1)S(1)}, bf16[240,128]{1,0:T(8,128)(2,1)S(1)}, u32[]{:S(2)}, u32[]{:S(2)}) collective-permute-start(bf16[240,128]{1,0:T(8,128)(2,1)S(1)} %shard_map.97._.refs_6_.product), channel_id=1, source_target_pairs={{0,112},{32,16},{64,48},{96,80},{16,32},{48,64},{80,96},{112,0},{1... | collective-permute-start | bytes 184328 | tf_op jit(solution)/shard_map/ppermute | solution.py:477
  87.0 5.4 %copy-start.2 = (f32[240,320]{0,1:T(8,128)S(1)}, f32[240,320]{0,1:T(8,128)}, u32[]{:S(2)}) copy-start(f32[240,320]{0,1:T(8,128)} %param.8) | copy-start | bytes 921604
  87.1 5.4 %copy-start.3 = (f32[240,320]{0,1:T(8,128)S(1)}, f32[240,320]{0,1:T(8,128)}, u32[]{:S(2)}) copy-start(f32[240,320]{0,1:T(8,128)} %param.9) | copy-start | bytes 921604

commit v6 on v5

--- a/solution.py
+++ b/solution.py
@@ -210,7 +210,7 @@
         + [far((count,) + block.shape, jnp.bfloat16)],
         input_output_aliases={4 + place: place for place in range(len(held))},
         compiler_params=params(),
-        cost_estimate=cost(block.size, 2 * count * block.size),
+        cost_estimate=cost(10**11, 2 * count * block.size),
     )(*[to_near(array) for array in (block, *arrived)], *[to_far(array) for array in held])
     return outs[-1], outs[:-1]
 
@@ -513,10 +513,6 @@
     return lax.ppermute(values, axis, [(place, place ^ bit) for place in range(size)])
 
 
-def shift(values, by):
-    return lax.ppermute(values, "z", [(place, (place + by) % 8) for place in range(8)])
-
-
 def local(pseudo_grad, error_buffer, basis_prev, master_weights, outer_momentum):
     core = lax.axis_index("core").astype(jnp.int32)
     rank = basis_prev.shape[1]
@@ -537,8 +533,10 @@
     up, down = shift(bundle, 1), shift(bundle, -1)
     chunks = lax.all_to_all(mine.reshape(16, rank // 16, half), plane, 0, 0, tiled=True)
     block = sum_chunks(chunks, (up, down), merged)
-    block, _ = add_after(block, swap(block, "z", 8, 1), [to_near(array) for array in merged])
-    copies, (up, down) = spread(block, from_pairs(block), 16, (up, down))
+    block, (up, down) = add_after(
+        block, swap(block, "z", 8, 1), [to_near(array) for array in merged], (up, down)
+    )
+    copies, _ = spread(block, from_pairs(block), 16, ())
     pieces = [bundle, up, down]
     up, down = pass_through((shift(up, 1), shift(down, -1)))
     pieces += [up, down]
@@ -546,18 +544,18 @@
     up, down = shift(up, 1), shift(down, -1)
     far_side = shift(up, 1)
     mine = lax.all_to_all(copies, plane, 0, 0, tiled=True)
-    mine = pass_after(mine, (up, down, token, merged)).reshape(rank, half)
+    mine = pass_after(mine, (up, token, merged)).reshape(rank, half)
     other = swap(mine, "core", 2, 1)
 
     before, _ = product_of(merged_mine, mine)
     (product, gram_mat), _ = product_of(merged_other, other, before)
 
     inverse = inverse_factor(gram_mat, (mine, other, *merged))
-    product = add_quad(product, from_quad(product), (inverse, mine, other, *merged))
+    product = add_quad(product, from_quad(product), (inverse, mine, other, down, *merged))
     arrived = from_pairs(product)
     basis_bf, basis_block = basis_of(which_mine, side, depth, inverse, mine, other, master.shape[0], product)
     carried, _ = gather_pieces(
-        side, depth, [*map(to_far, (*pieces[3:], up, down)), to_near(far_side)], (-2, 2, -3, 3, -4), (begun, product)
+        side, depth, [*map(to_far, pieces[3:]), *all_near((up, down, far_side))], (-2, 2, -3, 3, -4), (begun, product)
     )
 
     error_next, weights_next, master_next, momentum_next = final(

time: 96.3 us -> 91.8 us (0.953)
  starting transfers between devices: 48.9 us -> 44.9 us
    ppermute x6, waiting for transfers between devices: 5.17 us -> 0.8 us  [send(): lax.ppermute(values, 'z', routes + [(place, (place + odd_by) % 8) for pla...]
    ppermute x7, waiting for transfers between devices: 12.3 us -> 15.1 us  [shift(): lax.ppermute(values, 'z', [(place, (place + by) % 8) for place in range(8)])]
    ppermute x6, starting transfers between devices: 14.5 us -> 12.2 us  [send(): lax.ppermute(values, 'z', routes + [(place, (place + odd_by) % 8) for pla...]
    ppermute x7, starting transfers between devices: 13.2 us -> 11.6 us  [shift(): lax.ppermute(values, 'z', [(place, (place + by) % 8) for place in range(8)])]
    ppermute x3, waiting for transfers between devices: 1.18 us -> 2.51 us  [send(): lax.ppermute(values, island, [(place, place ^ mask) for place in range(16)])]
    unnamed x14 -> x12, local copies, waits for them, and re-layouts: 2.17 us -> 2.16 us
  transfers between devices with their start and end apart: 22 -> 22, of which waited for: 9 -> 7; matrix products, arithmetic and copies ran while one was open for 0% -> 0% of each run, Pallas kernels for 15% -> 16%
where the time goes in v6:
time: 91.8 us; the launch traced here: 91 us
  starting transfers between devices  44.9 us (49%)
  waiting for transfers between devices  22.4 us (24%)
  Pallas kernels  20.5 us (22%)
  local copies, waits for them, and re-layouts  2.16 us (2%)
  between operations  0.99 us (1%)
    ppermute x7, waiting for transfers between devices, shift(): lax.ppermute(values, 'z', [(place, (place + by) % 8) for place in range(8)])  15.1 us
    ppermute x6, starting transfers between devices, send(): lax.ppermute(values, 'z', routes + [(place, (place + odd_by) % 8) for pla...  12.2 us
    ppermute x7, starting transfers between devices, shift(): lax.ppermute(values, 'z', [(place, (place + by) % 8) for place in range(8)])  11.6 us
    all_to_all x1, starting transfers between devices, local(): mine = lax.all_to_all(copies, plane, 0, 0, tiled=True)  7.23 us
    all_to_all x1, starting transfers between devices, local(): lax.all_to_all(mine.reshape(16, rank // 16, half), plane, 0, 0, tiled=True)  5.51 us
    ppermute x3, starting transfers between devices, send(): lax.ppermute(values, island, [(place, place ^ mask) for place in range(16)])  5.08 us
    pallas_call x2, Pallas kernels, project(): pl.pallas_call(functools.partial(project_kernel, pieces), in_specs=[scala...  4.73 us
    pallas_call x2, Pallas kernels, gather_pieces(): pl.pallas_call(functools.partial(gather_kernel, shifts), in_specs=[scalar...  4 us
  transfers between devices with their start and end apart: 22, of which 7 were waited for; matrix products, arithmetic and copies ran while one was open for 0% of the time, Pallas kernels for 16%

profile of v6, /device:TPU:8, one launch (start us, length us, event | category | flops | bytes accessed | tf_op | source)
XLA Modules:
  0.0 91.0 jit_solution(13646401519791799482)
XLA Ops:
  0.6 2.4 %shard_map.84 = (bf16[128,2560]{1,0:T(8,128)(2,1)S(1)}, bf16[240,2560]{1,0:T(8,128)(2,1)S(1)}, bf16[320,240]{1,0:T(8,128)(2,1)S(1)}) custom-call(s32[1]{0:T(128)} %bitcast.1.which, bf16[240,5120]{1,0:T(8,128)(2,1)} %bitcast.22, bf16[240,5120]{1,0:T(8,128)(2,1)} %bitcast.24, bf16[240,128]{1,0:T(8,128)(2,1)} %basis.3, f32[320,240]{1,0:T(8,128)} %bitcast.18, ...), custom_call_target="tpu_custom_call" | custom-call | flops 157286400 | bytes 2457600 | tf_op jit(solution)/shard_map/pallas_call | solution.py:132
  3.1 3.1 %collective-permute-start.1 = (bf16[320,240]{1,0:T(8,128)(2,1)S(1)}, bf16[320,240]{1,0:T(8,128)(2,1)S(1)}, u32[]{:S(2)}, u32[]{:S(2)}) collective-permute-start(bf16[320,240]{1,0:T(8,128)(2,1)S(1)} %get-tuple-element.31.own), channel_id=1, source_target_pairs={{0,128},{128,0},{1,129},{129,1},{2,130},{130,2},{3,131},{131,3},{4... | collective-permute-start | bytes 460808 | tf_op jit(solution)/shard_map/ppermute | solution.py:513
  6.2 2.3 %shard_map.85 = (f32[128,2560]{1,0:T(8,128)S(1)}, bf16[240,2560]{1,0:T(8,128)(2,1)S(1)}) custom-call(s32[1]{0:T(128)} %bitcast.which, bf16[240,5120]{1,0:T(8,128)(2,1)} %bitcast.23, bf16[240,5120]{1,0:T(8,128)(2,1)} %bitcast.25, bf16[240,128]{1,0:T(8,128)(2,1)} %basis.3, ...), custom_call_target="tpu_custom_call" | custom-call | flops 157286400 | bytes 2457600 | tf_op jit(solution)/shard_map/pallas_call | solution.py:132
  8.6 0.9 %shard_map.86 = bf16[128,2560]{1,0:T(8,128)(2,1)} custom-call(f32[128,2560]{1,0:T(8,128)S(1)} %get-tuple-element.28.kept, bf16[128,2560]{1,0:T(8,128)(2,1)S(1)} %collective-permute-done.received, bf16[240,2560]{1,0:T(8,128)(2,1)S(1)} %get-tuple-element.30.rest_0_.rest_2_.refs_3_.merged.refs_2_.rest_4_.merged_mine, ...), custom_call_target="tpu_custom_call" | custom-call | flops 327680 | bytes 2621440 | tf_op jit(solution)/shard_map/pallas_call | solution.py:148
  9.6 5.5 %all-to-all-start = ((bf16[16,8,2560]{2,1,0:T(8,128)(2,1)}), bf16[16,8,2560]{2,1,0:T(8,128)(2,1)S(1)}, u32[]{:S(2)}, u32[]{:S(2)}) async-start(bf16[16,8,2560]{2,1,0:T(8,128)(2,1)} %bitcast.6), calls=%async_computation | async-start | bytes 1310720 | tf_op jit(solution)/shard_map/all_to_all | solution.py:534
  15.1 0.7 shard_map.87.refs_0_
  15.8 5.9 %collective-permute-start.3 = (bf16[2,320,240]{2,1,0:T(8,128)(2,1)}, bf16[2,320,240]{2,1,0:T(8,128)(2,1)S(1)}, u32[]{:S(2)}, u32[]{:S(2)}) collective-permute-start(bf16[2,320,240]{2,1,0:T(8,128)(2,1)} %shard_map.87.refs_0_), channel_id=1, source_target_pairs={{0,112},{16,0},{32,16},{48,32},{64,48},{80,64},{96,80},{112,96},{1... | collective-permute-start | bytes 921608 | tf_op jit(solution)/shard_map/ppermute | solution.py:509
  21.7 7.0 %collective-permute-done.3.rest_1_.rest_3_ = bf16[2,320,240]{2,1,0:T(8,128)(2,1)S(1)} collective-permute-done((bf16[2,320,240]{2,1,0:T(8,128)(2,1)}, bf16[2,320,240]{2,1,0:T(8,128)(2,1)S(1)}, u32[]{:S(2)}, u32[]{:S(2)}) %collective-permute-start.3) | collective-permute-done | bytes 307232 | tf_op jit(solution)/shard_map/ppermute | solution.py:509
  28.7 3.4 %collective-permute-done.2.rest_0_.rest_2_ = bf16[2,320,240]{2,1,0:T(8,128)(2,1)} collective-permute-done((bf16[2,320,240]{2,1,0:T(8,128)(2,1)}, bf16[2,320,240]{2,1,0:T(8,128)(2,1)}, u32[]{:S(2)}, u32[]{:S(2)}) %collective-permute-start.2) | collective-permute-done | bytes 307232 | tf_op jit(solution)/shard_map/ppermute | solution.py:509
  32.3 4.0 %collective-permute-done.4.second = bf16[8,2560]{1,0:T(8,128)(2,1)S(1)} collective-permute-done((bf16[8,2560]{1,0:T(8,128)(2,1)S(1)}, bf16[8,2560]{1,0:T(8,128)(2,1)S(1)}, u32[]{:S(2)}, u32[]{:S(2)}) %collective-permute-start.4) | collective-permute-done | bytes 40992 | tf_op jit(solution)/shard_map/ppermute | solution.py:513
  36.3 0.8 collective-permute-start.7
  37.1 1.8 %collective-permute-start.6 = (bf16[8,2560]{1,0:T(8,128)(2,1)S(1)}, bf16[8,2560]{1,0:T(8,128)(2,1)S(1)}, u32[]{:S(2)}, u32[]{:S(2)}) collective-permute-start(bf16[8,2560]{1,0:T(8,128)(2,1)S(1)} %get-tuple-element.32.block), channel_id=1, source_target_pairs={{0,96},{32,0},{64,32},{96,64},{16,48},{48,80},{80,112},{112,16},{1... | collective-permute-start | bytes 122888 | tf_op jit(solution)/shard_map/ppermute | solution.py:477
  38.9 2.3 %collective-permute-start.5 = (bf16[8,2560]{1,0:T(8,128)(2,1)S(1)}, bf16[8,2560]{1,0:T(8,128)(2,1)S(1)}, u32[]{:S(2)}, u32[]{:S(2)}) collective-permute-start(bf16[8,2560]{1,0:T(8,128)(2,1)S(1)} %get-tuple-element.32.block), channel_id=1, source_target_pairs={{0,112},{32,16},{64,48},{96,80},{16,32},{48,64},{80,96},{112,0},{1... | collective-permute-start | bytes 122888 | tf_op jit(solution)/shard_map/ppermute | solution.py:477
  41.3 3.2 %collective-permute-start.9 = (bf16[2,320,240]{2,1,0:T(8,128)(2,1)}, bf16[2,320,240]{2,1,0:T(8,128)(2,1)}, u32[]{:S(2)}, u32[]{:S(2)}) collective-permute-start(bf16[2,320,240]{2,1,0:T(8,128)(2,1)} %get-tuple-element.34.refs_2_), channel_id=1, source_target_pairs={{0,112},{16,0},{32,16},{48,32},{64,48},{80,64},{96,80},{112,96},{1... | collective-permute-start | bytes 921608 | tf_op jit(solution)/shard_map/ppermute | solution.py:509
  45.0 0.9 shard_map.90
  45.9 7.2 %all-to-all-start.1 = ((bf16[16,8,2560]{2,1,0:T(8,128)(2,1)}), bf16[16,8,2560]{2,1,0:T(8,128)(2,1)S(1)}, u32[]{:S(2)}, u32[]{:S(2)}) async-start(bf16[16,8,2560]{2,1,0:T(8,128)(2,1)} %shard_map.90), calls=%async_computation.1 | async-start | bytes 1310720 | tf_op jit(solution)/shard_map/all_to_all | solution.py:546
  53.1 0.7 copy-done.5
  54.3 2.0 %shard_map.92 = (bf16[240,5120]{1,0:T(8,128)(2,1)S(1)}, f32[8,128]{1,0:T(8,128)S(1)}) custom-call(s32[1]{0:T(128)} %bitcast.7.side_of.side, s32[1]{0:T(128)} %bitcast.8.depth, bf16[2,320,240]{2,1,0:T(8,128)(2,1)} %shard_map.87.refs_0_, bf16[2,320,240]{2,1,0:T(8,128)(2,1)} %get-tuple-element.33.refs_1_, bf16[2,320,240]{2,1,0:T(8,128)(2,1)} %get-tuple-element.34.refs_2_, ...), custom_call_target="tpu_custom_call" | custom-call | flops 1000000000 | bytes 1536000 | tf_op jit(solution)/shard_map/pallas_call | solution.py:412
  56.3 1.4 %copy-done = bf16[240,5120]{1,0:T(8,128)(2,1)} copy-done((bf16[240,5120]{1,0:T(8,128)(2,1)}, bf16[240,5120]{1,0:T(8,128)(2,1)S(1)}, u32[]{:S(2)}) %copy-start) | copy-done | bytes 2457624
  57.7 4.6 %collective-permute-done.10.refs_1_.refs_2_ = bf16[2,320,240]{2,1,0:T(8,128)(2,1)S(1)} collective-permute-done((bf16[2,320,240]{2,1,0:T(8,128)(2,1)}, bf16[2,320,240]{2,1,0:T(8,128)(2,1)S(1)}, u32[]{:S(2)}, u32[]{:S(2)}) %collective-permute-start.10) | collective-permute-done | bytes 307232 | tf_op jit(solution)/shard_map/ppermute | solution.py:509
  62.3 1.5 %collective-permute-start.15 = (bf16[2,320,240]{2,1,0:T(8,128)(2,1)}, bf16[2,320,240]{2,1,0:T(8,128)(2,1)S(1)}, u32[]{:S(2)}, u32[]{:S(2)}) collective-permute-start(bf16[2,320,240]{2,1,0:T(8,128)(2,1)} %get-tuple-element.36.refs_4_.refs_1_), channel_id=1, source_target_pairs={{0,112},{16,0},{32,16},{48,32},{64,48},{80,64},{96,80},{112,96},{1... | collective-permute-start | bytes 921608 | tf_op jit(solution)/shard_map/ppermute | solution.py:509
  65.8 2.5 %collective-permute-start.14 = (bf16[240,128]{1,0:T(8,128)(2,1)S(1)}, bf16[240,128]{1,0:T(8,128)(2,1)S(1)}, u32[]{:S(2)}, u32[]{:S(2)}) collective-permute-start(bf16[240,128]{1,0:T(8,128)(2,1)S(1)} %get-tuple-element.41.own), channel_id=1, source_target_pairs={{0,144},{16,128},{32,176},{48,160},{64,208},{80,192},{96,240},{112... | collective-permute-start | bytes 184328 | tf_op jit(solution)/shard_map/ppermute | solution.py:486
  68.3 0.7 collective-permute-start.13
  68.9 1.9 %collective-permute-start.12 = (bf16[240,128]{1,0:T(8,128)(2,1)S(1)}, bf16[240,128]{1,0:T(8,128)(2,1)S(1)}, u32[]{:S(2)}, u32[]{:S(2)}) collective-permute-start(bf16[240,128]{1,0:T(8,128)(2,1)S(1)} %get-tuple-element.41.own), channel_id=1, source_target_pairs={{0,16},{16,0},{32,48},{48,32},{64,80},{80,64},{96,112},{112,96},{1... | collective-permute-start | bytes 184328 | tf_op jit(solution)/shard_map/ppermute | solution.py:486
  70.8 3.5 %shard_map.96.rest_0_.inverse = f32[128,128]{1,0:T(8,128)S(1)} custom-call(f32[128,128]{1,0:T(8,128)S(1)} %get-tuple-element.40.gram_mat, bf16[128,2560]{1,0:T(8,128)(2,1)S(1)} %bitcast.15, bf16[128,2560]{1,0:T(8,128)(2,1)S(1)} %collective-permute-done.11.left.refs_1_.rest_2_.other, ...), custom_call_target="tpu_custom_call" | custom-call | flops 1000000000 | bytes 262144 | tf_op jit(solution)/shard_map/pallas_call | solution.py:282
  74.4 2.5 %collective-permute-done.14.corner = bf16[240,128]{1,0:T(8,128)(2,1)S(1)} collective-permute-done((bf16[240,128]{1,0:T(8,128)(2,1)S(1)}, bf16[240,128]{1,0:T(8,128)(2,1)S(1)}, u32[]{:S(2)}, u32[]{:S(2)}) %collective-permute-start.14) | collective-permute-done | bytes 61472 | tf_op jit(solution)/shard_map/ppermute | solution.py:486
  76.9 4.3 %collective-permute-start.18 = (bf16[240,128]{1,0:T(8,128)(2,1)S(1)}, bf16[240,128]{1,0:T(8,128)(2,1)S(1)}, u32[]{:S(2)}, u32[]{:S(2)}) collective-permute-start(bf16[240,128]{1,0:T(8,128)(2,1)S(1)} %shard_map.97._.refs_6_.product), channel_id=1, source_target_pairs={{0,80},{32,112},{64,16},{96,48},{16,64},{48,96},{80,0},{112,32},{1... | collective-permute-start | bytes 184328 | tf_op jit(solution)/shard_map/ppermute | solution.py:477
  81.2 0.9 collective-permute-start.17
  82.1 2.1 %collective-permute-start.16 = (bf16[240,128]{1,0:T(8,128)(2,1)S(1)}, bf16[240,128]{1,0:T(8,128)(2,1)S(1)}, u32[]{:S(2)}, u32[]{:S(2)}) collective-permute-start(bf16[240,128]{1,0:T(8,128)(2,1)S(1)} %shard_map.97._.refs_6_.product), channel_id=1, source_target_pairs={{0,112},{32,16},{64,48},{96,80},{16,32},{48,64},{80,96},{112,0},{1... | collective-permute-start | bytes 184328 | tf_op jit(solution)/shard_map/ppermute | solution.py:477
  84.2 2.0 %shard_map.99 = (bf16[240,5120]{1,0:T(8,128)(2,1)S(1)}, f32[8,128]{1,0:T(8,128)}) custom-call(s32[1]{0:T(128)} %bitcast.7.side_of.side, s32[1]{0:T(128)} %bitcast.8.depth, bf16[2,320,240]{2,1,0:T(8,128)(2,1)} %get-tuple-element.35.refs_3_.refs_0_, bf16[2,320,240]{2,1,0:T(8,128)(2,1)} %get-tuple-element.36.refs_4_.refs_1_, ...), custom_call_target="tpu_custom_call", output_to_operand_aliasing={{0}: (7, {})} | custom-call | flops 1000000000 | bytes 1536000 | tf_op jit(solution)/shard_map/pallas_call | solution.py:412
  86.2 1.0 %shard_map.98 = (bf16[128,5120]{1,0:T(8,128)(2,1)S(1)}, bf16[320,128]{1,0:T(8,128)(2,1)S(1)}) custom-call(s32[1]{0:T(128)} %bitcast.which, s32[1]{0:T(128)} %bitcast.7.side_of.side, s32[1]{0:T(128)} %bitcast.8.depth, f32[128,128]{1,0:T(8,128)S(1)} %shard_map.96.rest_0_.inverse, bf16[128,2560]{1,0:T(8,128)(2,1)S(1)} %bitcast.17, ...), custom_call_target="tpu_custom_call" | custom-call | flops 335544320 | bytes 2621440 | tf_op jit(solution)/shard_map/pallas_call | solution.py:314
  87.5 3.3 %shard_map.100 = (bf16[240,5120]{1,0:T(8,128)(2,1)}, bf16[240,5120]{1,0:T(8,128)(2,1)}, f32[320,240]{1,0:T(8,128)}, f32[320,240]{1,0:T(8,128)}) custom-call(s32[1]{0:T(128)} %bitcast.which, f32[128,128]{1,0:T(8,128)S(1)} %shard_map.96.rest_0_.inverse, bf16[240,128]{1,0:T(8,128)(2,1)S(1)} %shard_map.97._.refs_6_.product, ...), custom_call_target="tpu_custom_call" | custom-call | flops 314572800 | bytes 9830400 | tf_op jit(solution)/shard_map/pallas_call | solution.py:359
  (41 shorter events, 3.5 us)
Async XLA Ops:
  3.0 5.6 %collective-permute-start = (bf16[128,2560]{1,0:T(8,128)(2,1)S(1)}, bf16[128,2560]{1,0:T(8,128)(2,1)S(1)}, u32[]{:S(2)}, u32[]{:S(2)}) collective-permute-start(bf16[128,2560]{1,0:T(8,128)(2,1)S(1)} %get-tuple-element.29), channel_id=1, source_target_pairs={{0,1},{1,0},{2,3},{3,2},{4,5},{5,4},{6,7},{7,6},{8,9},{9,8},{10,11... | collective-permute-start | bytes 1966088 | tf_op jit(solution)/shard_map/ppermute | solution.py:513
  3.1 11.9 %collective-permute-start.1 = (bf16[320,240]{1,0:T(8,128)(2,1)S(1)}, bf16[320,240]{1,0:T(8,128)(2,1)S(1)}, u32[]{:S(2)}, u32[]{:S(2)}) collective-permute-start(bf16[320,240]{1,0:T(8,128)(2,1)S(1)} %get-tuple-element.31.own), channel_id=1, source_target_pairs={{0,128},{128,0},{1,129},{129,1},{2,130},{130,2},{3,131},{131,3},{4... | collective-permute-start | bytes 460808 | tf_op jit(solution)/shard_map/ppermute | solution.py:513
  9.6 22.6 %all-to-all-start = ((bf16[16,8,2560]{2,1,0:T(8,128)(2,1)}), bf16[16,8,2560]{2,1,0:T(8,128)(2,1)S(1)}, u32[]{:S(2)}, u32[]{:S(2)}) async-start(bf16[16,8,2560]{2,1,0:T(8,128)(2,1)} %bitcast.6), calls=%async_computation | async-start | bytes 1310720 | tf_op jit(solution)/shard_map/all_to_all | solution.py:534
  15.8 12.9 %collective-permute-start.3 = (bf16[2,320,240]{2,1,0:T(8,128)(2,1)}, bf16[2,320,240]{2,1,0:T(8,128)(2,1)S(1)}, u32[]{:S(2)}, u32[]{:S(2)}) collective-permute-start(bf16[2,320,240]{2,1,0:T(8,128)(2,1)} %shard_map.87.refs_0_), channel_id=1, source_target_pairs={{0,112},{16,0},{32,16},{48,32},{64,48},{80,64},{96,80},{112,96},{1... | collective-permute-start | bytes 921608 | tf_op jit(solution)/shard_map/ppermute | solution.py:509
  21.7 10.5 %collective-permute-start.2 = (bf16[2,320,240]{2,1,0:T(8,128)(2,1)}, bf16[2,320,240]{2,1,0:T(8,128)(2,1)}, u32[]{:S(2)}, u32[]{:S(2)}) collective-permute-start(bf16[2,320,240]{2,1,0:T(8,128)(2,1)} %shard_map.87.refs_0_), channel_id=1, source_target_pairs={{0,16},{16,32},{32,48},{48,64},{64,80},{80,96},{96,112},{112,0},{1... | collective-permute-start | bytes 921608 | tf_op jit(solution)/shard_map/ppermute | solution.py:509
  28.7 3.4 %copy-start.4 = (bf16[2,320,240]{2,1,0:T(8,128)(2,1)}, bf16[2,320,240]{2,1,0:T(8,128)(2,1)S(1)}, u32[]{:S(2)}) copy-start(bf16[2,320,240]{2,1,0:T(8,128)(2,1)S(1)} %collective-permute-done.3.rest_1_.rest_3_) | copy-start | bytes 921604
  32.2 4.1 %collective-permute-start.4 = (bf16[8,2560]{1,0:T(8,128)(2,1)S(1)}, bf16[8,2560]{1,0:T(8,128)(2,1)S(1)}, u32[]{:S(2)}, u32[]{:S(2)}) collective-permute-start(bf16[8,2560]{1,0:T(8,128)(2,1)S(1)} %shard_map.88.first), channel_id=1, source_target_pairs={{0,16},{16,0},{32,48},{48,32},{64,80},{80,64},{96,112},{112,96},{1... | collective-permute-start | bytes 122888 | tf_op jit(solution)/shard_map/ppermute | solution.py:513
  36.3 8.2 %collective-permute-start.7 = (bf16[8,2560]{1,0:T(8,128)(2,1)S(1)}, bf16[8,2560]{1,0:T(8,128)(2,1)S(1)}, u32[]{:S(2)}, u32[]{:S(2)}) collective-permute-start(bf16[8,2560]{1,0:T(8,128)(2,1)S(1)} %get-tuple-element.32.block), channel_id=1, source_target_pairs={{0,80},{32,112},{64,16},{96,48},{16,64},{48,96},{80,0},{112,32},{1... | collective-permute-start | bytes 122888 | tf_op jit(solution)/shard_map/ppermute | solution.py:477
  37.1 7.4 %collective-permute-start.6 = (bf16[8,2560]{1,0:T(8,128)(2,1)S(1)}, bf16[8,2560]{1,0:T(8,128)(2,1)S(1)}, u32[]{:S(2)}, u32[]{:S(2)}) collective-permute-start(bf16[8,2560]{1,0:T(8,128)(2,1)S(1)} %get-tuple-element.32.block), channel_id=1, source_target_pairs={{0,96},{32,0},{64,32},{96,64},{16,48},{48,80},{80,112},{112,16},{1... | collective-permute-start | bytes 122888 | tf_op jit(solution)/shard_map/ppermute | solution.py:477
  38.9 6.1 %collective-permute-start.5 = (bf16[8,2560]{1,0:T(8,128)(2,1)S(1)}, bf16[8,2560]{1,0:T(8,128)(2,1)S(1)}, u32[]{:S(2)}, u32[]{:S(2)}) collective-permute-start(bf16[8,2560]{1,0:T(8,128)(2,1)S(1)} %get-tuple-element.32.block), channel_id=1, source_target_pairs={{0,112},{32,16},{64,48},{96,80},{16,32},{48,64},{80,96},{112,0},{1... | collective-permute-start | bytes 122888 | tf_op jit(solution)/shard_map/ppermute | solution.py:477
  41.3 11.8 %collective-permute-start.8 = (bf16[2,320,240]{2,1,0:T(8,128)(2,1)}, bf16[2,320,240]{2,1,0:T(8,128)(2,1)S(1)}, u32[]{:S(2)}, u32[]{:S(2)}) collective-permute-start(bf16[2,320,240]{2,1,0:T(8,128)(2,1)} %get-tuple-element.33.refs_1_), channel_id=1, source_target_pairs={{0,16},{16,32},{32,48},{48,64},{64,80},{80,96},{96,112},{112,0},{1... | collective-permute-start | bytes 921608 | tf_op jit(solution)/shard_map/ppermute | solution.py:509
  41.3 11.8 %collective-permute-start.9 = (bf16[2,320,240]{2,1,0:T(8,128)(2,1)}, bf16[2,320,240]{2,1,0:T(8,128)(2,1)}, u32[]{:S(2)}, u32[]{:S(2)}) collective-permute-start(bf16[2,320,240]{2,1,0:T(8,128)(2,1)} %get-tuple-element.34.refs_2_), channel_id=1, source_target_pairs={{0,112},{16,0},{32,16},{48,32},{64,48},{80,64},{96,80},{112,96},{1... | collective-permute-start | bytes 921608 | tf_op jit(solution)/shard_map/ppermute | solution.py:509
  45.9 16.5 %all-to-all-start.1 = ((bf16[16,8,2560]{2,1,0:T(8,128)(2,1)}), bf16[16,8,2560]{2,1,0:T(8,128)(2,1)S(1)}, u32[]{:S(2)}, u32[]{:S(2)}) async-start(bf16[16,8,2560]{2,1,0:T(8,128)(2,1)} %shard_map.90), calls=%async_computation.1 | async-start | bytes 1310720 | tf_op jit(solution)/shard_map/all_to_all | solution.py:546
  53.1 0.7 copy-start.5
  53.8 8.5 %collective-permute-start.10 = (bf16[2,320,240]{2,1,0:T(8,128)(2,1)}, bf16[2,320,240]{2,1,0:T(8,128)(2,1)S(1)}, u32[]{:S(2)}, u32[]{:S(2)}) collective-permute-start(bf16[2,320,240]{2,1,0:T(8,128)(2,1)} %get-tuple-element.35.refs_3_.refs_0_), channel_id=1, source_target_pairs={{0,16},{16,32},{32,48},{48,64},{64,80},{80,96},{96,112},{112,0},{1... | collective-permute-start | bytes 921608 | tf_op jit(solution)/shard_map/ppermute | solution.py:509
  56.3 1.4 %copy-start = (bf16[240,5120]{1,0:T(8,128)(2,1)}, bf16[240,5120]{1,0:T(8,128)(2,1)S(1)}, u32[]{:S(2)}) copy-start(bf16[240,5120]{1,0:T(8,128)(2,1)S(1)} %get-tuple-element.43.refs_5_) | copy-start | bytes 7372804
  62.3 2.8 %collective-permute-start.11 = (bf16[128,2560]{1,0:T(8,128)(2,1)S(1)}, bf16[128,2560]{1,0:T(8,128)(2,1)S(1)}, u32[]{:S(2)}, u32[]{:S(2)}) collective-permute-start(bf16[128,2560]{1,0:T(8,128)(2,1)S(1)} %bitcast.13), channel_id=1, source_target_pairs={{0,1},{1,0},{2,3},{3,2},{4,5},{5,4},{6,7},{7,6},{8,9},{9,8},{10,11... | collective-permute-start | bytes 1966088 | tf_op jit(solution)/shard_map/ppermute | solution.py:513
  62.3 12.0 %collective-permute-start.15 = (bf16[2,320,240]{2,1,0:T(8,128)(2,1)}, bf16[2,320,240]{2,1,0:T(8,128)(2,1)S(1)}, u32[]{:S(2)}, u32[]{:S(2)}) collective-permute-start(bf16[2,320,240]{2,1,0:T(8,128)(2,1)} %get-tuple-element.36.refs_4_.refs_1_), channel_id=1, source_target_pairs={{0,112},{16,0},{32,16},{48,32},{64,48},{80,64},{96,80},{112,96},{1... | collective-permute-start | bytes 921608 | tf_op jit(solution)/shard_map/ppermute | solution.py:509
  63.9 20.3 %collective-permute-start.19 = (bf16[2,320,240]{2,1,0:T(8,128)(2,1)S(1)}, bf16[2,320,240]{2,1,0:T(8,128)(2,1)S(1)}, u32[]{:S(2)}, u32[]{:S(2)}) collective-permute-start(bf16[2,320,240]{2,1,0:T(8,128)(2,1)S(1)} %collective-permute-done.10.refs_1_.refs_2_), channel_id=1, source_target_pairs={{0,16},{16,32},{32,48},{48,64},{64,80},{80,96},{96,112},{112,0},{1... | collective-permute-start | bytes 921608 | tf_op jit(solution)/shard_map/ppermute | solution.py:509
  65.8 11.1 %collective-permute-start.14 = (bf16[240,128]{1,0:T(8,128)(2,1)S(1)}, bf16[240,128]{1,0:T(8,128)(2,1)S(1)}, u32[]{:S(2)}, u32[]{:S(2)}) collective-permute-start(bf16[240,128]{1,0:T(8,128)(2,1)S(1)} %get-tuple-element.41.own), channel_id=1, source_target_pairs={{0,144},{16,128},{32,176},{48,160},{64,208},{80,192},{96,240},{112... | collective-permute-start | bytes 184328 | tf_op jit(solution)/shard_map/ppermute | solution.py:486
  68.3 8.6 %collective-permute-start.13 = (bf16[240,128]{1,0:T(8,128)(2,1)S(1)}, bf16[240,128]{1,0:T(8,128)(2,1)S(1)}, u32[]{:S(2)}, u32[]{:S(2)}) collective-permute-start(bf16[240,128]{1,0:T(8,128)(2,1)S(1)} %get-tuple-element.41.own), channel_id=1, source_target_pairs={{0,128},{16,144},{32,160},{48,176},{64,192},{80,208},{96,224},{112... | collective-permute-start | bytes 184328 | tf_op jit(solution)/shard_map/ppermute | solution.py:486
  68.9 8.0 %collective-permute-start.12 = (bf16[240,128]{1,0:T(8,128)(2,1)S(1)}, bf16[240,128]{1,0:T(8,128)(2,1)S(1)}, u32[]{:S(2)}, u32[]{:S(2)}) collective-permute-start(bf16[240,128]{1,0:T(8,128)(2,1)S(1)} %get-tuple-element.41.own), channel_id=1, source_target_pairs={{0,16},{16,0},{32,48},{48,32},{64,80},{80,64},{96,112},{112,96},{1... | collective-permute-start | bytes 184328 | tf_op jit(solution)/shard_map/ppermute | solution.py:486
  74.3 9.8 %copy-start.1 = (bf16[240,5120]{1,0:T(8,128)(2,1)S(1)}, bf16[240,5120]{1,0:T(8,128)(2,1)}, u32[]{:S(2)}) copy-start(bf16[240,5120]{1,0:T(8,128)(2,1)} %copy-done) | copy-start | bytes 7372804
  76.9 10.3 %collective-permute-start.18 = (bf16[240,128]{1,0:T(8,128)(2,1)S(1)}, bf16[240,128]{1,0:T(8,128)(2,1)S(1)}, u32[]{:S(2)}, u32[]{:S(2)}) collective-permute-start(bf16[240,128]{1,0:T(8,128)(2,1)S(1)} %shard_map.97._.refs_6_.product), channel_id=1, source_target_pairs={{0,80},{32,112},{64,16},{96,48},{16,64},{48,96},{80,0},{112,32},{1... | collective-permute-start | bytes 184328 | tf_op jit(solution)/shard_map/ppermute | solution.py:477
  81.2 6.0 %collective-permute-start.17 = (bf16[240,128]{1,0:T(8,128)(2,1)S(1)}, bf16[240,128]{1,0:T(8,128)(2,1)S(1)}, u32[]{:S(2)}, u32[]{:S(2)}) collective-permute-start(bf16[240,128]{1,0:T(8,128)(2,1)S(1)} %shard_map.97._.refs_6_.product), channel_id=1, source_target_pairs={{0,96},{32,0},{64,32},{96,64},{16,48},{48,80},{80,112},{112,16},{1... | collective-permute-start | bytes 184328 | tf_op jit(solution)/shard_map/ppermute | solution.py:477
  82.1 5.4 %collective-permute-start.16 = (bf16[240,128]{1,0:T(8,128)(2,1)S(1)}, bf16[240,128]{1,0:T(8,128)(2,1)S(1)}, u32[]{:S(2)}, u32[]{:S(2)}) collective-permute-start(bf16[240,128]{1,0:T(8,128)(2,1)S(1)} %shard_map.97._.refs_6_.product), channel_id=1, source_target_pairs={{0,112},{32,16},{64,48},{96,80},{16,32},{48,64},{80,96},{112,0},{1... | collective-permute-start | bytes 184328 | tf_op jit(solution)/shard_map/ppermute | solution.py:477
  84.2 3.4 %copy-start.2 = (f32[240,320]{0,1:T(8,128)S(1)}, f32[240,320]{0,1:T(8,128)}, u32[]{:S(2)}) copy-start(f32[240,320]{0,1:T(8,128)} %param.8) | copy-start | bytes 921604
  84.2 3.4 %copy-start.3 = (f32[240,320]{0,1:T(8,128)S(1)}, f32[240,320]{0,1:T(8,128)}, u32[]{:S(2)}) copy-start(f32[240,320]{0,1:T(8,128)} %param.9) | copy-start | bytes 921604

commit v7 on v6

--- a/solution.py
+++ b/solution.py
@@ -215,41 +215,33 @@
     return outs[-1], outs[:-1]
 
 
-def product_kernel(first, merged, left, *rest):
-    values = left[...]
-    product = times(merged[...], values, 1, 1)
-    gram_mat = times(values, values, 1, 1)
-    product_out, gram_out = rest[-2:]
-    if not first:
+def product_kernel(merged, left, *rest):
+    product = times(merged[...], left[...], 1, 1)
+    if len(rest) == 2:
         product = rest[0][...] + product
-        gram_mat = rest[1][...] + gram_mat
-    product_out[...] = product.astype(product_out.dtype)
-    gram_out[...] = gram_mat
-
-
-def product_of(merged, left, before=(), held=()):
+    rest[-1][...] = product.astype(rest[-1].dtype)
+
+
+def product_of(merged, left, before=()):
     rows = merged.shape[0]
     rank = left.shape[0]
-    outs = pl.pallas_call(
-        functools.partial(product_kernel, not before),
-        in_specs=[whole] * (2 + len(before)) + [anywhere] * len(held),
-        out_specs=[anywhere] * len(held) + [whole] * 2,
-        out_shape=[far(array.shape, array.dtype) for array in held]
-        + [near((rows, rank), jnp.bfloat16 if before else jnp.float32), near((rank, rank), jnp.float32)],
-        input_output_aliases={2 + len(before) + place: place for place in range(len(held))},
+    return pl.pallas_call(
+        product_kernel,
+        in_specs=[whole] * (2 + len(before)),
+        out_specs=whole,
+        out_shape=near((rows, rank), jnp.bfloat16 if before else jnp.float32),
         compiler_params=params(),
         cost_estimate=cost(2 * rows * left.size, 4 * left.size),
-    )(to_near(merged), to_near(left), *[to_near(array) for array in before], *[to_far(array) for array in held])
-    return outs[-2:], outs[:-2]
-
-
-def factor_kernel(gram_mat, *refs):
+    )(*all_near((merged, left, *before)))
+
+
+def factor_kernel(mine, other, *refs):
     inverse_out, state, below_all = refs[-3:]
-    rank = gram_mat.shape[0]
+    rank = mine.shape[0]
     exact = lax.Precision.HIGHEST
     row_of = lax.broadcasted_iota(jnp.int32, (rank, rank), 0)
     col_of = lax.broadcasted_iota(jnp.int32, (rank, rank), 1)
-    state[...] = gram_mat[...]
+    state[...] = times(mine[...], mine[...], 1, 1) + times(other[...], other[...], 1, 1)
     below_all[...] = jnp.where(row_of == col_of, 1.0, 0.0)
     row_of, col_of = row_of[:panel], col_of[:panel]
     for start in range(0, rank, panel):
@@ -277,17 +269,17 @@
             below_all[stop:, :] -= times(later, below, precision=exact)
 
 
-def inverse_factor(gram_mat, kept):
-    rank = gram_mat.shape[0]
+def inverse_factor(mine, other, kept):
+    rank = mine.shape[0]
     return pl.pallas_call(
         factor_kernel,
-        in_specs=[whole] + [anywhere] * len(kept),
+        in_specs=[whole] * 2 + [anywhere] * len(kept),
         out_specs=whole,
         out_shape=near((rank, rank), jnp.float32),
         scratch_shapes=[pltpu.VMEM((rank, rank), jnp.float32)] * 2,
         compiler_params=params(),
         cost_estimate=cost(10**9, 4 * rank * rank * 4),
-    )(to_near(gram_mat), *[to_near(array) for array in kept])
+    )(*all_near((mine, other, *kept)))
 
 
 def basis_kernel(which, side, depth, inverse, mine, other, _, out, block_out, held):
@@ -547,10 +539,10 @@
     mine = pass_after(mine, (up, token, merged)).reshape(rank, half)
     other = swap(mine, "core", 2, 1)
 
-    before, _ = product_of(merged_mine, mine)
-    (product, gram_mat), _ = product_of(merged_other, other, before)
-
-    inverse = inverse_factor(gram_mat, (mine, other, *merged))
+    product = product_of(merged_mine, mine)
+    product = product_of(merged_other, other, (product,))
+
+    inverse = inverse_factor(mine, other, merged)
     product = add_quad(product, from_quad(product), (inverse, mine, other, down, *merged))
     arrived = from_pairs(product)
     basis_bf, basis_block = basis_of(which_mine, side, depth, inverse, mine, other, master.shape[0], product)

time: 91.8 us -> 91.9 us (level)
  no operation moved by 1% of the time
where the time goes in v7:
time: 91.9 us; the launch traced here: 91 us
  starting transfers between devices  44.9 us (49%)
  waiting for transfers between devices  22.1 us (24%)
  Pallas kernels  20.8 us (23%)
  local copies, waits for them, and re-layouts  2.15 us (2%)
  between operations  0.98 us (1%)
    ppermute x7, waiting for transfers between devices, shift(): lax.ppermute(values, 'z', [(place, (place + by) % 8) for place in range(8)])  15.1 us
    ppermute x6, starting transfers between devices, send(): lax.ppermute(values, 'z', routes + [(place, (place + odd_by) % 8) for pla...  12.2 us
    ppermute x7, starting transfers between devices, shift(): lax.ppermute(values, 'z', [(place, (place + by) % 8) for place in range(8)])  11.6 us
    all_to_all x1, starting transfers between devices, local(): mine = lax.all_to_all(copies, plane, 0, 0, tiled=True)  7.23 us
    all_to_all x1, starting transfers between devices, local(): lax.all_to_all(mine.reshape(16, rank // 16, half), plane, 0, 0, tiled=True)  5.51 us
    ppermute x3, starting transfers between devices, send(): lax.ppermute(values, island, [(place, place ^ mask) for place in range(16)])  5.08 us
    pallas_call x2, Pallas kernels, project(): pl.pallas_call(functools.partial(project_kernel, pieces), in_specs=[scala...  4.73 us
    pallas_call x1, Pallas kernels, inverse_factor(): pl.pallas_call(factor_kernel, in_specs=[whole] * 2 + [anywhere] * len(kep...  4.12 us
  transfers between devices with their start and end apart: 22, of which 7 were waited for; matrix products, arithmetic and copies ran while one was open for 0% of the time, Pallas kernels for 16%

profile of v7, /device:TPU:8, one launch (start us, length us, event | category | flops | bytes accessed | tf_op | source)
XLA Modules:
  0.0 91.0 jit_solution(432632201522516780)
XLA Ops:
  0.6 2.4 %shard_map.84 = (bf16[128,2560]{1,0:T(8,128)(2,1)S(1)}, bf16[240,2560]{1,0:T(8,128)(2,1)S(1)}, bf16[320,240]{1,0:T(8,128)(2,1)S(1)}) custom-call(s32[1]{0:T(128)} %bitcast.3.which, bf16[240,5120]{1,0:T(8,128)(2,1)} %bitcast.22, bf16[240,5120]{1,0:T(8,128)(2,1)} %bitcast.24, bf16[240,128]{1,0:T(8,128)(2,1)} %basis.3, f32[320,240]{1,0:T(8,128)} %bitcast.18, ...), custom_call_target="tpu_custom_call" | custom-call | flops 157286400 | bytes 2457600 | tf_op jit(solution)/shard_map/pallas_call | solution.py:132
  3.1 3.1 %collective-permute-start.1 = (bf16[320,240]{1,0:T(8,128)(2,1)S(1)}, bf16[320,240]{1,0:T(8,128)(2,1)S(1)}, u32[]{:S(2)}, u32[]{:S(2)}) collective-permute-start(bf16[320,240]{1,0:T(8,128)(2,1)S(1)} %get-tuple-element.27.own), channel_id=1, source_target_pairs={{0,128},{128,0},{1,129},{129,1},{2,130},{130,2},{3,131},{131,3},{4... | collective-permute-start | bytes 460808 | tf_op jit(solution)/shard_map/ppermute | solution.py:505
  6.2 2.3 %shard_map.85 = (f32[128,2560]{1,0:T(8,128)S(1)}, bf16[240,2560]{1,0:T(8,128)(2,1)S(1)}) custom-call(s32[1]{0:T(128)} %bitcast.which, bf16[240,5120]{1,0:T(8,128)(2,1)} %bitcast.23, bf16[240,5120]{1,0:T(8,128)(2,1)} %bitcast.25, bf16[240,128]{1,0:T(8,128)(2,1)} %basis.3, ...), custom_call_target="tpu_custom_call" | custom-call | flops 157286400 | bytes 2457600 | tf_op jit(solution)/shard_map/pallas_call | solution.py:132
  8.6 0.9 %shard_map.86 = bf16[128,2560]{1,0:T(8,128)(2,1)} custom-call(f32[128,2560]{1,0:T(8,128)S(1)} %get-tuple-element.24.kept, bf16[128,2560]{1,0:T(8,128)(2,1)S(1)} %collective-permute-done.received, bf16[240,2560]{1,0:T(8,128)(2,1)S(1)} %get-tuple-element.26.rest_0_.rest_2_.refs_3_.refs_0_.merged.rest_4_.merged_mine, ...), custom_call_target="tpu_custom_call" | custom-call | flops 327680 | bytes 2621440 | tf_op jit(solution)/shard_map/pallas_call | solution.py:148
  9.6 5.5 %all-to-all-start = ((bf16[16,8,2560]{2,1,0:T(8,128)(2,1)}), bf16[16,8,2560]{2,1,0:T(8,128)(2,1)S(1)}, u32[]{:S(2)}, u32[]{:S(2)}) async-start(bf16[16,8,2560]{2,1,0:T(8,128)(2,1)} %bitcast.6), calls=%async_computation | async-start | bytes 1310720 | tf_op jit(solution)/shard_map/all_to_all | solution.py:526
  15.1 0.7 shard_map.87.refs_0_
  15.8 5.9 %collective-permute-start.3 = (bf16[2,320,240]{2,1,0:T(8,128)(2,1)}, bf16[2,320,240]{2,1,0:T(8,128)(2,1)S(1)}, u32[]{:S(2)}, u32[]{:S(2)}) collective-permute-start(bf16[2,320,240]{2,1,0:T(8,128)(2,1)} %shard_map.87.refs_0_), channel_id=1, source_target_pairs={{0,112},{16,0},{32,16},{48,32},{64,48},{80,64},{96,80},{112,96},{1... | collective-permute-start | bytes 921608 | tf_op jit(solution)/shard_map/ppermute | solution.py:501
  21.7 7.0 %collective-permute-done.3.rest_1_.rest_3_ = bf16[2,320,240]{2,1,0:T(8,128)(2,1)S(1)} collective-permute-done((bf16[2,320,240]{2,1,0:T(8,128)(2,1)}, bf16[2,320,240]{2,1,0:T(8,128)(2,1)S(1)}, u32[]{:S(2)}, u32[]{:S(2)}) %collective-permute-start.3) | collective-permute-done | bytes 307232 | tf_op jit(solution)/shard_map/ppermute | solution.py:501
  28.7 3.4 %collective-permute-done.2.rest_0_.rest_2_ = bf16[2,320,240]{2,1,0:T(8,128)(2,1)} collective-permute-done((bf16[2,320,240]{2,1,0:T(8,128)(2,1)}, bf16[2,320,240]{2,1,0:T(8,128)(2,1)}, u32[]{:S(2)}, u32[]{:S(2)}) %collective-permute-start.2) | collective-permute-done | bytes 307232 | tf_op jit(solution)/shard_map/ppermute | solution.py:501
  32.3 4.0 %collective-permute-done.4.second = bf16[8,2560]{1,0:T(8,128)(2,1)S(1)} collective-permute-done((bf16[8,2560]{1,0:T(8,128)(2,1)S(1)}, bf16[8,2560]{1,0:T(8,128)(2,1)S(1)}, u32[]{:S(2)}, u32[]{:S(2)}) %collective-permute-start.4) | collective-permute-done | bytes 40992 | tf_op jit(solution)/shard_map/ppermute | solution.py:505
  36.3 0.8 collective-permute-start.7
  37.1 1.8 %collective-permute-start.6 = (bf16[8,2560]{1,0:T(8,128)(2,1)S(1)}, bf16[8,2560]{1,0:T(8,128)(2,1)S(1)}, u32[]{:S(2)}, u32[]{:S(2)}) collective-permute-start(bf16[8,2560]{1,0:T(8,128)(2,1)S(1)} %get-tuple-element.28.block), channel_id=1, source_target_pairs={{0,96},{32,0},{64,32},{96,64},{16,48},{48,80},{80,112},{112,16},{1... | collective-permute-start | bytes 122888 | tf_op jit(solution)/shard_map/ppermute | solution.py:469
  38.9 2.3 %collective-permute-start.5 = (bf16[8,2560]{1,0:T(8,128)(2,1)S(1)}, bf16[8,2560]{1,0:T(8,128)(2,1)S(1)}, u32[]{:S(2)}, u32[]{:S(2)}) collective-permute-start(bf16[8,2560]{1,0:T(8,128)(2,1)S(1)} %get-tuple-element.28.block), channel_id=1, source_target_pairs={{0,112},{32,16},{64,48},{96,80},{16,32},{48,64},{80,96},{112,0},{1... | collective-permute-start | bytes 122888 | tf_op jit(solution)/shard_map/ppermute | solution.py:469
  41.3 3.2 %collective-permute-start.9 = (bf16[2,320,240]{2,1,0:T(8,128)(2,1)}, bf16[2,320,240]{2,1,0:T(8,128)(2,1)}, u32[]{:S(2)}, u32[]{:S(2)}) collective-permute-start(bf16[2,320,240]{2,1,0:T(8,128)(2,1)} %get-tuple-element.30.refs_2_), channel_id=1, source_target_pairs={{0,112},{16,0},{32,16},{48,32},{64,48},{80,64},{96,80},{112,96},{1... | collective-permute-start | bytes 921608 | tf_op jit(solution)/shard_map/ppermute | solution.py:501
  45.0 0.9 shard_map.90
  45.9 7.2 %all-to-all-start.1 = ((bf16[16,8,2560]{2,1,0:T(8,128)(2,1)}), bf16[16,8,2560]{2,1,0:T(8,128)(2,1)S(1)}, u32[]{:S(2)}, u32[]{:S(2)}) async-start(bf16[16,8,2560]{2,1,0:T(8,128)(2,1)} %shard_map.90), calls=%async_computation.1 | async-start | bytes 1310720 | tf_op jit(solution)/shard_map/all_to_all | solution.py:538
  53.1 0.7 copy-done.5
  54.3 2.0 %shard_map.92 = (bf16[240,5120]{1,0:T(8,128)(2,1)S(1)}, f32[8,128]{1,0:T(8,128)S(1)}) custom-call(s32[1]{0:T(128)} %bitcast.7.side_of.side, s32[1]{0:T(128)} %bitcast.8.depth, bf16[2,320,240]{2,1,0:T(8,128)(2,1)} %shard_map.87.refs_0_, bf16[2,320,240]{2,1,0:T(8,128)(2,1)} %get-tuple-element.29.refs_1_, bf16[2,320,240]{2,1,0:T(8,128)(2,1)} %get-tuple-element.30.refs_2_, ...), custom_call_target="tpu_custom_call" | custom-call | flops 1000000000 | bytes 1536000 | tf_op jit(solution)/shard_map/pallas_call | solution.py:404
  56.3 1.4 %copy-done = bf16[240,5120]{1,0:T(8,128)(2,1)} copy-done((bf16[240,5120]{1,0:T(8,128)(2,1)}, bf16[240,5120]{1,0:T(8,128)(2,1)S(1)}, u32[]{:S(2)}) %copy-start) | copy-done | bytes 2457624
  57.7 4.6 %collective-permute-done.10.refs_1_.refs_2_ = bf16[2,320,240]{2,1,0:T(8,128)(2,1)S(1)} collective-permute-done((bf16[2,320,240]{2,1,0:T(8,128)(2,1)}, bf16[2,320,240]{2,1,0:T(8,128)(2,1)S(1)}, u32[]{:S(2)}, u32[]{:S(2)}) %collective-permute-start.10) | collective-permute-done | bytes 307232 | tf_op jit(solution)/shard_map/ppermute | solution.py:501
  62.3 1.5 %collective-permute-start.15 = (bf16[2,320,240]{2,1,0:T(8,128)(2,1)}, bf16[2,320,240]{2,1,0:T(8,128)(2,1)S(1)}, u32[]{:S(2)}, u32[]{:S(2)}) collective-permute-start(bf16[2,320,240]{2,1,0:T(8,128)(2,1)} %get-tuple-element.32.refs_4_.refs_1_), channel_id=1, source_target_pairs={{0,112},{16,0},{32,16},{48,32},{64,48},{80,64},{96,80},{112,96},{1... | collective-permute-start | bytes 921608 | tf_op jit(solution)/shard_map/ppermute | solution.py:501
  65.4 2.5 %collective-permute-start.14 = (bf16[240,128]{1,0:T(8,128)(2,1)S(1)}, bf16[240,128]{1,0:T(8,128)(2,1)S(1)}, u32[]{:S(2)}, u32[]{:S(2)}) collective-permute-start(bf16[240,128]{1,0:T(8,128)(2,1)S(1)} %shard_map.96.own), channel_id=1, source_target_pairs={{0,144},{16,128},{32,176},{48,160},{64,208},{80,192},{96,240},{112... | collective-permute-start | bytes 184328 | tf_op jit(solution)/shard_map/ppermute | solution.py:478
  67.9 0.7 collective-permute-start.13
  68.6 1.9 %collective-permute-start.12 = (bf16[240,128]{1,0:T(8,128)(2,1)S(1)}, bf16[240,128]{1,0:T(8,128)(2,1)S(1)}, u32[]{:S(2)}, u32[]{:S(2)}) collective-permute-start(bf16[240,128]{1,0:T(8,128)(2,1)S(1)} %shard_map.96.own), channel_id=1, source_target_pairs={{0,16},{16,0},{32,48},{48,32},{64,80},{80,64},{96,112},{112,96},{1... | collective-permute-start | bytes 184328 | tf_op jit(solution)/shard_map/ppermute | solution.py:478
  70.5 4.1 %shard_map.94.rest_0_.inverse = f32[128,128]{1,0:T(8,128)S(1)} custom-call(bf16[128,2560]{1,0:T(8,128)(2,1)S(1)} %bitcast.15, bf16[128,2560]{1,0:T(8,128)(2,1)S(1)} %collective-permute-done.11.other.left.rest_2_, bf16[240,2560]{1,0:T(8,128)(2,1)S(1)} %get-tuple-element.26.rest_0_.rest_2_.refs_3_.refs_0_.merged.rest_4_.merged_mine, ...), custom_call_target="tpu_custom_call" | custom-call | flops 1000000000 | bytes 262144 | tf_op jit(solution)/shard_map/pallas_call | solution.py:274
  74.6 2.2 %collective-permute-done.14.corner = bf16[240,128]{1,0:T(8,128)(2,1)S(1)} collective-permute-done((bf16[240,128]{1,0:T(8,128)(2,1)S(1)}, bf16[240,128]{1,0:T(8,128)(2,1)S(1)}, u32[]{:S(2)}, u32[]{:S(2)}) %collective-permute-start.14) | collective-permute-done | bytes 61472 | tf_op jit(solution)/shard_map/ppermute | solution.py:478
  76.9 4.3 %collective-permute-start.18 = (bf16[240,128]{1,0:T(8,128)(2,1)S(1)}, bf16[240,128]{1,0:T(8,128)(2,1)S(1)}, u32[]{:S(2)}, u32[]{:S(2)}) collective-permute-start(bf16[240,128]{1,0:T(8,128)(2,1)S(1)} %shard_map.97._.refs_6_.product), channel_id=1, source_target_pairs={{0,80},{32,112},{64,16},{96,48},{16,64},{48,96},{80,0},{112,32},{1... | collective-permute-start | bytes 184328 | tf_op jit(solution)/shard_map/ppermute | solution.py:469
  81.2 0.9 collective-permute-start.17
  82.1 2.1 %collective-permute-start.16 = (bf16[240,128]{1,0:T(8,128)(2,1)S(1)}, bf16[240,128]{1,0:T(8,128)(2,1)S(1)}, u32[]{:S(2)}, u32[]{:S(2)}) collective-permute-start(bf16[240,128]{1,0:T(8,128)(2,1)S(1)} %shard_map.97._.refs_6_.product), channel_id=1, source_target_pairs={{0,112},{32,16},{64,48},{96,80},{16,32},{48,64},{80,96},{112,0},{1... | collective-permute-start | bytes 184328 | tf_op jit(solution)/shard_map/ppermute | solution.py:469
  84.2 2.0 %shard_map.99 = (bf16[240,5120]{1,0:T(8,128)(2,1)S(1)}, f32[8,128]{1,0:T(8,128)}) custom-call(s32[1]{0:T(128)} %bitcast.7.side_of.side, s32[1]{0:T(128)} %bitcast.8.depth, bf16[2,320,240]{2,1,0:T(8,128)(2,1)} %get-tuple-element.31.refs_3_.refs_0_, bf16[2,320,240]{2,1,0:T(8,128)(2,1)} %get-tuple-element.32.refs_4_.refs_1_, ...), custom_call_target="tpu_custom_call", output_to_operand_aliasing={{0}: (7, {})} | custom-call | flops 1000000000 | bytes 1536000 | tf_op jit(solution)/shard_map/pallas_call | solution.py:404
  86.2 1.0 %shard_map.98 = (bf16[128,5120]{1,0:T(8,128)(2,1)S(1)}, bf16[320,128]{1,0:T(8,128)(2,1)S(1)}) custom-call(s32[1]{0:T(128)} %bitcast.which, s32[1]{0:T(128)} %bitcast.7.side_of.side, s32[1]{0:T(128)} %bitcast.8.depth, f32[128,128]{1,0:T(8,128)S(1)} %shard_map.94.rest_0_.inverse, bf16[128,2560]{1,0:T(8,128)(2,1)S(1)} %bitcast.17, ...), custom_call_target="tpu_custom_call" | custom-call | flops 335544320 | bytes 2621440 | tf_op jit(solution)/shard_map/pallas_call | solution.py:306
  87.5 3.3 %shard_map.100 = (bf16[240,5120]{1,0:T(8,128)(2,1)}, bf16[240,5120]{1,0:T(8,128)(2,1)}, f32[320,240]{1,0:T(8,128)}, f32[320,240]{1,0:T(8,128)}) custom-call(s32[1]{0:T(128)} %bitcast.which, f32[128,128]{1,0:T(8,128)S(1)} %shard_map.94.rest_0_.inverse, bf16[240,128]{1,0:T(8,128)(2,1)S(1)} %shard_map.97._.refs_6_.product, ...), custom_call_target="tpu_custom_call" | custom-call | flops 314572800 | bytes 9830400 | tf_op jit(solution)/shard_map/pallas_call | solution.py:351
  (41 shorter events, 3.2 us)
Async XLA Ops:
  3.0 5.6 %collective-permute-start = (bf16[128,2560]{1,0:T(8,128)(2,1)S(1)}, bf16[128,2560]{1,0:T(8,128)(2,1)S(1)}, u32[]{:S(2)}, u32[]{:S(2)}) collective-permute-start(bf16[128,2560]{1,0:T(8,128)(2,1)S(1)} %get-tuple-element.25), channel_id=1, source_target_pairs={{0,1},{1,0},{2,3},{3,2},{4,5},{5,4},{6,7},{7,6},{8,9},{9,8},{10,11... | collective-permute-start | bytes 1966088 | tf_op jit(solution)/shard_map/ppermute | solution.py:505
  3.1 11.9 %collective-permute-start.1 = (bf16[320,240]{1,0:T(8,128)(2,1)S(1)}, bf16[320,240]{1,0:T(8,128)(2,1)S(1)}, u32[]{:S(2)}, u32[]{:S(2)}) collective-permute-start(bf16[320,240]{1,0:T(8,128)(2,1)S(1)} %get-tuple-element.27.own), channel_id=1, source_target_pairs={{0,128},{128,0},{1,129},{129,1},{2,130},{130,2},{3,131},{131,3},{4... | collective-permute-start | bytes 460808 | tf_op jit(solution)/shard_map/ppermute | solution.py:505
  9.6 22.6 %all-to-all-start = ((bf16[16,8,2560]{2,1,0:T(8,128)(2,1)}), bf16[16,8,2560]{2,1,0:T(8,128)(2,1)S(1)}, u32[]{:S(2)}, u32[]{:S(2)}) async-start(bf16[16,8,2560]{2,1,0:T(8,128)(2,1)} %bitcast.6), calls=%async_computation | async-start | bytes 1310720 | tf_op jit(solution)/shard_map/all_to_all | solution.py:526
  15.8 12.9 %collective-permute-start.3 = (bf16[2,320,240]{2,1,0:T(8,128)(2,1)}, bf16[2,320,240]{2,1,0:T(8,128)(2,1)S(1)}, u32[]{:S(2)}, u32[]{:S(2)}) collective-permute-start(bf16[2,320,240]{2,1,0:T(8,128)(2,1)} %shard_map.87.refs_0_), channel_id=1, source_target_pairs={{0,112},{16,0},{32,16},{48,32},{64,48},{80,64},{96,80},{112,96},{1... | collective-permute-start | bytes 921608 | tf_op jit(solution)/shard_map/ppermute | solution.py:501
  21.7 10.5 %collective-permute-start.2 = (bf16[2,320,240]{2,1,0:T(8,128)(2,1)}, bf16[2,320,240]{2,1,0:T(8,128)(2,1)}, u32[]{:S(2)}, u32[]{:S(2)}) collective-permute-start(bf16[2,320,240]{2,1,0:T(8,128)(2,1)} %shard_map.87.refs_0_), channel_id=1, source_target_pairs={{0,16},{16,32},{32,48},{48,64},{64,80},{80,96},{96,112},{112,0},{1... | collective-permute-start | bytes 921608 | tf_op jit(solution)/shard_map/ppermute | solution.py:501
  28.7 3.4 %copy-start.4 = (bf16[2,320,240]{2,1,0:T(8,128)(2,1)}, bf16[2,320,240]{2,1,0:T(8,128)(2,1)S(1)}, u32[]{:S(2)}) copy-start(bf16[2,320,240]{2,1,0:T(8,128)(2,1)S(1)} %collective-permute-done.3.rest_1_.rest_3_) | copy-start | bytes 921604
  32.2 4.1 %collective-permute-start.4 = (bf16[8,2560]{1,0:T(8,128)(2,1)S(1)}, bf16[8,2560]{1,0:T(8,128)(2,1)S(1)}, u32[]{:S(2)}, u32[]{:S(2)}) collective-permute-start(bf16[8,2560]{1,0:T(8,128)(2,1)S(1)} %shard_map.88.first), channel_id=1, source_target_pairs={{0,16},{16,0},{32,48},{48,32},{64,80},{80,64},{96,112},{112,96},{1... | collective-permute-start | bytes 122888 | tf_op jit(solution)/shard_map/ppermute | solution.py:505
  36.3 8.2 %collective-permute-start.7 = (bf16[8,2560]{1,0:T(8,128)(2,1)S(1)}, bf16[8,2560]{1,0:T(8,128)(2,1)S(1)}, u32[]{:S(2)}, u32[]{:S(2)}) collective-permute-start(bf16[8,2560]{1,0:T(8,128)(2,1)S(1)} %get-tuple-element.28.block), channel_id=1, source_target_pairs={{0,80},{32,112},{64,16},{96,48},{16,64},{48,96},{80,0},{112,32},{1... | collective-permute-start | bytes 122888 | tf_op jit(solution)/shard_map/ppermute | solution.py:469
  37.1 7.4 %collective-permute-start.6 = (bf16[8,2560]{1,0:T(8,128)(2,1)S(1)}, bf16[8,2560]{1,0:T(8,128)(2,1)S(1)}, u32[]{:S(2)}, u32[]{:S(2)}) collective-permute-start(bf16[8,2560]{1,0:T(8,128)(2,1)S(1)} %get-tuple-element.28.block), channel_id=1, source_target_pairs={{0,96},{32,0},{64,32},{96,64},{16,48},{48,80},{80,112},{112,16},{1... | collective-permute-start | bytes 122888 | tf_op jit(solution)/shard_map/ppermute | solution.py:469
  38.9 6.1 %collective-permute-start.5 = (bf16[8,2560]{1,0:T(8,128)(2,1)S(1)}, bf16[8,2560]{1,0:T(8,128)(2,1)S(1)}, u32[]{:S(2)}, u32[]{:S(2)}) collective-permute-start(bf16[8,2560]{1,0:T(8,128)(2,1)S(1)} %get-tuple-element.28.block), channel_id=1, source_target_pairs={{0,112},{32,16},{64,48},{96,80},{16,32},{48,64},{80,96},{112,0},{1... | collective-permute-start | bytes 122888 | tf_op jit(solution)/shard_map/ppermute | solution.py:469
  41.3 11.8 %collective-permute-start.8 = (bf16[2,320,240]{2,1,0:T(8,128)(2,1)}, bf16[2,320,240]{2,1,0:T(8,128)(2,1)S(1)}, u32[]{:S(2)}, u32[]{:S(2)}) collective-permute-start(bf16[2,320,240]{2,1,0:T(8,128)(2,1)} %get-tuple-element.29.refs_1_), channel_id=1, source_target_pairs={{0,16},{16,32},{32,48},{48,64},{64,80},{80,96},{96,112},{112,0},{1... | collective-permute-start | bytes 921608 | tf_op jit(solution)/shard_map/ppermute | solution.py:501
  41.3 11.8 %collective-permute-start.9 = (bf16[2,320,240]{2,1,0:T(8,128)(2,1)}, bf16[2,320,240]{2,1,0:T(8,128)(2,1)}, u32[]{:S(2)}, u32[]{:S(2)}) collective-permute-start(bf16[2,320,240]{2,1,0:T(8,128)(2,1)} %get-tuple-element.30.refs_2_), channel_id=1, source_target_pairs={{0,112},{16,0},{32,16},{48,32},{64,48},{80,64},{96,80},{112,96},{1... | collective-permute-start | bytes 921608 | tf_op jit(solution)/shard_map/ppermute | solution.py:501
  45.9 16.5 %all-to-all-start.1 = ((bf16[16,8,2560]{2,1,0:T(8,128)(2,1)}), bf16[16,8,2560]{2,1,0:T(8,128)(2,1)S(1)}, u32[]{:S(2)}, u32[]{:S(2)}) async-start(bf16[16,8,2560]{2,1,0:T(8,128)(2,1)} %shard_map.90), calls=%async_computation.1 | async-start | bytes 1310720 | tf_op jit(solution)/shard_map/all_to_all | solution.py:538
  53.1 0.7 copy-start.5
  53.8 8.5 %collective-permute-start.10 = (bf16[2,320,240]{2,1,0:T(8,128)(2,1)}, bf16[2,320,240]{2,1,0:T(8,128)(2,1)S(1)}, u32[]{:S(2)}, u32[]{:S(2)}) collective-permute-start(bf16[2,320,240]{2,1,0:T(8,128)(2,1)} %get-tuple-element.31.refs_3_.refs_0_), channel_id=1, source_target_pairs={{0,16},{16,32},{32,48},{48,64},{64,80},{80,96},{96,112},{112,0},{1... | collective-permute-start | bytes 921608 | tf_op jit(solution)/shard_map/ppermute | solution.py:501
  56.3 1.4 %copy-start = (bf16[240,5120]{1,0:T(8,128)(2,1)}, bf16[240,5120]{1,0:T(8,128)(2,1)S(1)}, u32[]{:S(2)}) copy-start(bf16[240,5120]{1,0:T(8,128)(2,1)S(1)} %get-tuple-element.35.refs_5_) | copy-start | bytes 7372804
  62.3 2.6 %collective-permute-start.11 = (bf16[128,2560]{1,0:T(8,128)(2,1)S(1)}, bf16[128,2560]{1,0:T(8,128)(2,1)S(1)}, u32[]{:S(2)}, u32[]{:S(2)}) collective-permute-start(bf16[128,2560]{1,0:T(8,128)(2,1)S(1)} %bitcast.13), channel_id=1, source_target_pairs={{0,1},{1,0},{2,3},{3,2},{4,5},{5,4},{6,7},{7,6},{8,9},{9,8},{10,11... | collective-permute-start | bytes 1966088 | tf_op jit(solution)/shard_map/ppermute | solution.py:505
  62.3 12.3 %collective-permute-start.15 = (bf16[2,320,240]{2,1,0:T(8,128)(2,1)}, bf16[2,320,240]{2,1,0:T(8,128)(2,1)S(1)}, u32[]{:S(2)}, u32[]{:S(2)}) collective-permute-start(bf16[2,320,240]{2,1,0:T(8,128)(2,1)} %get-tuple-element.32.refs_4_.refs_1_), channel_id=1, source_target_pairs={{0,112},{16,0},{32,16},{48,32},{64,48},{80,64},{96,80},{112,96},{1... | collective-permute-start | bytes 921608 | tf_op jit(solution)/shard_map/ppermute | solution.py:501
  63.9 20.3 %collective-permute-start.19 = (bf16[2,320,240]{2,1,0:T(8,128)(2,1)S(1)}, bf16[2,320,240]{2,1,0:T(8,128)(2,1)S(1)}, u32[]{:S(2)}, u32[]{:S(2)}) collective-permute-start(bf16[2,320,240]{2,1,0:T(8,128)(2,1)S(1)} %collective-permute-done.10.refs_1_.refs_2_), channel_id=1, source_target_pairs={{0,16},{16,32},{32,48},{48,64},{64,80},{80,96},{96,112},{112,0},{1... | collective-permute-start | bytes 921608 | tf_op jit(solution)/shard_map/ppermute | solution.py:501
  65.4 11.5 %collective-permute-start.14 = (bf16[240,128]{1,0:T(8,128)(2,1)S(1)}, bf16[240,128]{1,0:T(8,128)(2,1)S(1)}, u32[]{:S(2)}, u32[]{:S(2)}) collective-permute-start(bf16[240,128]{1,0:T(8,128)(2,1)S(1)} %shard_map.96.own), channel_id=1, source_target_pairs={{0,144},{16,128},{32,176},{48,160},{64,208},{80,192},{96,240},{112... | collective-permute-start | bytes 184328 | tf_op jit(solution)/shard_map/ppermute | solution.py:478
  67.9 9.0 %collective-permute-start.13 = (bf16[240,128]{1,0:T(8,128)(2,1)S(1)}, bf16[240,128]{1,0:T(8,128)(2,1)S(1)}, u32[]{:S(2)}, u32[]{:S(2)}) collective-permute-start(bf16[240,128]{1,0:T(8,128)(2,1)S(1)} %shard_map.96.own), channel_id=1, source_target_pairs={{0,128},{16,144},{32,160},{48,176},{64,192},{80,208},{96,224},{112... | collective-permute-start | bytes 184328 | tf_op jit(solution)/shard_map/ppermute | solution.py:478
  68.6 8.3 %collective-permute-start.12 = (bf16[240,128]{1,0:T(8,128)(2,1)S(1)}, bf16[240,128]{1,0:T(8,128)(2,1)S(1)}, u32[]{:S(2)}, u32[]{:S(2)}) collective-permute-start(bf16[240,128]{1,0:T(8,128)(2,1)S(1)} %shard_map.96.own), channel_id=1, source_target_pairs={{0,16},{16,0},{32,48},{48,32},{64,80},{80,64},{96,112},{112,96},{1... | collective-permute-start | bytes 184328 | tf_op jit(solution)/shard_map/ppermute | solution.py:478
  74.6 9.5 %copy-start.1 = (bf16[240,5120]{1,0:T(8,128)(2,1)S(1)}, bf16[240,5120]{1,0:T(8,128)(2,1)}, u32[]{:S(2)}) copy-start(bf16[240,5120]{1,0:T(8,128)(2,1)} %copy-done) | copy-start | bytes 7372804
  76.9 10.3 %collective-permute-start.18 = (bf16[240,128]{1,0:T(8,128)(2,1)S(1)}, bf16[240,128]{1,0:T(8,128)(2,1)S(1)}, u32[]{:S(2)}, u32[]{:S(2)}) collective-permute-start(bf16[240,128]{1,0:T(8,128)(2,1)S(1)} %shard_map.97._.refs_6_.product), channel_id=1, source_target_pairs={{0,80},{32,112},{64,16},{96,48},{16,64},{48,96},{80,0},{112,32},{1... | collective-permute-start | bytes 184328 | tf_op jit(solution)/shard_map/ppermute | solution.py:469
  81.2 6.0 %collective-permute-start.17 = (bf16[240,128]{1,0:T(8,128)(2,1)S(1)}, bf16[240,128]{1,0:T(8,128)(2,1)S(1)}, u32[]{:S(2)}, u32[]{:S(2)}) collective-permute-start(bf16[240,128]{1,0:T(8,128)(2,1)S(1)} %shard_map.97._.refs_6_.product), channel_id=1, source_target_pairs={{0,96},{32,0},{64,32},{96,64},{16,48},{48,80},{80,112},{112,16},{1... | collective-permute-start | bytes 184328 | tf_op jit(solution)/shard_map/ppermute | solution.py:469
  82.1 5.4 %collective-permute-start.16 = (bf16[240,128]{1,0:T(8,128)(2,1)S(1)}, bf16[240,128]{1,0:T(8,128)(2,1)S(1)}, u32[]{:S(2)}, u32[]{:S(2)}) collective-permute-start(bf16[240,128]{1,0:T(8,128)(2,1)S(1)} %shard_map.97._.refs_6_.product), channel_id=1, source_target_pairs={{0,112},{32,16},{64,48},{96,80},{16,32},{48,64},{80,96},{112,0},{1... | collective-permute-start | bytes 184328 | tf_op jit(solution)/shard_map/ppermute | solution.py:469
  84.1 3.4 %copy-start.2 = (f32[240,320]{0,1:T(8,128)S(1)}, f32[240,320]{0,1:T(8,128)}, u32[]{:S(2)}) copy-start(f32[240,320]{0,1:T(8,128)} %param.8) | copy-start | bytes 921604
  84.1 3.4 %copy-start.3 = (f32[240,320]{0,1:T(8,128)S(1)}, f32[240,320]{0,1:T(8,128)}, u32[]{:S(2)}) copy-start(f32[240,320]{0,1:T(8,128)} %param.9) | copy-start | bytes 921604
